TPU v7x, 256 devices: a whole 4x4x8 slice. The times are simulated.
256 devices in a mesh: node: 64 (over z, y, core), head: 4 (over x).
Axes of the slice: x: 4, y: 4, z: 8, core: 2. Of those that a mesh axis runs over, the one named last changes fastest.
Arguments:
- features: bfloat16 [131072, 256], P(('node', 'head')), may hold values from -40 to 40
- in_weight: bfloat16 [256, 768], replicated, may hold values from -0.6 to 0.6
- out_weight: bfloat16 [256, 256], replicated, may hold values from -0.375 to 0.375
- cotangent: bfloat16 [131072, 256], P(('node', 'head')), may hold values from -6 to 6
- key_slots: int32 [1024, 12], P('node'), may hold values from 0 to 143, as said below
- block_count: int32 [1024], P('node'), may hold values from 1 to 12
- wanted: int32 [64, 64, 2], P('node'), may hold values from 0 to 15
Outputs:
- output: bfloat16 [131072, 256], P(('node', 'head'))
- feature_grad: bfloat16 [131072, 256], P(('node', 'head'))
- in_weight_grad: float32 [256, 768], P(None, 'head')
- out_weight_grad: float32 [256, 256], P('head')
Inputs may be any that keep to these rules, and one draw needn't show every extreme that they name: `key_slots`: slot 0 of a query block names the block itself; the slots of one query block are distinct.
All inputs are finite; a program needn't handle non-finite values.
Results may differ from a plain program's by a relative error of at most 0.02.
The roundings to bfloat16 on the way count: a program that leaves them out, or rounds other values in their place, can miss the bound.
Values may be sent and summed in bfloat16 or wider, within the bound.
A program may use at most 128 MiB of HBM per device.

v0:
```python
import math

import jax
import jax.numpy as jnp
from jax import lax
from jax.sharding import PartitionSpec as P

HEADS = 4
HD = 64
BLOCK = 128
BLK = 16
PER = 12
CAP = 2


def attention_weights(query_block, key_block, live_mask, score_scale):
    scores = (
        jnp.einsum("gqhd,gpkhd->ghqpk", query_block, key_block, preferred_element_type=jnp.float32)
        * score_scale
    )
    scores = jnp.where(live_mask[:, None, None, :, None], scores, -1e30)
    layout = scores.shape
    scores = scores.reshape(layout[0], layout[1], layout[2], layout[3] * layout[4])
    highest = jnp.max(scores, axis=-1, keepdims=True)
    raised = jnp.exp(scores - highest)
    return (raised / jnp.sum(raised, axis=-1, keepdims=True)).reshape(layout)


def on_device(features, in_weight, out_weight, cotangent, key_slots, block_count, wanted):
    head_count = lax.axis_size("head")
    node_count = lax.axis_size("node")
    row_count = features.shape[0]
    local_heads = HEADS // head_count
    node_rows = row_count * head_count
    total_nodes = node_rows * node_count
    head_width = local_heads * 3 * HD
    score_scale = HD ** (-0.5)
    projected = jnp.dot(features, in_weight, preferred_element_type=jnp.float32).astype(
        jnp.bfloat16
    )
    projected = lax.all_to_all(projected, "head", split_axis=1, concat_axis=0, tiled=True)
    projected = projected.reshape(BLK, BLOCK, local_heads, 3, HD)
    queries = projected[:, :, :, 0]
    paired = projected[:, :, :, 1:].reshape(BLK, BLOCK, local_heads * 2 * HD)
    requests = lax.all_to_all(wanted, "node", split_axis=1, concat_axis=0, tiled=True).reshape(-1)
    outgoing = paired[requests].reshape(node_count, CAP, BLOCK, local_heads * 2 * HD)
    incoming = lax.all_to_all(outgoing, "node", split_axis=0, concat_axis=0, tiled=True)
    table = jnp.concatenate(
        [paired, incoming.reshape(node_count * CAP, BLOCK, local_heads * 2 * HD)], axis=0
    )
    group_size = math.gcd(BLK, max(1, 512 // BLOCK))
    step_count = BLK // group_size
    live_slots = jnp.arange(PER, dtype=jnp.int32)[None, :] < block_count[:, None]
    query_groups = queries.reshape(step_count, group_size, BLOCK, local_heads, HD)
    slot_groups = key_slots.reshape(step_count, group_size, PER)
    live_groups = live_slots.reshape(step_count, group_size, PER)

    def fetch_keys(slots):
        chosen = table[slots.reshape(-1)].reshape(group_size, PER, BLOCK, local_heads, 2, HD)
        return (chosen[:, :, :, :, 0], chosen[:, :, :, :, 1])

    def forward_step(inputs):
        query_block, slots, live_mask = inputs
        key_block, value_block = fetch_keys(slots)
        attention = attention_weights(query_block, key_block, live_mask, score_scale)
        result = jnp.einsum(
            "ghqpk,gpkhd->gqhd",
            attention.astype(jnp.bfloat16),
            value_block,
            preferred_element_type=jnp.float32,
        )
        return result.astype(jnp.bfloat16)

    attended = lax.map(forward_step, (query_groups, slot_groups, live_groups)).reshape(
        node_rows, local_heads * HD
    )
    attended_rows = lax.all_to_all(attended, "head", split_axis=0, concat_axis=1, tiled=True)
    summed = features.astype(jnp.float32) + jnp.dot(
        attended_rows, out_weight, preferred_element_type=jnp.float32
    )
    root_mean = jnp.sqrt(jnp.mean(summed * summed, axis=-1, keepdims=True) + 1e-06)
    normed = summed / root_mean
    output = normed.astype(jnp.bfloat16)
    upstream = cotangent.astype(jnp.float32)
    norm_grad = (
        upstream - normed * jnp.mean(upstream * normed, axis=-1, keepdims=True)
    ) / root_mean
    norm_grad_low = norm_grad.astype(jnp.bfloat16)
    out_weight_grad = jnp.dot(attended_rows.T, norm_grad_low, preferred_element_type=jnp.float32)
    attended_grad = jnp.dot(norm_grad_low, out_weight.T, preferred_element_type=jnp.float32).astype(
        jnp.bfloat16
    )
    attended_grad = lax.all_to_all(attended_grad, "head", split_axis=1, concat_axis=0, tiled=True)
    grad_blocks = attended_grad.reshape(BLK, BLOCK, local_heads, HD)
    attended_blocks = attended.reshape(BLK, BLOCK, local_heads, HD)
    row_dots = jnp.sum(
        grad_blocks.astype(jnp.float32) * attended_blocks.astype(jnp.float32), axis=-1
    )
    grad_groups = grad_blocks.reshape(step_count, group_size, BLOCK, local_heads, HD)
    dot_groups = row_dots.reshape(step_count, group_size, BLOCK, local_heads)

    def backward_step(accumulated, inputs):
        query_block, slots, live_mask, grad_block, dot_block = inputs
        key_block, value_block = fetch_keys(slots)
        attention = attention_weights(query_block, key_block, live_mask, score_scale)
        attention_low = attention.astype(jnp.bfloat16)
        prob_grad = jnp.einsum(
            "gqhd,gpkhd->ghqpk", grad_block, value_block, preferred_element_type=jnp.float32
        )
        row_term = jnp.transpose(dot_block, (0, 2, 1))[:, :, :, None, None]
        score_grad = (attention * (prob_grad - row_term) * score_scale).astype(jnp.bfloat16)
        query_grad = jnp.einsum(
            "ghqpk,gpkhd->gqhd", score_grad, key_block, preferred_element_type=jnp.float32
        )
        key_grad = jnp.einsum(
            "ghqpk,gqhd->gpkhd", score_grad, query_block, preferred_element_type=jnp.float32
        )
        value_grad = jnp.einsum(
            "ghqpk,gqhd->gpkhd", attention_low, grad_block, preferred_element_type=jnp.float32
        )
        pair_grads = jnp.stack([key_grad, value_grad], axis=4).reshape(
            group_size * PER, BLOCK, local_heads * 2 * HD
        )
        accumulated = accumulated.at[slots.reshape(-1)].add(pair_grads)
        return (accumulated, query_grad.astype(jnp.bfloat16))

    blank = jnp.zeros((BLK + node_count * CAP, BLOCK, local_heads * 2 * HD), jnp.float32)
    accumulated, query_grads = lax.scan(
        backward_step, blank, (query_groups, slot_groups, live_groups, grad_groups, dot_groups)
    )
    leaving = (
        accumulated[BLK:].astype(jnp.bfloat16).reshape(node_count, CAP, BLOCK, local_heads * 2 * HD)
    )
    returned = lax.all_to_all(leaving, "node", split_axis=0, concat_axis=0, tiled=True)
    returned = returned.astype(jnp.float32).reshape(node_count * CAP, BLOCK, local_heads * 2 * HD)
    pair_grad_sums = accumulated[:BLK].at[requests].add(returned)
    pair_grad_sums = pair_grad_sums.astype(jnp.bfloat16).reshape(BLK, BLOCK, local_heads, 2, HD)
    query_grads = query_grads.reshape(BLK, BLOCK, local_heads, 1, HD)
    projected_grad = jnp.concatenate([query_grads, pair_grad_sums], axis=3).reshape(
        node_rows, head_width
    )
    grad_rows_back = lax.all_to_all(projected_grad, "head", split_axis=0, concat_axis=1, tiled=True)
    feature_grad = norm_grad + jnp.dot(
        grad_rows_back, in_weight.T, preferred_element_type=jnp.float32
    )
    in_weight_grad = jnp.dot(features.T, grad_rows_back, preferred_element_type=jnp.float32)
    in_weight_grad, out_weight_grad = (
        lax.psum_scatter(in_weight_grad, "head", scatter_dimension=1, tiled=True),
        lax.psum_scatter(out_weight_grad, "head", scatter_dimension=0, tiled=True),
    )
    in_weight_grad, out_weight_grad = lax.psum((in_weight_grad, out_weight_grad), "node")
    grad_factor = total_nodes ** (-0.5)
    return (
        output,
        feature_grad.astype(jnp.bfloat16),
        in_weight_grad * grad_factor,
        out_weight_grad * grad_factor,
    )


def solution(mesh):
    placed = (
        P(("node", "head"), None),
        P(),
        P(),
        P(("node", "head"), None),
        P("node", None),
        P("node"),
        P("node", None, None),
    )
    return jax.shard_map(
        on_device,
        mesh=mesh,
        in_specs=placed,
        out_specs=(
            P(("node", "head"), None),
            P(("node", "head"), None),
            P(None, "head"),
            P("head", None),
        ),
        check_vma=False,
    )
```

profile of v0, /device:TPU:1, one launch (start us, length us, event | category | flops | bytes accessed | tf_op | source)
XLA Modules:
  0.0 718.2 jit_solution(406709541692996917)
XLA Ops:
  8.6 13.2 %all-to-all-start.1 = ((s32[1,64,2]{2,0,1:T(1,128)}), s32[1,64,2]{2,0,1:T(1,128)S(1)}, u32[]{:S(2)}, u32[]{:S(2)}) async-start(s32[1,64,2]{2,0,1:T(1,128)} %copy.101), calls=%async_computation.1 | async-start | bytes 65536 | tf_op jit(solution)/shard_map/all_to_all | solution.py:45
  24.3 6.8 all-to-all-done.1
  31.1 4.0 all-to-all-start
  36.5 10.0 %all-to-all-done = bf16[512,4,192]{0,2,1:T(8,128)(2,1)S(1)} async-done(((bf16[512,4,192]{0,2,1:T(8,128)(2,1)}), bf16[512,4,192]{0,2,1:T(8,128)(2,1)S(1)}, u32[]{:S(2)}, u32[]{:S(2)}) %all-to-all-start) | async-done | bytes 786464 | tf_op jit(solution)/shard_map/all_to_all | solution.py:41
  47.6 3.1 gather_fusion.2
  50.6 7.0 all-to-all-start.2
  59.1 93.2 %all-to-all-done.2 = bf16[64,2,128,128]{2,3,1,0:T(8,128)(2,1)} async-done(((bf16[64,2,128,128]{2,3,1,0:T(8,128)(2,1)}), bf16[64,2,128,128]{2,3,1,0:T(8,128)(2,1)}, u32[]{:S(2)}, u32[]{:S(2)}) %all-to-all-start.2) | async-done | bytes 4194336 | tf_op jit(solution)/shard_map/all_to_all | solution.py:47
  152.3 6.4 copy.102
  158.8 4.8 pad_maximum_fusion.1
  163.6 34.3 %while.22 = (s32[]{:T(128)}, bf16[4,4,128,1,64]{2,1,4,0,3:T(4,128)(2,1)}, s32[4,4,12]{2,1,0:T(4,128)S(1)}, bf16[144,128,128]{2,1,0:T(8,128)(2,1)}, pred[4,4,12]{...) while((s32[]{:T(128)}, bf16[4,4,128,1,64]{2,1,4,0,3:T(4,128)(2,1)}, ...), condition=%wide.region_3.4_spmd, body=%wide.region_0.3_spmd.sunk | while | flops 210796688 | bytes 17580788 | solution.py:74
  163.7 3.2 gather_fusion
  172.3 3.2 gather_fusion
  176.4 1.8 fusion.69
  180.8 3.2 gather_fusion
  189.4 3.2 gather_fusion
  197.9 1.8 all_to_all.70
  199.6 3.4 all-to-all-start.3
  205.3 3.3 all-to-all-done.3
  212.6 3.6 all-to-all-start.4
  216.2 5.3 all-to-all-done.4
  222.6 4.8 broadcast_in_dim.49
  227.4 108.8 %while.23 = (s32[]{:T(128)}, f32[144,128,128]{2,1,0:T(8,128)}, bf16[4,4,128,1,64]{2,4,1,3,0:T(8,128)(2,1)}, s32[4,4,12]{2,1,0:T(4,128)S(1)}, bf16[4,4,128,1,64]{...) while((s32[]{:T(128)}, f32[144,128,128]{2,1,0:T(8,128)}, ...), condition=%wide.region_11.12_spmd, body=%wide.region_7.11_spmd.sunk | while | flops 520650880 | bytes 60322728 | solution.py:128
  229.3 3.2 gather_fusion.1
  233.4 1.8 fusion.77
  242.0 2.3 copy.151
  244.3 10.4 %scatter_fusion = f32[144,128,128]{2,1,0:T(8,128)} fusion(f32[144,128,128]{2,1,0:T(8,128)} %get-tuple-element.320, s32[48]{0:T(128)S(1)} %fusion.76, f32[48,128,128]{2,1,0:T(8,128)} %copy.151), kind=kCustom, calls=%fused_computation.3.clone.1 | custom fusion | flops 786432 | bytes 9437376 | tf_op jit(solution)/shard_map/while/body/eval_jaxpr/scatter-add | solution.py:124
  256.6 3.2 gather_fusion.1
  260.7 1.8 fusion.77
  269.2 2.3 copy.151
  271.5 10.4 %scatter_fusion = f32[144,128,128]{2,1,0:T(8,128)} fusion(f32[144,128,128]{2,1,0:T(8,128)} %get-tuple-element.320, s32[48]{0:T(128)S(1)} %fusion.76, f32[48,128,128]{2,1,0:T(8,128)} %copy.151), kind=kCustom, calls=%fused_computation.3.clone.1 | custom fusion | flops 786432 | bytes 9437376 | tf_op jit(solution)/shard_map/while/body/eval_jaxpr/scatter-add | solution.py:124
  283.8 3.2 gather_fusion.1
  287.9 1.8 fusion.77
  296.4 2.3 copy.151
  298.7 10.3 %scatter_fusion = f32[144,128,128]{2,1,0:T(8,128)} fusion(f32[144,128,128]{2,1,0:T(8,128)} %get-tuple-element.320, s32[48]{0:T(128)S(1)} %fusion.76, f32[48,128,128]{2,1,0:T(8,128)} %copy.151), kind=kCustom, calls=%fused_computation.3.clone.1 | custom fusion | flops 786432 | bytes 9437376 | tf_op jit(solution)/shard_map/while/body/eval_jaxpr/scatter-add | solution.py:124
  311.0 3.2 gather_fusion.1
  315.1 1.8 fusion.77
  323.6 2.3 copy.151
  325.9 10.4 %scatter_fusion = f32[144,128,128]{2,1,0:T(8,128)} fusion(f32[144,128,128]{2,1,0:T(8,128)} %get-tuple-element.320, s32[48]{0:T(128)S(1)} %fusion.76, f32[48,128,128]{2,1,0:T(8,128)} %copy.151), kind=kCustom, calls=%fused_computation.3.clone.1 | custom fusion | flops 786432 | bytes 9437376 | tf_op jit(solution)/shard_map/while/body/eval_jaxpr/scatter-add | solution.py:124
  336.3 6.3 slice.52
  342.6 10.1 %all-to-all-start.5 = ((bf16[64,2,128,128]{3,2,1,0:T(8,128)(2,1)}), bf16[64,2,128,128]{3,2,1,0:T(8,128)(2,1)}, u32[]{:S(2)}, u32[]{:S(2)}) async-start(bf16[64,2,128,128]{3,2,1,0:T(8,128)(2,1)} %bitcast.218), calls=%async_computation.5 | async-start | bytes 8388608 | tf_op jit(solution)/shard_map/all_to_all | solution.py:134
  354.1 93.1 %all-to-all-done.5 = bf16[64,2,128,128]{3,2,1,0:T(8,128)(2,1)} async-done(((bf16[64,2,128,128]{3,2,1,0:T(8,128)(2,1)}), bf16[64,2,128,128]{3,2,1,0:T(8,128)(2,1)}, u32[]{:S(2)}, u32[]{:S(2)}) %all-to-all-start.5) | async-done | bytes 4194336 | tf_op jit(solution)/shard_map/all_to_all | solution.py:134
  447.1 6.5 bitcast_convert_fusion
  453.6 17.0 %scatter_fusion.1 = f32[16,128,128]{2,1,0:T(8,128)S(1)} fusion(f32[16,128,128]{2,1,0:T(8,128)S(1)} %slice.27, s32[128]{0:T(128)S(1)} %copy-done.17, f32[128,128,128]{2,1,0:T(8,128)} %bitcast_convert_fusion), kind=kCustom, calls=%fused_computation.4 | custom fusion | flops 2097152 | bytes 25166336 | tf_op jit(solution)/shard_map/scatter-add | solution.py:136
  473.1 3.6 all-to-all-start.6
  477.8 8.5 %all-to-all-done.6 = bf16[4,512,192]{1,2,0:T(8,128)(2,1)S(1)} async-done(((bf16[4,512,192]{1,2,0:T(8,128)(2,1)}), bf16[4,512,192]{1,2,0:T(8,128)(2,1)S(1)}, u32[]{:S(2)}, u32[]{:S(2)}) %all-to-all-start.6) | async-done | bytes 786464 | tf_op jit(solution)/shard_map/all_to_all | solution.py:142
  488.5 10.7 %reduce-scatter.5.cloned.1.call-done = f32[64,256]{1,0:T(8,128)} async-done(((f32[256,256]{1,0:T(8,128)}), f32[64,256]{1,0:T(8,128)}) %reduce-scatter.5.cloned.1.call-update) | async-done | bytes 65552 | tf_op jit(solution)/shard_map/reduce_scatter | solution.py:149
  499.2 28.6 %reduce-scatter.3.cloned.1.call-done = f32[256,192]{0,1:T(8,128)} async-done(((f32[256,768]{0,1:T(8,128)}), f32[256,192]{0,1:T(8,128)}) %reduce-scatter.3.cloned.1.call-update) | async-done | bytes 196624 | tf_op jit(solution)/shard_map/reduce_scatter | solution.py:148
  529.1 179.4 %all-reduce.3.cloned.1.call-done = (f32[256,192]{0,1:T(8,128)}, f32[64,256]{1,0:T(8,128)}) async-done(((f32[256,192]{0,1:T(8,128)}, f32[64,256]{1,0:T(8,128)}), (f32[256,192]{0,1:T(8,128)}, f32[64,256]{1,0:T(8,128)})) %all-reduce.3.cloned.1.call-update) | async-done | bytes 262160 | tf_op jit(solution)/shard_map/psum | solution.py:151
  (239 shorter events, 83.6 us)
Async XLA Ops:
  7.2 14.6 %copy-start = (bf16[256,768]{1,0:T(8,128)(2,1)S(1)}, bf16[256,768]{1,0:T(8,128)(2,1)}, u32[]{:S(2)}) copy-start(bf16[256,768]{1,0:T(8,128)(2,1)} %param.12) | copy-start | bytes 1179652
  8.6 22.5 %all-to-all-start.1 = ((s32[1,64,2]{2,0,1:T(1,128)}), s32[1,64,2]{2,0,1:T(1,128)S(1)}, u32[]{:S(2)}, u32[]{:S(2)}) async-start(s32[1,64,2]{2,0,1:T(1,128)} %copy.101), calls=%async_computation.1 | async-start | bytes 65536 | tf_op jit(solution)/shard_map/all_to_all | solution.py:45
  31.1 15.4 %all-to-all-start = ((bf16[512,4,192]{0,2,1:T(8,128)(2,1)}), bf16[512,4,192]{0,2,1:T(8,128)(2,1)S(1)}, u32[]{:S(2)}, u32[]{:S(2)}) async-start(bf16[512,4,192]{0,2,1:T(8,128)(2,1)} %bitcast.42), calls=%async_computation | async-start | bytes 1572864 | tf_op jit(solution)/shard_map/all_to_all | solution.py:41
  36.5 10.6 %copy-start.16 = (s32[128]{0:T(128)}, s32[128]{0:T(128)S(1)}, u32[]{:S(2)}) copy-start(s32[128]{0:T(128)S(1)} %fusion.41) | copy-start | bytes 1540
  50.6 7.0 copy-start.20
  50.6 101.7 %all-to-all-start.2 = ((bf16[64,2,128,128]{2,3,1,0:T(8,128)(2,1)}), bf16[64,2,128,128]{2,3,1,0:T(8,128)(2,1)}, u32[]{:S(2)}, u32[]{:S(2)}) async-start(bf16[64,2,128,128]{2,3,1,0:T(8,128)(2,1)} %bitcast.217), calls=%async_computation.2 | async-start | bytes 8388608 | tf_op jit(solution)/shard_map/all_to_all | solution.py:47
  158.8 4.8 copy-start.12
  197.9 13.8 %copy-start.10 = (bf16[256,256]{1,0:T(8,128)(2,1)S(1)}, bf16[256,256]{1,0:T(8,128)(2,1)}, u32[]{:S(2)}) copy-start(bf16[256,256]{1,0:T(8,128)(2,1)} %param.13) | copy-start | bytes 393220
  199.6 8.9 %all-to-all-start.3 = ((bf16[4,512,64]{1,2,0:T(8,128)(2,1)}), bf16[4,512,64]{1,2,0:T(8,128)(2,1)S(1)}, u32[]{:S(2)}, u32[]{:S(2)}) async-start(bf16[4,512,64]{1,2,0:T(8,128)(2,1)} %all_to_all.70), calls=%async_computation.3 | async-start | bytes 524288 | tf_op jit(solution)/shard_map/all_to_all | solution.py:77
  208.6 18.9 %copy-start.4 = (bf16[4,512,64]{1,2,0:T(8,128)(2,1)}, bf16[4,512,64]{1,2,0:T(8,128)(2,1)S(1)}, u32[]{:S(2)}) copy-start(bf16[4,512,64]{1,2,0:T(8,128)(2,1)S(1)} %all-to-all-done.3) | copy-start | bytes 786436
  212.6 8.9 %all-to-all-start.4 = ((bf16[512,4,64]{0,2,1:T(8,128)(2,1)}), bf16[512,4,64]{0,2,1:T(8,128)(2,1)S(1)}, u32[]{:S(2)}, u32[]{:S(2)}) async-start(bf16[512,4,64]{0,2,1:T(8,128)(2,1)} %bitcast.52), calls=%async_computation.4 | async-start | bytes 524288 | tf_op jit(solution)/shard_map/all_to_all | solution.py:93
  227.4 1.9 copy-start.7
  227.4 1.9 copy-start.14
  233.4 1.9 copy-start.13
  233.4 2.7 copy-start.6
  244.3 10.4 %copy-start.8 = (bf16[4,4,128,1,64]{2,1,4,0,3:T(4,128)(2,1)S(1)}, bf16[4,4,128,1,64]{2,1,4,0,3:T(4,128)(2,1)}, u32[]{:S(2)}) copy-start(bf16[4,4,128,1,64]{2,1,4,0,3:T(4,128)(2,1)} %copy-done.7) | copy-start | bytes 786436 | tf_op jit(solution)/shard_map/while
  244.3 10.4 %copy-start.15 = (f32[4,4,128,1]{2,1,3,0:T(4,128)S(1)}, f32[4,4,128,1]{2,1,3,0:T(4,128)}, u32[]{:S(2)}) copy-start(f32[4,4,128,1]{2,1,3,0:T(4,128)} %copy-done.14) | copy-start | bytes 24580 | tf_op jit(solution)/shard_map/while
  244.3 10.4 %copy-start.19 = (pred[4,4,12]{2,1,0:T(4,128)(4,1)S(1)}, pred[4,4,12]{2,1,0:T(4,128)(4,1)}, u32[]{:S(2)}) copy-start(pred[4,4,12]{2,1,0:T(4,128)(4,1)} %copy-done.18) | copy-start | bytes 580 | tf_op jit(solution)/shard_map/while
  254.7 1.9 copy-start.7
  254.7 1.9 copy-start.14
  260.7 1.9 copy-start.13
  260.7 2.7 copy-start.6
  271.5 10.4 %copy-start.8 = (bf16[4,4,128,1,64]{2,1,4,0,3:T(4,128)(2,1)S(1)}, bf16[4,4,128,1,64]{2,1,4,0,3:T(4,128)(2,1)}, u32[]{:S(2)}) copy-start(bf16[4,4,128,1,64]{2,1,4,0,3:T(4,128)(2,1)} %copy-done.7) | copy-start | bytes 786436 | tf_op jit(solution)/shard_map/while
  271.5 10.4 %copy-start.15 = (f32[4,4,128,1]{2,1,3,0:T(4,128)S(1)}, f32[4,4,128,1]{2,1,3,0:T(4,128)}, u32[]{:S(2)}) copy-start(f32[4,4,128,1]{2,1,3,0:T(4,128)} %copy-done.14) | copy-start | bytes 24580 | tf_op jit(solution)/shard_map/while
  271.5 10.4 %copy-start.19 = (pred[4,4,12]{2,1,0:T(4,128)(4,1)S(1)}, pred[4,4,12]{2,1,0:T(4,128)(4,1)}, u32[]{:S(2)}) copy-start(pred[4,4,12]{2,1,0:T(4,128)(4,1)} %copy-done.18) | copy-start | bytes 580 | tf_op jit(solution)/shard_map/while
  281.9 1.9 copy-start.7
  287.9 1.9 copy-start.13
  287.9 2.7 copy-start.6
  298.7 10.3 %copy-start.8 = (bf16[4,4,128,1,64]{2,1,4,0,3:T(4,128)(2,1)S(1)}, bf16[4,4,128,1,64]{2,1,4,0,3:T(4,128)(2,1)}, u32[]{:S(2)}) copy-start(bf16[4,4,128,1,64]{2,1,4,0,3:T(4,128)(2,1)} %copy-done.7) | copy-start | bytes 786436 | tf_op jit(solution)/shard_map/while
  298.7 10.3 %copy-start.15 = (f32[4,4,128,1]{2,1,3,0:T(4,128)S(1)}, f32[4,4,128,1]{2,1,3,0:T(4,128)}, u32[]{:S(2)}) copy-start(f32[4,4,128,1]{2,1,3,0:T(4,128)} %copy-done.14) | copy-start | bytes 24580 | tf_op jit(solution)/shard_map/while
  298.7 10.3 %copy-start.19 = (pred[4,4,12]{2,1,0:T(4,128)(4,1)S(1)}, pred[4,4,12]{2,1,0:T(4,128)(4,1)}, u32[]{:S(2)}) copy-start(pred[4,4,12]{2,1,0:T(4,128)(4,1)} %copy-done.18) | copy-start | bytes 580 | tf_op jit(solution)/shard_map/while
  309.1 1.9 copy-start.7
  315.1 1.9 copy-start.13
  315.1 2.7 copy-start.6
  325.9 10.4 %copy-start.8 = (bf16[4,4,128,1,64]{2,1,4,0,3:T(4,128)(2,1)S(1)}, bf16[4,4,128,1,64]{2,1,4,0,3:T(4,128)(2,1)}, u32[]{:S(2)}) copy-start(bf16[4,4,128,1,64]{2,1,4,0,3:T(4,128)(2,1)} %copy-done.7) | copy-start | bytes 786436 | tf_op jit(solution)/shard_map/while
  325.9 10.4 %copy-start.15 = (f32[4,4,128,1]{2,1,3,0:T(4,128)S(1)}, f32[4,4,128,1]{2,1,3,0:T(4,128)}, u32[]{:S(2)}) copy-start(f32[4,4,128,1]{2,1,3,0:T(4,128)} %copy-done.14) | copy-start | bytes 24580 | tf_op jit(solution)/shard_map/while
  325.9 10.4 %copy-start.19 = (pred[4,4,12]{2,1,0:T(4,128)(4,1)S(1)}, pred[4,4,12]{2,1,0:T(4,128)(4,1)}, u32[]{:S(2)}) copy-start(pred[4,4,12]{2,1,0:T(4,128)(4,1)} %copy-done.18) | copy-start | bytes 580 | tf_op jit(solution)/shard_map/while
  342.6 104.5 %all-to-all-start.5 = ((bf16[64,2,128,128]{3,2,1,0:T(8,128)(2,1)}), bf16[64,2,128,128]{3,2,1,0:T(8,128)(2,1)}, u32[]{:S(2)}, u32[]{:S(2)}) async-start(bf16[64,2,128,128]{3,2,1,0:T(8,128)(2,1)} %bitcast.218), calls=%async_computation.5 | async-start | bytes 8388608 | tf_op jit(solution)/shard_map/all_to_all | solution.py:134
  354.1 99.6 %copy-start.17 = (s32[128]{0:T(128)S(1)}, s32[128]{0:T(128)}, u32[]{:S(2)}) copy-start(s32[128]{0:T(128)} %copy-done.16) | copy-start | bytes 1540
  453.6 17.4 %copy-start.11 = (bf16[4,4,128,1,64]{2,4,1,3,0:T(8,128)(2,1)S(1)}, bf16[4,4,128,1,64]{2,4,1,3,0:T(8,128)(2,1)}, u32[]{:S(2)}) copy-start(bf16[4,4,128,1,64]{2,4,1,3,0:T(8,128)(2,1)} %get-tuple-element.85) | copy-start | bytes 786436
  471.2 5.6 copy-start.2
  471.2 5.6 copy-start.5
  471.7 14.6 %copy-start.3 = (bf16[512,256]{1,0:T(8,128)(2,1)S(1)}, bf16[512,256]{1,0:T(8,128)(2,1)}, u32[]{:S(2)}) copy-start(bf16[512,256]{1,0:T(8,128)(2,1)} %param.11) | copy-start | bytes 786436
  473.0 14.6 %copy-start.9 = (bf16[512,256]{0,1:T(8,128)(2,1)S(1)}, bf16[512,256]{0,1:T(8,128)(2,1)}, u32[]{:S(2)}) copy-start(bf16[512,256]{0,1:T(8,128)(2,1)} %get-tuple-element.185) | copy-start | bytes 786436
  473.1 13.3 %all-to-all-start.6 = ((bf16[4,512,192]{1,2,0:T(8,128)(2,1)}), bf16[4,512,192]{1,2,0:T(8,128)(2,1)S(1)}, u32[]{:S(2)}, u32[]{:S(2)}) async-start(bf16[4,512,192]{1,2,0:T(8,128)(2,1)} %copy.111), calls=%async_computation.6 | async-start | bytes 1572864 | tf_op jit(solution)/shard_map/all_to_all | solution.py:142
  476.7 22.5 %reduce-scatter.5.cloned.1.call-start = ((), (), s32[]{:S(2)}) async-start(), calls=%async_computation.10 | async-start | bytes 327680 | tf_op jit(solution)/shard_map/reduce_scatter | solution.py:149
  477.8 50.1 %reduce-scatter.3.cloned.1.call-start = ((), (), s32[]{:S(2)}) async-start(), calls=%async_computation.9 | async-start | bytes 983040 | tf_op jit(solution)/shard_map/reduce_scatter | solution.py:148
  487.6 220.9 %all-reduce.3.cloned.1.call-start = ((), (), s32[]{:S(2)}) async-start(), calls=%async_computation.11 | async-start | bytes 524288 | tf_op jit(solution)/shard_map/psum | solution.py:151
  (7 other events, 6.9 us)
Sparse Core Ops, SparseCore 0:
  480.0 19.1 reduce-scatter.4
  501.9 25.8 reduce-scatter.2
  532.0 176.5 all-reduce.2
where the time goes:
time: 721 us; the launch traced here: 718 us
  waiting for transfers between devices  439 us (61%)
  local copies, waits for them, and re-layouts  89.7 us (12%)
  other arithmetic  84.1 us (12%)
  matrix products  45.6 us (6%)
  starting transfers between devices  45.1 us (6%)
  between operations  14.1 us (2%)
    psum x1, waiting for transfers between devices, on_device(): lax.psum((in_weight_grad, out_weight_grad), 'node')  179 us
    all_to_all x1, waiting for transfers between devices, on_device(): lax.all_to_all(outgoing, 'node', split_axis=0, concat_axis=0, tiled=True)  93.2 us
    all_to_all x1, waiting for transfers between devices, on_device(): lax.all_to_all(leaving, 'node', split_axis=0, concat_axis=0, tiled=True)  93.1 us
    scatter-add x4, other arithmetic, backward_step(): accumulated = accumulated.at[slots.reshape(-1)].add(pair_grads)  41.4 us
    gather x16, local copies, waits for them, and re-layouts, fetch_keys(): table[slots.reshape(-1)].reshape(group_size, PER, BLOCK, local_heads, 2, HD)  32.7 us
    reduce_scatter x1, waiting for transfers between devices, on_device(): lax.psum_scatter(in_weight_grad, 'head', scatter_dimension=1, tiled=True)  28.6 us
    scatter-add x1, other arithmetic, on_device(): pair_grad_sums = accumulated[:BLK].at[requests].add(returned)  17 us
    dot_general x8, matrix products, attention_weights(): jnp.einsum('gqhd,gpkhd->ghqpk', query_block, key_block, preferred_element...  14.5 us
  transfers between devices with their start and end apart: 10, of which 10 were waited for; matrix products, arithmetic and copies ran while one was open for 2% of the time, Pallas kernels for 0%

commit v1 on v0

v1 whole, which is shorter than its diff:
```python
import jax
import jax.numpy as jnp
from jax import lax
from jax.experimental import pallas as pl
from jax.experimental.pallas import tpu as pltpu
from jax.sharding import PartitionSpec as P

HEADS = 4
HD = 64
BLOCK = 128
BLK = 16
PER = 12
CAP = 2
PAIR = 2 * HD
SCALE = HD ** (-0.5)
NT = (((1,), (1,)), ((), ()))
TN = (((0,), (0,)), ((), ()))


def dot(a, b, dims=(((1,), (0,)), ((), ()))):
    return lax.dot_general(a, b, dims, preferred_element_type=jnp.float32)


def forward_kernel(slots_ref, count_ref, q_ref, table_ref, out_ref, stat_ref):
    b = pl.program_id(0)
    count = count_ref[b]
    query = q_ref[...]
    chosen = [table_ref[slots_ref[b * PER + j]] for j in range(PER)]
    scores = []
    for j in range(0, PER, 2):
        pair = dot(query, jnp.concatenate(chosen[j : j + 2], axis=0), NT)
        key = lax.broadcasted_iota(jnp.int32, pair.shape, 1) + j * BLOCK
        scores.append(jnp.where(key < count * BLOCK, pair, -1e30))
    highest = scores[0]
    for part in scores[1:]:
        highest = jnp.maximum(highest, part)
    highest = jnp.max(highest, axis=1, keepdims=True)
    total = jnp.zeros((BLOCK, 2 * BLOCK), jnp.float32)
    result = jnp.zeros((BLOCK, PAIR), jnp.float32)
    for j, part in enumerate(scores):
        raised = jnp.exp(part - highest)
        total = total + raised
        result = result + dot(
            raised.astype(jnp.bfloat16), jnp.concatenate(chosen[2 * j : 2 * j + 2], axis=0)
        )
    total = jnp.sum(total, axis=1, keepdims=True)
    out_ref[...] = (result / total).astype(jnp.bfloat16)
    lane = lax.broadcasted_iota(jnp.int32, stat_ref.shape, 1)
    stat_ref[...] = jnp.where(lane < HD, highest, 1.0 / total)


def forward(slots, count, query, table):
    rows = BLK * BLOCK
    grid_spec = pltpu.PrefetchScalarGridSpec(
        num_scalar_prefetch=2,
        grid=(BLK,),
        in_specs=[
            pl.BlockSpec((BLOCK, PAIR), lambda b, *_: (b, 0)),
            pl.BlockSpec(table.shape, lambda b, *_: (0, 0, 0)),
        ],
        out_specs=[
            pl.BlockSpec((BLOCK, PAIR), lambda b, *_: (b, 0)),
            pl.BlockSpec((BLOCK, PAIR), lambda b, *_: (b, 0)),
        ],
    )
    return pl.pallas_call(
        forward_kernel,
        grid_spec=grid_spec,
        out_shape=(
            jax.ShapeDtypeStruct((rows, PAIR), jnp.bfloat16),
            jax.ShapeDtypeStruct((rows, PAIR), jnp.float32),
        ),
        compiler_params=pltpu.CompilerParams(vmem_limit_bytes=40 << 20),
        cost_estimate=pl.CostEstimate(
            flops=4 * BLK * PER * BLOCK**3, bytes_accessed=8 << 20, transcendentals=BLK * PER * BLOCK**2
        ),
        name="attend",
    )(slots, count, query, table)


def backward_kernel(
    slots_ref, count_ref, qg_ref, att_ref, stat_ref, table_ref, dq_ref, own_ref, far_ref, acc_ref
):
    b = pl.program_id(0)
    own_slots = own_ref.shape[0]

    @pl.when(b == 0)
    def _():
        acc_ref[...] = jnp.zeros_like(acc_ref)

    count = count_ref[b]
    both = qg_ref[...]
    lane = lax.broadcasted_iota(jnp.int32, both.shape, 1)
    zero = jnp.zeros_like(both)
    stacked = jnp.concatenate(
        [jnp.where(lane < HD, both, zero), jnp.where(lane < HD, zero, both)], axis=0
    )
    dots = jnp.sum(
        jnp.where(lane < HD, 0.0, both.astype(jnp.float32) * att_ref[...].astype(jnp.float32)),
        axis=1,
        keepdims=True,
    )
    highest = stat_ref[:, 0:1]
    inverse = stat_ref[:, HD : HD + 1]
    dq = jnp.zeros((BLOCK, PAIR), jnp.float32)
    for j in range(0, PER, 2):
        slots = [slots_ref[b * PER + j + i] for i in range(2)]
        chosen = jnp.concatenate([table_ref[s] for s in slots], axis=0)
        products = dot(stacked, chosen, NT)
        key = lax.broadcasted_iota(jnp.int32, (BLOCK, 2 * BLOCK), 1) + j * BLOCK
        scores = jnp.where(key < count * BLOCK, products[:BLOCK], -1e30)
        attention = jnp.exp(scores - highest) * inverse
        score_grad = (attention * (products[BLOCK:] - dots)).astype(jnp.bfloat16)
        dq = dq + dot(score_grad, chosen)
        pair = jnp.concatenate([score_grad, attention.astype(jnp.bfloat16)], axis=0)
        grads = dot(pair, stacked, TN)
        for i in range(2):
            acc_ref[slots[i]] += grads[i * BLOCK : (i + 1) * BLOCK]
    dq_ref[...] = (dq * SCALE).astype(jnp.bfloat16)

    @pl.when(b == pl.num_programs(0) - 1)
    def _():
        own_ref[...] = acc_ref[:own_slots]
        far_ref[...] = acc_ref[own_slots:].astype(jnp.bfloat16)


def backward(slots, count, query_grad, attended, stat, table):
    rows = BLK * BLOCK
    far = table.shape[0] - BLK
    whole = lambda shape: pl.BlockSpec(shape, lambda b, *_: (0,) * len(shape))
    rowwise = pl.BlockSpec((BLOCK, PAIR), lambda b, *_: (b, 0))
    grid_spec = pltpu.PrefetchScalarGridSpec(
        num_scalar_prefetch=2,
        grid=(BLK,),
        in_specs=[rowwise, rowwise, rowwise, whole(table.shape)],
        out_specs=[rowwise, whole((BLK, BLOCK, PAIR)), whole((far, BLOCK, PAIR))],
        scratch_shapes=[pltpu.VMEM(table.shape, jnp.float32)],
    )
    return pl.pallas_call(
        backward_kernel,
        grid_spec=grid_spec,
        out_shape=(
            jax.ShapeDtypeStruct((rows, PAIR), jnp.bfloat16),
            jax.ShapeDtypeStruct((BLK, BLOCK, PAIR), jnp.float32),
            jax.ShapeDtypeStruct((far, BLOCK, PAIR), jnp.bfloat16),
        ),
        compiler_params=pltpu.CompilerParams(vmem_limit_bytes=56 << 20),
        cost_estimate=pl.CostEstimate(
            flops=10 * BLK * PER * BLOCK**3, bytes_accessed=16 << 20, transcendentals=BLK * PER * BLOCK**2
        ),
        name="attend_back",
    )(slots, count, query_grad, attended, stat, table)


def on_device(features, in_weight, out_weight, cotangent, key_slots, block_count, wanted):
    node_count = lax.axis_size("node")
    node_rows = BLK * BLOCK
    total_nodes = node_rows * node_count
    projected = jnp.dot(features, in_weight, preferred_element_type=jnp.float32).astype(
        jnp.bfloat16
    )
    projected = lax.all_to_all(projected, "head", split_axis=1, concat_axis=0, tiled=True)
    queries = projected[:, :HD] * jnp.bfloat16(SCALE)
    paired = projected[:, HD:].reshape(BLK, BLOCK, PAIR)
    requests = lax.all_to_all(wanted, "node", split_axis=1, concat_axis=0, tiled=True).reshape(-1)
    outgoing = paired[requests].reshape(node_count, CAP, BLOCK, PAIR)
    incoming = lax.all_to_all(outgoing, "node", split_axis=0, concat_axis=0, tiled=True)
    table = jnp.concatenate([paired, incoming.reshape(node_count * CAP, BLOCK, PAIR)], axis=0)
    slots = key_slots.reshape(-1)
    padded = jnp.concatenate([queries, jnp.zeros_like(queries)], axis=1)
    wide, stat = forward(slots, block_count, padded, table)
    attended = wide[:, HD:]
    attended_rows = lax.all_to_all(attended, "head", split_axis=0, concat_axis=1, tiled=True)
    summed = features.astype(jnp.float32) + jnp.dot(
        attended_rows, out_weight, preferred_element_type=jnp.float32
    )
    root_mean = jnp.sqrt(jnp.mean(summed * summed, axis=-1, keepdims=True) + 1e-06)
    normed = summed / root_mean
    output = normed.astype(jnp.bfloat16)
    upstream = cotangent.astype(jnp.float32)
    norm_grad = (
        upstream - normed * jnp.mean(upstream * normed, axis=-1, keepdims=True)
    ) / root_mean
    norm_grad_low = norm_grad.astype(jnp.bfloat16)
    out_weight_grad = jnp.dot(attended_rows.T, norm_grad_low, preferred_element_type=jnp.float32)
    attended_grad = jnp.dot(norm_grad_low, out_weight.T, preferred_element_type=jnp.float32).astype(
        jnp.bfloat16
    )
    attended_grad = lax.all_to_all(attended_grad, "head", split_axis=1, concat_axis=0, tiled=True)
    both = jnp.concatenate([queries, attended_grad], axis=1)
    dq, own, leaving = backward(slots, block_count, both, wide, stat, table)
    returned = lax.all_to_all(
        leaving.reshape(node_count, CAP, BLOCK, PAIR), "node", split_axis=0, concat_axis=0, tiled=True
    )
    returned = returned.astype(jnp.float32).reshape(node_count * CAP, BLOCK, PAIR)
    pair_grads = own.at[requests].add(returned).astype(jnp.bfloat16).reshape(node_rows, PAIR)
    projected_grad = jnp.concatenate([dq[:, :HD], pair_grads], axis=1)
    grad_rows_back = lax.all_to_all(projected_grad, "head", split_axis=0, concat_axis=1, tiled=True)
    feature_grad = norm_grad + jnp.dot(
        grad_rows_back, in_weight.T, preferred_element_type=jnp.float32
    )
    in_weight_grad = jnp.dot(features.T, grad_rows_back, preferred_element_type=jnp.float32)
    in_weight_grad, out_weight_grad = (
        lax.psum_scatter(in_weight_grad, "head", scatter_dimension=1, tiled=True),
        lax.psum_scatter(out_weight_grad, "head", scatter_dimension=0, tiled=True),
    )
    in_weight_grad, out_weight_grad = lax.psum((in_weight_grad, out_weight_grad), "node")
    grad_factor = total_nodes ** (-0.5)
    return (
        output,
        feature_grad.astype(jnp.bfloat16),
        in_weight_grad * grad_factor,
        out_weight_grad * grad_factor,
    )


def solution(mesh):
    placed = (
        P(("node", "head"), None),
        P(),
        P(),
        P(("node", "head"), None),
        P("node", None),
        P("node"),
        P("node", None, None),
    )
    return jax.shard_map(
        on_device,
        mesh=mesh,
        in_specs=placed,
        out_specs=(
            P(("node", "head"), None),
            P(("node", "head"), None),
            P(None, "head"),
            P("head", None),
        ),
        check_vma=False,
    )
```

time: 721 us -> 597 us (0.83)
  local copies, waits for them, and re-layouts: 89.7 us -> 14.1 us
  other arithmetic: 84.1 us -> 32.4 us
  Pallas kernels: 0 us -> 42.7 us
  matrix products: 45.6 us -> 4.43 us
  blocking collectives: 0 us -> 7.92 us
    pallas_call x0 -> x2, Pallas kernels: none -> 42.7 us  [the longest x1 32 us: backward(): pl.pallas_call(backward_kernel, grid_spec=grid_spec, out_shape=(jax.Shape...]
    scatter-add x5 -> x1, other arithmetic: 58.5 us -> 17 us  [on_device(): own.at[requests].add(returned).astype(jnp.bfloat16).reshape(node_rows, PAIR)]
    dot_general x28 -> x0, matrix products: 39.5 us -> none  [the longest x8 14.5 us: attention_weights(): jnp.einsum('gqhd,gpkhd->ghqpk', query_block, key_block, preferred_element...]
    gather x17 -> x1, local copies, waits for them, and re-layouts: 35.8 us -> 3.07 us  [on_device(): outgoing = paired[requests].reshape(node_count, CAP, BLOCK, PAIR)]
    reshape x15 -> x1, local copies, waits for them, and re-layouts: 10.7 us -> 0.08 us  [on_device(): slots = key_slots.reshape(-1)]
    all_to_all x0 -> x1, blocking collectives: none -> 7.92 us  [on_device(): lax.all_to_all(attended_grad, 'head', split_axis=1, concat_axis=0, tiled=...]
    reduce_sum x9 -> x0, other arithmetic: 7.6 us -> none  [the longest x8 6.56 us: attention_weights(): return (raised / jnp.sum(raised, axis=-1, keepdims=True)).reshape(layout)]
    all_to_all x3 -> x1, local copies, waits for them, and re-layouts: 7.75 us -> 0.27 us  [on_device(): lax.all_to_all(attended_grad, 'head', split_axis=1, concat_axis=0, tiled=...]
  transfers between devices with their start and end apart: 10 -> 9, of which waited for: 10 -> 9; matrix products, arithmetic and copies ran while one was open for 2% -> 1% of each run, Pallas kernels for 0% -> 0%
where the time goes in v1:
time: 597 us; the launch traced here: 595 us
  waiting for transfers between devices  438 us (73%)
  Pallas kernels  42.7 us (7%)
  starting transfers between devices  41.5 us (7%)
  other arithmetic  32.4 us (5%)
  local copies, waits for them, and re-layouts  14.1 us (2%)
  between operations  14.1 us (2%)
  blocking collectives  7.92 us (1%)
    psum x1, waiting for transfers between devices, on_device(): lax.psum((in_weight_grad, out_weight_grad), 'node')  179 us
    all_to_all x1, waiting for transfers between devices, on_device(): lax.all_to_all(outgoing, 'node', split_axis=0, concat_axis=0, tiled=True)  94.4 us
    all_to_all x1, waiting for transfers between devices, on_device(): lax.all_to_all(leaving.reshape(node_count, CAP, BLOCK, PAIR), 'node', spl...  94.2 us
    pallas_call x1, Pallas kernels, backward(): pl.pallas_call(backward_kernel, grid_spec=grid_spec, out_shape=(jax.Shape...  32 us
    reduce_scatter x1, waiting for transfers between devices, on_device(): lax.psum_scatter(in_weight_grad, 'head', scatter_dimension=1, tiled=True)  28.6 us
    scatter-add x1, other arithmetic, on_device(): own.at[requests].add(returned).astype(jnp.bfloat16).reshape(node_rows, PAIR)  17 us
    all_to_all x1, starting transfers between devices, on_device(): lax.all_to_all(wanted, 'node', split_axis=1, concat_axis=0, tiled=True)  13.2 us
  transfers between devices with their start and end apart: 9, of which 9 were waited for; matrix products, arithmetic and copies ran while one was open for 1% of the time, Pallas kernels for 0%

profile of v1, /device:TPU:1, one launch (start us, length us, event | category | flops | bytes accessed | tf_op | source)
XLA Modules:
  0.0 595.4 jit_solution(9478361378544169945)
XLA Ops:
  7.2 1.4 copy.34
  8.6 13.2 %all-to-all-start.1 = ((s32[1,64,2]{2,0,1:T(1,128)}), s32[1,64,2]{2,0,1:T(1,128)S(1)}, u32[]{:S(2)}, u32[]{:S(2)}) async-start(s32[1,64,2]{2,0,1:T(1,128)} %copy.34), calls=%async_computation.1 | async-start | bytes 65536 | tf_op jit(solution)/shard_map/all_to_all | solution.py:165
  21.8 1.3 convolution_convert_fusion
  23.1 1.2 copy.32
  24.3 6.8 %all-to-all-done.1 = s32[1,64,2]{2,0,1:T(1,128)S(1)} async-done(((s32[1,64,2]{2,0,1:T(1,128)}), s32[1,64,2]{2,0,1:T(1,128)S(1)}, u32[]{:S(2)}, u32[]{:S(2)}) %all-to-all-start.1) | async-done | bytes 544 | tf_op jit(solution)/shard_map/all_to_all | solution.py:165
  31.1 4.0 all-to-all-start
  35.1 0.5 broadcast.56
  35.6 0.7 reduce.3
  36.5 10.0 %all-to-all-done = bf16[512,4,192]{0,2,1:T(8,128)(2,1)S(1)} async-done(((bf16[512,4,192]{0,2,1:T(8,128)(2,1)}), bf16[512,4,192]{0,2,1:T(8,128)(2,1)S(1)}, u32[]{:S(2)}, u32[]{:S(2)}) %all-to-all-start) | async-done | bytes 786464 | tf_op jit(solution)/shard_map/all_to_all | solution.py:162
  46.5 0.5 copy.33
  47.0 0.2 slice.19
  47.2 3.1 gather_fusion
  50.3 7.0 %all-to-all-start.2 = ((bf16[64,2,128,128]{3,2,1,0:T(8,128)(2,1)}), bf16[64,2,128,128]{3,2,1,0:T(8,128)(2,1)}, u32[]{:S(2)}, u32[]{:S(2)}) async-start(bf16[64,2,128,128]{3,2,1,0:T(8,128)(2,1)} %bitcast.40), calls=%async_computation.2 | async-start | bytes 8388608 | tf_op jit(solution)/shard_map/all_to_all | solution.py:167
  57.6 94.4 %all-to-all-done.2 = bf16[64,2,128,128]{3,2,1,0:T(8,128)(2,1)} async-done(((bf16[64,2,128,128]{3,2,1,0:T(8,128)(2,1)}), bf16[64,2,128,128]{3,2,1,0:T(8,128)(2,1)}, u32[]{:S(2)}, u32[]{:S(2)}) %all-to-all-start.2) | async-done | bytes 4194336 | tf_op jit(solution)/shard_map/all_to_all | solution.py:167
  152.0 2.6 pad_maximum_fusion.table_ref
  154.6 10.8 %attend.1 = (bf16[2048,128]{1,0:T(8,128)(2,1)S(1)}, f32[2048,128]{1,0:T(8,128)S(1)}) custom-call(s32[192]{0:T(256)S(1)} %reshape.92.slots_ref, s32[16]{0:T(128)S(1)} %copy-done.4, bf16[2048,128]{1,0:T(8,128)(2,1)S(1)} %concatenate.17.q_ref, bf16[144,128,128]{2,1,0:T(8,128)(2,1)S(1)} %pad_maximum_fusion.table_ref), custom_call_target="tpu_custom_call" | custom-call | flops 1610612736 | bytes 8388608 | tf_op jit(solution)/shard_map/attend/pallas_call | solution.py:66
  165.4 2.1 copy-done.1
  167.5 1.0 copy-done.5
  168.5 0.2 slice.14
  168.7 0.9 copy.35
  169.6 3.4 all-to-all-start.3
  173.0 0.1 copy.31
  173.3 5.2 all-to-all-done.3
  178.5 0.3 multiply_reduce_fusion
  179.1 0.2 convolution_convert_fusion.1
  179.3 7.9 %all_to_all.92 = bf16[512,4,64]{0,2,1:T(8,128)(2,1)S(1)} all-to-all(bf16[512,4,64]{0,2,1:T(8,128)(2,1)S(1)} %bitcast.53), channel_id=1, replica_groups=mesh['node'=64,'head'=4] {'head'}, dimensions={1} | all-to-all | bytes 524288 | tf_op jit(solution)/shard_map/all_to_all | solution.py:189
  187.2 0.3 copy.37
  187.5 1.1 pad_maximum_fusion.2.qg_ref
  188.6 32.0 %attend_back.1 = (bf16[2048,128]{1,0:T(8,128)(2,1)}, f32[16,128,128]{2,1,0:T(8,128)}, bf16[128,128,128]{2,1,0:T(8,128)(2,1)}) custom-call(s32[192]{0:T(256)} %copy-done.3, s32[16]{0:T(128)} %count_ref.3, bf16[2048,128]{1,0:T(8,128)(2,1)} %pad_maximum_fusion.2.qg_ref, bf16[2048,128]{1,0:T(8,128)(2,1)} %copy-done.2, f32[2048,128]{1,0:T(8,128)} %copy-done.5, ...), custom_call_target="tpu_custom_call" | custom-call | flops 4026531840 | bytes 16777216 | tf_op jit(solution)/shard_map/attend_back/pallas_call | solution.py:139
  220.6 10.3 %all-to-all-start.5 = ((bf16[64,2,128,128]{3,2,1,0:T(8,128)(2,1)}), bf16[64,2,128,128]{3,2,1,0:T(8,128)(2,1)}, u32[]{:S(2)}, u32[]{:S(2)}) async-start(bf16[64,2,128,128]{3,2,1,0:T(8,128)(2,1)} %bitcast.45), calls=%async_computation.5 | async-start | bytes 8388608 | tf_op jit(solution)/shard_map/all_to_all | solution.py:192
  230.9 0.2 copy.38
  231.1 94.2 %all-to-all-done.5 = bf16[64,2,128,128]{3,2,1,0:T(8,128)(2,1)} async-done(((bf16[64,2,128,128]{3,2,1,0:T(8,128)(2,1)}), bf16[64,2,128,128]{3,2,1,0:T(8,128)(2,1)}, u32[]{:S(2)}, u32[]{:S(2)}) %all-to-all-start.5) | async-done | bytes 4194336 | tf_op jit(solution)/shard_map/all_to_all | solution.py:192
  325.3 6.5 %bitcast_convert_fusion = f32[128,128,128]{2,1,0:T(8,128)} fusion(bf16[64,2,128,128]{3,2,1,0:T(8,128)(2,1)} %all-to-all-done.5), kind=kLoop, calls=%fused_computation.3 | loop fusion | flops 2097152 | bytes 12582912 | tf_op jit(solution)/shard_map/reshape | solution.py:195
  331.8 17.0 %scatter_fusion = f32[16,128,128]{2,1,0:T(8,128)S(1)} fusion(f32[16,128,128]{2,1,0:T(8,128)S(1)} %copy-done.6, s32[128]{0:T(128)S(1)} %fusion.6, f32[128,128,128]{2,1,0:T(8,128)} %bitcast_convert_fusion), kind=kCustom, calls=%fused_computation.1 | custom fusion | flops 2097152 | bytes 25166336 | tf_op jit(solution)/shard_map/scatter-add | solution.py:196
  348.9 0.2 copy.39
  349.2 0.9 pad_maximum_fusion.1
  350.1 3.5 all-to-all-start.6
  353.7 1.0 fusion.3
  354.7 8.6 %all-to-all-done.6 = bf16[4,512,192]{1,2,0:T(8,128)(2,1)S(1)} async-done(((bf16[4,512,192]{1,2,0:T(8,128)(2,1)}), bf16[4,512,192]{1,2,0:T(8,128)(2,1)S(1)}, u32[]{:S(2)}, u32[]{:S(2)}) %all-to-all-start.6) | async-done | bytes 786464 | tf_op jit(solution)/shard_map/all_to_all | solution.py:198
  363.3 1.3 convolution_bitcast_fusion
  364.6 0.8 copy.41
  365.4 11.3 %reduce-scatter.5.cloned.1.call-done = f32[64,256]{1,0:T(8,128)} async-done(((f32[256,256]{1,0:T(8,128)}), f32[64,256]{1,0:T(8,128)}) %reduce-scatter.5.cloned.1.call-update) | async-done | bytes 65552 | tf_op jit(solution)/shard_map/reduce_scatter | solution.py:205
  376.7 28.6 %reduce-scatter.3.cloned.1.call-done = f32[256,192]{0,1:T(8,128)} async-done(((f32[256,768]{0,1:T(8,128)}), f32[256,192]{0,1:T(8,128)}) %reduce-scatter.3.cloned.1.call-update) | async-done | bytes 196624 | tf_op jit(solution)/shard_map/reduce_scatter | solution.py:204
  405.3 0.4 fusion
  405.7 0.8 copy.42
  406.5 179.3 %all-reduce.4.cloned.1.call-done = (f32[256,192]{0,1:T(8,128)}, f32[64,256]{1,0:T(8,128)}) async-done(((f32[256,192]{0,1:T(8,128)}, f32[64,256]{1,0:T(8,128)}), (f32[256,192]{0,1:T(8,128)}, f32[64,256]{1,0:T(8,128)})) %all-reduce.4.cloned.1.call-update) | async-done | bytes 262160 | tf_op jit(solution)/shard_map/psum | solution.py:207
  585.8 1.6 broadcast_multiply_fusion
  587.4 1.5 broadcast_multiply_fusion.1
  (40 shorter events, 1.1 us)
Async XLA Ops:
  7.2 14.6 %copy-start = (bf16[256,768]{1,0:T(8,128)(2,1)S(1)}, bf16[256,768]{1,0:T(8,128)(2,1)}, u32[]{:S(2)}) copy-start(bf16[256,768]{1,0:T(8,128)(2,1)} %param.8) | copy-start | bytes 1179652
  8.6 22.5 %all-to-all-start.1 = ((s32[1,64,2]{2,0,1:T(1,128)}), s32[1,64,2]{2,0,1:T(1,128)S(1)}, u32[]{:S(2)}, u32[]{:S(2)}) async-start(s32[1,64,2]{2,0,1:T(1,128)} %copy.34), calls=%async_computation.1 | async-start | bytes 65536 | tf_op jit(solution)/shard_map/all_to_all | solution.py:165
  31.1 15.4 %all-to-all-start = ((bf16[512,4,192]{0,2,1:T(8,128)(2,1)}), bf16[512,4,192]{0,2,1:T(8,128)(2,1)S(1)}, u32[]{:S(2)}, u32[]{:S(2)}) async-start(bf16[512,4,192]{0,2,1:T(8,128)(2,1)} %bitcast), calls=%async_computation | async-start | bytes 1572864 | tf_op jit(solution)/shard_map/all_to_all | solution.py:162
  50.3 7.0 %copy-start.11 = (s32[16,12]{1,0:T(8,128)S(1)}, s32[16,12]{1,0:T(8,128)}, u32[]{:S(2)}) copy-start(s32[16,12]{1,0:T(8,128)} %param.11) | copy-start | bytes 2308
  50.3 101.7 %all-to-all-start.2 = ((bf16[64,2,128,128]{3,2,1,0:T(8,128)(2,1)}), bf16[64,2,128,128]{3,2,1,0:T(8,128)(2,1)}, u32[]{:S(2)}, u32[]{:S(2)}) async-start(bf16[64,2,128,128]{3,2,1,0:T(8,128)(2,1)} %bitcast.40), calls=%async_computation.2 | async-start | bytes 8388608 | tf_op jit(solution)/shard_map/all_to_all | solution.py:167
  57.4 97.2 %copy-start.3 = (s32[192]{0:T(256)}, s32[192]{0:T(256)S(1)}, u32[]{:S(2)}) copy-start(s32[192]{0:T(256)S(1)} %reshape.92.slots_ref) | copy-start | bytes 2308
  152.0 2.6 copy-start.4
  154.6 18.4 %copy-start.7 = (bf16[512,256]{1,0:T(8,128)(2,1)S(1)}, bf16[512,256]{1,0:T(8,128)(2,1)}, u32[]{:S(2)}) copy-start(bf16[512,256]{1,0:T(8,128)(2,1)} %param.7) | copy-start | bytes 786436
  154.6 18.6 %copy-start.10 = (bf16[512,256]{1,0:T(8,128)(2,1)S(1)}, bf16[512,256]{1,0:T(8,128)(2,1)}, u32[]{:S(2)}) copy-start(bf16[512,256]{1,0:T(8,128)(2,1)} %param.10) | copy-start | bytes 786436
  154.6 23.9 %copy-start.8 = (bf16[256,256]{1,0:T(8,128)(2,1)S(1)}, bf16[256,256]{1,0:T(8,128)(2,1)}, u32[]{:S(2)}) copy-start(bf16[256,256]{1,0:T(8,128)(2,1)} %param.9) | copy-start | bytes 393220
  165.4 2.1 copy-start.1
  167.5 1.0 copy-start.5
  168.5 18.7 %copy-start.2 = (bf16[2048,128]{1,0:T(8,128)(2,1)}, bf16[2048,128]{1,0:T(8,128)(2,1)S(1)}, u32[]{:S(2)}) copy-start(bf16[2048,128]{1,0:T(8,128)(2,1)S(1)} %get-tuple-element.9.att_ref) | copy-start | bytes 1572868
  169.6 8.9 %all-to-all-start.3 = ((bf16[4,512,64]{1,2,0:T(8,128)(2,1)}), bf16[4,512,64]{1,2,0:T(8,128)(2,1)S(1)}, u32[]{:S(2)}, u32[]{:S(2)}) async-start(bf16[4,512,64]{1,2,0:T(8,128)(2,1)} %copy.35), calls=%async_computation.3 | async-start | bytes 524288 | tf_op jit(solution)/shard_map/all_to_all | solution.py:173
  220.6 10.3 %copy-start.9 = (bf16[2048,128]{1,0:T(8,128)(2,1)S(1)}, bf16[2048,128]{1,0:T(8,128)(2,1)}, u32[]{:S(2)}) copy-start(bf16[2048,128]{1,0:T(8,128)(2,1)} %get-tuple-element.11) | copy-start | bytes 1572868
  220.6 104.7 %all-to-all-start.5 = ((bf16[64,2,128,128]{3,2,1,0:T(8,128)(2,1)}), bf16[64,2,128,128]{3,2,1,0:T(8,128)(2,1)}, u32[]{:S(2)}, u32[]{:S(2)}) async-start(bf16[64,2,128,128]{3,2,1,0:T(8,128)(2,1)} %bitcast.45), calls=%async_computation.5 | async-start | bytes 8388608 | tf_op jit(solution)/shard_map/all_to_all | solution.py:192
  231.1 100.7 %copy-start.6 = (f32[16,128,128]{2,1,0:T(8,128)S(1)}, f32[16,128,128]{2,1,0:T(8,128)}, u32[]{:S(2)}) copy-start(f32[16,128,128]{2,1,0:T(8,128)} %get-tuple-element.12) | copy-start | bytes 3145732
  350.1 13.1 %all-to-all-start.6 = ((bf16[4,512,192]{1,2,0:T(8,128)(2,1)}), bf16[4,512,192]{1,2,0:T(8,128)(2,1)S(1)}, u32[]{:S(2)}, u32[]{:S(2)}) async-start(bf16[4,512,192]{1,2,0:T(8,128)(2,1)} %pad_maximum_fusion.1), calls=%async_computation.6 | async-start | bytes 1572864 | tf_op jit(solution)/shard_map/all_to_all | solution.py:198
  353.6 23.1 %reduce-scatter.5.cloned.1.call-start = ((), (), s32[]{:S(2)}) async-start(), calls=%async_computation.10 | async-start | bytes 327680 | tf_op jit(solution)/shard_map/reduce_scatter | solution.py:205
  354.7 50.6 %reduce-scatter.3.cloned.1.call-start = ((), (), s32[]{:S(2)}) async-start(), calls=%async_computation.9 | async-start | bytes 983040 | tf_op jit(solution)/shard_map/reduce_scatter | solution.py:204
  364.5 221.3 %all-reduce.4.cloned.1.call-start = ((), (), s32[]{:S(2)}) async-start(), calls=%async_computation.11 | async-start | bytes 524288 | tf_op jit(solution)/shard_map/psum | solution.py:207
Sparse Core Ops, SparseCore 0:
  357.5 19.1 reduce-scatter.4
  379.4 25.8 reduce-scatter.2
  409.4 176.3 all-reduce.3

commit v2 on v1

--- a/solution.py
+++ b/solution.py
@@ -1,3 +1,5 @@
+import functools
+
 import jax
 import jax.numpy as jnp
 from jax import lax
@@ -15,6 +17,7 @@
 SCALE = HD ** (-0.5)
 NT = (((1,), (1,)), ((), ()))
 TN = (((0,), (0,)), ((), ()))
+MESH = pl.DeviceIdType.MESH
 
 
 def dot(a, b, dims=(((1,), (0,)), ((), ()))):
@@ -152,6 +155,136 @@
     )(slots, count, query_grad, attended, stat, table)
 
 
+def torus(node_count):
+    rows = 4 if node_count >= 64 else 2
+    return node_count // (2 * rows), rows * 2
+
+
+def weights_kernel(
+    planes, group, in_ref, out_ref, sum_ref,
+    mine, x_in, x_sum, z_in, z_sum, g_in, piece,
+    x_send, x_recv, z_send, z_recv, g_send, g_recv, p_send, p_recv, f_send, f_recv,
+):
+    node, head = lax.axis_index("node"), lax.axis_index("head")
+    z, g = node // group, node % group
+    rows = sum_ref.shape[2]
+    x_peers = [(node, (head + d) % HEADS) for d in range(1, HEADS)]
+    z_peers = [(((z + d) % planes) * group + g, head) for d in range(1, planes)]
+    g_peers = [(z * group + (g + d) % group, head) for d in range(1, group)]
+    barrier = pltpu.get_barrier_semaphore()
+    for peer in x_peers + z_peers + g_peers:
+        pl.semaphore_signal(barrier, inc=1, device_id=peer, device_id_type=MESH)
+
+    for h in range(HEADS):
+        chunk = jnp.concatenate(
+            [in_ref[h * 3 * HD : (h + 1) * 3 * HD], out_ref[h * HD : (h + 1) * HD]], axis=0
+        )
+        chunk = jnp.concatenate([chunk[:, :128], chunk[:, 128:]], axis=0)
+        mine[h] = chunk.reshape(planes, group, rows, 128)
+    pl.semaphore_wait(barrier, len(x_peers + z_peers + g_peers))
+
+    copies = [
+        pltpu.make_async_remote_copy(
+            mine.at[peer[1]], x_in.at[d], x_send.at[d], x_recv.at[d], device_id=peer, device_id_type=MESH
+        )
+        for d, peer in enumerate(x_peers)
+    ]
+    for copy in copies:
+        copy.start()
+    for copy in copies:
+        copy.wait()
+    x_sum[...] = mine[head] + x_in[0] + x_in[1] + x_in[2]
+
+    copies = [
+        pltpu.make_async_remote_copy(
+            x_sum.at[(z + d + 1) % planes], z_in.at[d], z_send.at[d], z_recv.at[d],
+            device_id=peer, device_id_type=MESH,
+        )
+        for d, peer in enumerate(z_peers)
+    ]
+    for copy in copies:
+        copy.start()
+    for copy in copies:
+        copy.wait()
+    total = x_sum[z]
+    for d in range(planes - 1):
+        total = total + z_in[d]
+    z_sum[...] = total
+
+    copies = [
+        pltpu.make_async_remote_copy(
+            z_sum.at[(g + d + 1) % group], g_in.at[d], g_send.at[d], g_recv.at[d],
+            device_id=peer, device_id_type=MESH,
+        )
+        for d, peer in enumerate(g_peers)
+    ]
+    for copy in copies:
+        copy.start()
+    for copy in copies:
+        copy.wait()
+    total = z_sum[g]
+    for d in range(group - 1):
+        total = total + g_in[d]
+    piece[...] = total
+
+    copies = [
+        pltpu.make_async_remote_copy(
+            piece, sum_ref.at[z, g], p_send.at[d], p_recv.at[d], device_id=peer, device_id_type=MESH
+        )
+        for d, peer in enumerate(g_peers)
+    ]
+    for copy in copies:
+        copy.start()
+    sum_ref[z, g] = total
+    for copy in copies:
+        copy.wait()
+
+    copies = [
+        pltpu.make_async_remote_copy(
+            sum_ref.at[z], sum_ref.at[z], f_send.at[d], f_recv.at[d], device_id=peer, device_id_type=MESH
+        )
+        for d, peer in enumerate(z_peers)
+    ]
+    for copy in copies:
+        copy.start()
+    for copy in copies:
+        copy.wait()
+
+
+def sum_weights(in_grad, out_grad, node_count):
+    planes, group = torus(node_count)
+    rows = 4 * HD * 2 // (planes * group)
+    full = (planes, group, rows, 128)
+    dma = lambda n: pltpu.SemaphoreType.DMA((n,))
+    vmem = pl.BlockSpec(memory_space=pltpu.VMEM)
+    total = pl.pallas_call(
+        functools.partial(weights_kernel, planes, group),
+        out_shape=jax.ShapeDtypeStruct(full, jnp.float32),
+        in_specs=[vmem, vmem],
+        out_specs=vmem,
+        scratch_shapes=[
+            pltpu.VMEM((HEADS,) + full, jnp.float32),
+            pltpu.VMEM((HEADS - 1,) + full, jnp.float32),
+            pltpu.VMEM(full, jnp.float32),
+            pltpu.VMEM((planes - 1,) + full[1:], jnp.float32),
+            pltpu.VMEM(full[1:], jnp.float32),
+            pltpu.VMEM((group - 1,) + full[2:], jnp.float32),
+            pltpu.VMEM(full[2:], jnp.float32),
+            dma(HEADS - 1), dma(HEADS - 1),
+            dma(planes - 1), dma(planes - 1),
+            dma(group - 1), dma(group - 1),
+            dma(group - 1), dma(group - 1),
+            dma(planes - 1), dma(planes - 1),
+        ],
+        compiler_params=pltpu.CompilerParams(
+            collective_id=1, has_side_effects=True, vmem_limit_bytes=32 << 20
+        ),
+        name="sum_weights",
+    )(in_grad, out_grad)
+    total = total.reshape(2, 4 * HD, 128).transpose(1, 0, 2).reshape(4 * HD, 2 * 128)
+    return total[: 3 * HD].T, total[3 * HD :]
+
+
 def on_device(features, in_weight, out_weight, cotangent, key_slots, block_count, wanted):
     node_count = lax.axis_size("node")
     node_rows = BLK * BLOCK
@@ -199,12 +332,10 @@
     feature_grad = norm_grad + jnp.dot(
         grad_rows_back, in_weight.T, preferred_element_type=jnp.float32
     )
-    in_weight_grad = jnp.dot(features.T, grad_rows_back, preferred_element_type=jnp.float32)
-    in_weight_grad, out_weight_grad = (
-        lax.psum_scatter(in_weight_grad, "head", scatter_dimension=1, tiled=True),
-        lax.psum_scatter(out_weight_grad, "head", scatter_dimension=0, tiled=True),
-    )
-    in_weight_grad, out_weight_grad = lax.psum((in_weight_grad, out_weight_grad), "node")
+    in_weight_grad = lax.dot_general(
+        grad_rows_back, features, TN, preferred_element_type=jnp.float32
+    )
+    in_weight_grad, out_weight_grad = sum_weights(in_weight_grad, out_weight_grad, node_count)
     grad_factor = total_nodes ** (-0.5)
     return (
         output,

time: 597 us -> 404 us (0.68)
  waiting for transfers between devices: 438 us -> 219 us
  Pallas kernels: 42.7 us -> 86.4 us
  between operations: 14.1 us -> 0.98 us
    psum x1 -> x0, waiting for transfers between devices: 179 us -> none  [on_device(): lax.psum((in_weight_grad, out_weight_grad), 'node')]
    pallas_call x0 -> x1, Pallas kernels: none -> 43.6 us  [sum_weights(): pl.pallas_call(functools.partial(weights_kernel, planes, group), out_shap...]
    reduce_scatter x2 -> x0, waiting for transfers between devices: 39.9 us -> none  [the longest x1 28.6 us: on_device(): lax.psum_scatter(in_weight_grad, 'head', scatter_dimension=1, tiled=True)]
  transfers between devices with their start and end apart: 9 -> 6, of which waited for: 9 -> 6; matrix products, arithmetic and copies ran while one was open for 1% -> 1% of each run, Pallas kernels for 0% -> 0%
where the time goes in v2:
time: 404 us; the launch traced here: 403 us
  waiting for transfers between devices  219 us (54%)
  Pallas kernels  86.4 us (21%)
  starting transfers between devices  41.4 us (10%)
  other arithmetic  30.7 us (8%)
  local copies, waits for them, and re-layouts  14.2 us (4%)
  blocking collectives  7.92 us (2%)
    all_to_all x1, waiting for transfers between devices, on_device(): lax.all_to_all(outgoing, 'node', split_axis=0, concat_axis=0, tiled=True)  94.4 us
    all_to_all x1, waiting for transfers between devices, on_device(): lax.all_to_all(leaving.reshape(node_count, CAP, BLOCK, PAIR), 'node', spl...  94.2 us
    pallas_call x1, Pallas kernels, sum_weights(): pl.pallas_call(functools.partial(weights_kernel, planes, group), out_shap...  43.6 us
    pallas_call x1, Pallas kernels, backward(): pl.pallas_call(backward_kernel, grid_spec=grid_spec, out_shape=(jax.Shape...  32 us
    scatter-add x1, other arithmetic, on_device(): own.at[requests].add(returned).astype(jnp.bfloat16).reshape(node_rows, PAIR)  17 us
    all_to_all x1, starting transfers between devices, on_device(): lax.all_to_all(wanted, 'node', split_axis=1, concat_axis=0, tiled=True)  13.2 us
    pallas_call x1, Pallas kernels, forward(): pl.pallas_call(forward_kernel, grid_spec=grid_spec, out_shape=(jax.ShapeD...  10.8 us
    all_to_all x1, starting transfers between devices, on_device(): lax.all_to_all(leaving.reshape(node_count, CAP, BLOCK, PAIR), 'node', spl...  10.3 us
  transfers between devices with their start and end apart: 6, of which 6 were waited for; matrix products, arithmetic and copies ran while one was open for 1% of the time, Pallas kernels for 0%

profile of v2, /device:TPU:1, one launch (start us, length us, event | category | flops | bytes accessed | tf_op | source)
XLA Modules:
  0.0 403.3 jit_solution(2310329176614660258)
XLA Ops:
  0.6 1.4 copy.38
  2.1 13.2 %all-to-all-start.1 = ((s32[1,64,2]{2,0,1:T(1,128)}), s32[1,64,2]{2,0,1:T(1,128)S(1)}, u32[]{:S(2)}, u32[]{:S(2)}) async-start(s32[1,64,2]{2,0,1:T(1,128)} %copy.38), calls=%async_computation.1 | async-start | bytes 65536 | tf_op jit(solution)/shard_map/all_to_all | solution.py:298
  15.3 1.3 convolution_convert_fusion
  16.6 1.2 copy.36
  17.8 6.8 %all-to-all-done.1 = s32[1,64,2]{2,0,1:T(1,128)S(1)} async-done(((s32[1,64,2]{2,0,1:T(1,128)}), s32[1,64,2]{2,0,1:T(1,128)S(1)}, u32[]{:S(2)}, u32[]{:S(2)}) %all-to-all-start.1) | async-done | bytes 544 | tf_op jit(solution)/shard_map/all_to_all | solution.py:298
  24.5 4.0 all-to-all-start
  28.6 0.5 broadcast.62
  29.1 0.7 reduce.3
  29.8 0.1 reshape.104
  30.0 10.0 %all-to-all-done = bf16[512,4,192]{0,2,1:T(8,128)(2,1)S(1)} async-done(((bf16[512,4,192]{0,2,1:T(8,128)(2,1)}), bf16[512,4,192]{0,2,1:T(8,128)(2,1)S(1)}, u32[]{:S(2)}, u32[]{:S(2)}) %all-to-all-start) | async-done | bytes 786464 | tf_op jit(solution)/shard_map/all_to_all | solution.py:295
  39.9 0.5 copy.37
  40.4 0.2 slice.29
  40.7 3.1 gather_fusion
  43.7 7.0 %all-to-all-start.2 = ((bf16[64,2,128,128]{3,2,1,0:T(8,128)(2,1)}), bf16[64,2,128,128]{3,2,1,0:T(8,128)(2,1)}, u32[]{:S(2)}, u32[]{:S(2)}) async-start(bf16[64,2,128,128]{3,2,1,0:T(8,128)(2,1)} %bitcast.55), calls=%async_computation.2 | async-start | bytes 8388608 | tf_op jit(solution)/shard_map/all_to_all | solution.py:300
  51.1 94.4 %all-to-all-done.2 = bf16[64,2,128,128]{3,2,1,0:T(8,128)(2,1)} async-done(((bf16[64,2,128,128]{3,2,1,0:T(8,128)(2,1)}), bf16[64,2,128,128]{3,2,1,0:T(8,128)(2,1)}, u32[]{:S(2)}, u32[]{:S(2)}) %all-to-all-start.2) | async-done | bytes 4194336 | tf_op jit(solution)/shard_map/all_to_all | solution.py:300
  145.4 2.6 pad_maximum_fusion.table_ref
  148.1 10.8 %attend.1 = (bf16[2048,128]{1,0:T(8,128)(2,1)S(1)}, f32[2048,128]{1,0:T(8,128)S(1)}) custom-call(s32[192]{0:T(256)S(1)} %reshape.102.slots_ref, s32[16]{0:T(128)S(1)} %copy-done.4, bf16[2048,128]{1,0:T(8,128)(2,1)S(1)} %concatenate.17.q_ref, bf16[144,128,128]{2,1,0:T(8,128)(2,1)S(1)} %pad_maximum_fusion.table_ref), custom_call_target="tpu_custom_call" | custom-call | flops 1610612736 | bytes 8388608 | tf_op jit(solution)/shard_map/attend/pallas_call | solution.py:69
  158.9 2.1 copy-done.1
  161.0 1.0 copy-done.5
  162.0 0.2 slice.22
  162.2 0.9 copy.39
  163.1 3.4 all-to-all-start.3
  166.5 0.1 copy.35
  166.7 0.1 copy.40
  166.8 5.2 %all-to-all-done.3 = bf16[4,512,64]{1,2,0:T(8,128)(2,1)S(1)} async-done(((bf16[4,512,64]{1,2,0:T(8,128)(2,1)}), bf16[4,512,64]{1,2,0:T(8,128)(2,1)S(1)}, u32[]{:S(2)}, u32[]{:S(2)}) %all-to-all-start.3) | async-done | bytes 262176 | tf_op jit(solution)/shard_map/all_to_all | solution.py:306
  172.0 0.3 multiply_reduce_fusion
  172.5 0.2 convolution_convert_fusion.1
  172.8 7.9 %all_to_all.92 = bf16[512,4,64]{0,2,1:T(8,128)(2,1)S(1)} all-to-all(bf16[512,4,64]{0,2,1:T(8,128)(2,1)S(1)} %bitcast.68), channel_id=1, replica_groups=mesh['node'=64,'head'=4] {'head'}, dimensions={1} | all-to-all | bytes 524288 | tf_op jit(solution)/shard_map/all_to_all | solution.py:322
  180.7 0.3 copy.41
  181.0 1.1 pad_maximum_fusion.2.qg_ref
  182.1 32.0 %attend_back.1 = (bf16[2048,128]{1,0:T(8,128)(2,1)}, f32[16,128,128]{2,1,0:T(8,128)}, bf16[128,128,128]{2,1,0:T(8,128)(2,1)}) custom-call(s32[192]{0:T(256)} %copy-done.3, s32[16]{0:T(128)} %count_ref.3, bf16[2048,128]{1,0:T(8,128)(2,1)} %pad_maximum_fusion.2.qg_ref, bf16[2048,128]{1,0:T(8,128)(2,1)} %copy-done.2, f32[2048,128]{1,0:T(8,128)} %copy-done.5, ...), custom_call_target="tpu_custom_call" | custom-call | flops 4026531840 | bytes 16777216 | tf_op jit(solution)/shard_map/attend_back/pallas_call | solution.py:142
  214.1 10.3 %all-to-all-start.5 = ((bf16[64,2,128,128]{3,2,1,0:T(8,128)(2,1)}), bf16[64,2,128,128]{3,2,1,0:T(8,128)(2,1)}, u32[]{:S(2)}, u32[]{:S(2)}) async-start(bf16[64,2,128,128]{3,2,1,0:T(8,128)(2,1)} %bitcast.60), calls=%async_computation.5 | async-start | bytes 8388608 | tf_op jit(solution)/shard_map/all_to_all | solution.py:325
  224.4 0.2 copy.42
  224.6 94.2 %all-to-all-done.5 = bf16[64,2,128,128]{3,2,1,0:T(8,128)(2,1)} async-done(((bf16[64,2,128,128]{3,2,1,0:T(8,128)(2,1)}), bf16[64,2,128,128]{3,2,1,0:T(8,128)(2,1)}, u32[]{:S(2)}, u32[]{:S(2)}) %all-to-all-start.5) | async-done | bytes 4194336 | tf_op jit(solution)/shard_map/all_to_all | solution.py:325
  318.8 6.5 %bitcast_convert_fusion = f32[128,128,128]{2,1,0:T(8,128)} fusion(bf16[64,2,128,128]{3,2,1,0:T(8,128)(2,1)} %all-to-all-done.5), kind=kLoop, calls=%fused_computation.3 | loop fusion | flops 2097152 | bytes 12582912 | tf_op jit(solution)/shard_map/reshape | solution.py:328
  325.3 17.0 %scatter_fusion = f32[16,128,128]{2,1,0:T(8,128)S(1)} fusion(f32[16,128,128]{2,1,0:T(8,128)S(1)} %copy-done.6, s32[128]{0:T(128)S(1)} %fusion.8, f32[128,128,128]{2,1,0:T(8,128)} %bitcast_convert_fusion), kind=kCustom, calls=%fused_computation.1 | custom fusion | flops 2097152 | bytes 25166336 | tf_op jit(solution)/shard_map/scatter-add | solution.py:329
  342.4 0.2 copy.43
  342.7 1.0 pad_maximum_fusion.1
  343.6 3.5 all-to-all-start.6
  347.1 0.8 copy.47
  348.0 0.3 fusion.4.out_ref
  348.2 8.5 %all-to-all-done.6 = bf16[4,512,192]{1,2,0:T(8,128)(2,1)S(1)} async-done(((bf16[4,512,192]{1,2,0:T(8,128)(2,1)}), bf16[4,512,192]{1,2,0:T(8,128)(2,1)S(1)}, u32[]{:S(2)}, u32[]{:S(2)}) %all-to-all-start.6) | async-done | bytes 786464 | tf_op jit(solution)/shard_map/all_to_all | solution.py:331
  356.8 0.4 fusion
  357.1 0.4 fusion.10.in_ref
  357.5 43.6 %sum_weights.1 = f32[8,8,8,128]{3,2,1,0:T(8,128)S(1)} custom-call(f32[768,256]{1,0:T(8,128)S(1)} %fusion.10.in_ref, f32[256,256]{1,0:T(8,128)S(1)} %fusion.4.out_ref), custom_call_target="tpu_custom_call" | custom-call | tf_op jit(solution)/shard_map/sum_weights/pallas_call | solution.py:260
  401.1 0.6 copy_bitcast_fusion
  401.8 0.7 bitcast_bitcast_fusion
  402.5 0.8 copy.48
  (32 shorter events, 0.7 us)
Async XLA Ops:
  0.6 14.6 %copy-start = (bf16[256,768]{1,0:T(8,128)(2,1)S(1)}, bf16[256,768]{1,0:T(8,128)(2,1)}, u32[]{:S(2)}) copy-start(bf16[256,768]{1,0:T(8,128)(2,1)} %param.8) | copy-start | bytes 1179652
  2.1 22.5 %all-to-all-start.1 = ((s32[1,64,2]{2,0,1:T(1,128)}), s32[1,64,2]{2,0,1:T(1,128)S(1)}, u32[]{:S(2)}, u32[]{:S(2)}) async-start(s32[1,64,2]{2,0,1:T(1,128)} %copy.38), calls=%async_computation.1 | async-start | bytes 65536 | tf_op jit(solution)/shard_map/all_to_all | solution.py:298
  24.5 15.4 %all-to-all-start = ((bf16[512,4,192]{0,2,1:T(8,128)(2,1)}), bf16[512,4,192]{0,2,1:T(8,128)(2,1)S(1)}, u32[]{:S(2)}, u32[]{:S(2)}) async-start(bf16[512,4,192]{0,2,1:T(8,128)(2,1)} %bitcast), calls=%async_computation | async-start | bytes 1572864 | tf_op jit(solution)/shard_map/all_to_all | solution.py:295
  43.7 7.0 %copy-start.11 = (s32[16,12]{1,0:T(8,128)S(1)}, s32[16,12]{1,0:T(8,128)}, u32[]{:S(2)}) copy-start(s32[16,12]{1,0:T(8,128)} %param.11) | copy-start | bytes 2308
  43.7 101.7 %all-to-all-start.2 = ((bf16[64,2,128,128]{3,2,1,0:T(8,128)(2,1)}), bf16[64,2,128,128]{3,2,1,0:T(8,128)(2,1)}, u32[]{:S(2)}, u32[]{:S(2)}) async-start(bf16[64,2,128,128]{3,2,1,0:T(8,128)(2,1)} %bitcast.55), calls=%async_computation.2 | async-start | bytes 8388608 | tf_op jit(solution)/shard_map/all_to_all | solution.py:300
  50.9 97.2 %copy-start.3 = (s32[192]{0:T(256)}, s32[192]{0:T(256)S(1)}, u32[]{:S(2)}) copy-start(s32[192]{0:T(256)S(1)} %reshape.102.slots_ref) | copy-start | bytes 2308
  145.4 2.6 copy-start.4
  148.1 18.4 %copy-start.7 = (bf16[512,256]{1,0:T(8,128)(2,1)S(1)}, bf16[512,256]{1,0:T(8,128)(2,1)}, u32[]{:S(2)}) copy-start(bf16[512,256]{1,0:T(8,128)(2,1)} %param.7) | copy-start | bytes 786436
  148.1 18.6 %copy-start.10 = (bf16[512,256]{1,0:T(8,128)(2,1)S(1)}, bf16[512,256]{1,0:T(8,128)(2,1)}, u32[]{:S(2)}) copy-start(bf16[512,256]{1,0:T(8,128)(2,1)} %param.10) | copy-start | bytes 786436
  148.1 23.9 %copy-start.8 = (bf16[256,256]{1,0:T(8,128)(2,1)S(1)}, bf16[256,256]{1,0:T(8,128)(2,1)}, u32[]{:S(2)}) copy-start(bf16[256,256]{1,0:T(8,128)(2,1)} %param.9) | copy-start | bytes 393220
  158.9 2.1 copy-start.1
  161.0 1.0 copy-start.5
  162.0 18.7 %copy-start.2 = (bf16[2048,128]{1,0:T(8,128)(2,1)}, bf16[2048,128]{1,0:T(8,128)(2,1)S(1)}, u32[]{:S(2)}) copy-start(bf16[2048,128]{1,0:T(8,128)(2,1)S(1)} %get-tuple-element.9.att_ref) | copy-start | bytes 1572868
  163.1 8.9 %all-to-all-start.3 = ((bf16[4,512,64]{1,2,0:T(8,128)(2,1)}), bf16[4,512,64]{1,2,0:T(8,128)(2,1)S(1)}, u32[]{:S(2)}, u32[]{:S(2)}) async-start(bf16[4,512,64]{1,2,0:T(8,128)(2,1)} %copy.39), calls=%async_computation.3 | async-start | bytes 524288 | tf_op jit(solution)/shard_map/all_to_all | solution.py:306
  214.1 10.3 %copy-start.9 = (bf16[2048,128]{1,0:T(8,128)(2,1)S(1)}, bf16[2048,128]{1,0:T(8,128)(2,1)}, u32[]{:S(2)}) copy-start(bf16[2048,128]{1,0:T(8,128)(2,1)} %get-tuple-element.11) | copy-start | bytes 1572868
  214.1 104.7 %all-to-all-start.5 = ((bf16[64,2,128,128]{3,2,1,0:T(8,128)(2,1)}), bf16[64,2,128,128]{3,2,1,0:T(8,128)(2,1)}, u32[]{:S(2)}, u32[]{:S(2)}) async-start(bf16[64,2,128,128]{3,2,1,0:T(8,128)(2,1)} %bitcast.60), calls=%async_computation.5 | async-start | bytes 8388608 | tf_op jit(solution)/shard_map/all_to_all | solution.py:325
  224.6 100.7 %copy-start.6 = (f32[16,128,128]{2,1,0:T(8,128)S(1)}, f32[16,128,128]{2,1,0:T(8,128)}, u32[]{:S(2)}) copy-start(f32[16,128,128]{2,1,0:T(8,128)} %get-tuple-element.12) | copy-start | bytes 3145732
  343.6 13.1 %all-to-all-start.6 = ((bf16[4,512,192]{1,2,0:T(8,128)(2,1)}), bf16[4,512,192]{1,2,0:T(8,128)(2,1)S(1)}, u32[]{:S(2)}, u32[]{:S(2)}) async-start(bf16[4,512,192]{1,2,0:T(8,128)(2,1)} %pad_maximum_fusion.1), calls=%async_computation.6 | async-start | bytes 1572864 | tf_op jit(solution)/shard_map/all_to_all | solution.py:331

commit v3 on v2

--- a/solution.py
+++ b/solution.py
@@ -285,23 +285,210 @@
     return total[: 3 * HD].T, total[3 * HD :]
 
 
+def ring_order(planes):
+    half = planes // 2
+    return [0] + [s * k for k in range(1, half) for s in (-1, 1)] + [half]
+
+
+def fetch_kernel(
+    planes, group, own_ref, asked_ref, pairs_ref, mine_ref, query_ref, table_ref, rows_ref, asks_ref,
+    whole, ring, chunk, picked, made, asks,
+    a_send, a_recv, b_send, b_recv, q_send, q_recv, r_send, r_recv, g_send, g_recv, x_send, x_recv, asks_sem,
+):
+    node, head = lax.axis_index("node"), lax.axis_index("head")
+    z, g = node // group, node % group
+    half = planes // 2
+    part = BLOCK // HEADS
+    x_peers = [(node, (head + d) % HEADS) for d in range(1, HEADS)]
+    g_peers = [(z * group + (g + d) % group, head) for d in range(1, group)]
+    right = (((z + 1) % planes) * group + g, head)
+    left = (((z + planes - 1) % planes) * group + g, head)
+
+    def remote(source, target, send, recv, peer):
+        return pltpu.make_async_remote_copy(
+            source, target, send, recv, device_id=peer, device_id_type=MESH
+        )
+
+    def quarter(h):
+        return pl.ds(pl.multiple_of(h * part, part), part)
+
+    barrier = pltpu.get_barrier_semaphore()
+    for peer in x_peers + g_peers + [left, right]:
+        pl.semaphore_signal(barrier, inc=1, device_id=peer, device_id_type=MESH)
+    pl.semaphore_wait(barrier, len(x_peers + g_peers) + 2)
+
+    own_blocks = pl.ds(head * HEADS, HEADS)
+    first, rest = [], []
+    for d, peer in enumerate(x_peers):
+        rows = quarter(peer[1])
+        first.append(
+            remote(own_ref.at[:, rows], whole.at[own_blocks, rows], a_send.at[d], a_recv.at[d], peer)
+        )
+    for e in range(1, HEADS):
+        for d, peer in enumerate(x_peers):
+            rows = quarter((peer[1] + e) % HEADS)
+            rest.append(
+                remote(
+                    own_ref.at[:, rows], whole.at[own_blocks, rows],
+                    b_send.at[d, e - 1], b_recv.at[d, e - 1], peer,
+                )
+            )
+    questions = [
+        remote(asked_ref.at[peer[0] % group], asks_ref.at[g], q_send.at[d], q_recv.at[d], peer)
+        for d, peer in enumerate(g_peers)
+    ]
+    for copy in first + questions + rest:
+        copy.start()
+    whole[own_blocks] = own_ref[...]
+    asks_ref[g] = asked_ref[g]
+    for copy in first:
+        copy.wait_recv()
+    ring[z] = whole[:, quarter(head)]
+
+    def hop(way, k):
+        at = (z - k + planes) % planes if way == 0 else (z + k) % planes
+        view = ring.at[at]
+        if k == half - 1:
+            view = view.at[pl.ds(0, BLK // 2)] if way == 0 else view.at[pl.ds(BLK // 2, BLK // 2)]
+        return remote(
+            view, view, r_send.at[way, k], r_recv.at[way, k], right if way == 0 else left
+        )
+
+    hops = {(way, k): hop(way, k) for way in range(2) for k in range(half)}
+    for way in range(2):
+        hops[way, 0].start()
+    for copy in questions:
+        copy.wait_recv()
+    answer = pltpu.make_async_copy(asks_ref, asks, asks_sem)
+    answer.start()
+    answer.wait()
+
+    order = ring_order(planes)
+    sent = []
+
+    def bring(t):
+        offset = order[t]
+        at = (z + offset + planes) % planes
+        if offset == half:
+            hops[0, half - 1].wait_recv()
+            hops[1, half - 1].wait_recv()
+        elif offset:
+            way, k = (0, -offset) if offset < 0 else (1, offset)
+            hops[way, k - 1].wait_recv()
+            hops[way, k].start()
+        chunk[...] = ring[at]
+        for d in range(group - 1, -1, -1):
+            peer = (g + d) % group
+            for c in range(CAP):
+                block = chunk[asks[peer, 0, at * CAP + c]]
+                if d:
+                    picked[at, d - 1, c] = block
+                else:
+                    rows_ref[at, g, c] = block
+            if d:
+                copy = remote(
+                    picked.at[at, d - 1], rows_ref.at[at, g], g_send.at[at, d - 1], g_recv.at[at, d - 1],
+                    g_peers[d - 1],
+                )
+                copy.start()
+                sent.append(copy)
+
+    arriving = []
+
+    def make(t):
+        at = (z + order[t] + planes) % planes
+        for d in range(1, group):
+            remote(
+                picked.at[at, d - 1], rows_ref.at[at, g], g_send.at[at, d - 1], g_recv.at[at, d - 1],
+                g_peers[d - 1],
+            ).wait_recv()
+        rows = rows_ref[at].reshape(group * CAP * part, 2 * BLOCK)
+        pairs = dot(rows, pairs_ref[...]).astype(jnp.bfloat16)
+        for h in range(HEADS):
+            made[at, h] = pairs[:, h * PAIR : (h + 1) * PAIR].reshape(group * CAP, part, PAIR)
+        slots = pl.ds(BLK + at * group * CAP, group * CAP)
+        for d, peer in enumerate(x_peers):
+            copy = remote(
+                made.at[at, peer[1]], table_ref.at[slots, quarter(head)], x_send.at[at, d], x_recv.at[at, d],
+                peer,
+            )
+            copy.start()
+            sent.append(copy)
+            arriving.append(copy)
+        table_ref[slots, quarter(head)] = made[at, head]
+
+    bring(0)
+    for copy in rest:
+        copy.wait_recv()
+
+    @pl.loop(0, BLK)
+    def _(b):
+        both = dot(whole[b], mine_ref[...])
+        query_ref[b] = (both[:, :PAIR] * SCALE).astype(jnp.bfloat16)
+        table_ref[b] = both[:, PAIR:].astype(jnp.bfloat16)
+
+    for t in range(1, planes):
+        bring(t)
+        make(t - 1)
+    make(planes - 1)
+    for copy in arriving:
+        copy.wait_recv()
+    for copy in first + rest + questions + list(hops.values()) + sent:
+        copy.wait_send()
+
+
+def fetch(features, in_weight, wanted, node_count):
+    planes, group = torus(node_count)
+    part = BLOCK // HEADS
+    head = lax.axis_index("head")
+    own = features.reshape(HEADS, BLOCK, 2 * BLOCK)
+    asked = wanted.reshape(planes, group, CAP).transpose(1, 0, 2).reshape(group, 1, planes * CAP)
+    asked = jnp.pad(asked, ((0, 0), (0, 7), (0, 128 - planes * CAP)))
+    columns = in_weight.reshape(2 * BLOCK, HEADS, 3 * HD)
+    pairs = columns[:, :, HD:].reshape(2 * BLOCK, HEADS * PAIR)
+    mine = lax.dynamic_index_in_dim(columns, head, axis=1, keepdims=False)
+    mine = jnp.concatenate([mine[:, :HD], jnp.zeros_like(mine[:, :HD]), mine[:, HD:]], axis=1)
+    dma = lambda *shape: pltpu.SemaphoreType.DMA(shape)
+    vmem = pl.BlockSpec(memory_space=pltpu.VMEM)
+    slots = BLK + planes * group * CAP
+    return pl.pallas_call(
+        functools.partial(fetch_kernel, planes, group),
+        out_shape=(
+            jax.ShapeDtypeStruct((BLK, BLOCK, PAIR), jnp.bfloat16),
+            jax.ShapeDtypeStruct((slots, BLOCK, PAIR), jnp.bfloat16),
+            jax.ShapeDtypeStruct((planes, group, CAP, part, 2 * BLOCK), jnp.bfloat16),
+            jax.ShapeDtypeStruct((group, 8, 128), jnp.int32),
+        ),
+        in_specs=[vmem] * 4,
+        out_specs=(vmem,) * 4,
+        scratch_shapes=[
+            pltpu.VMEM((BLK, BLOCK, 2 * BLOCK), jnp.bfloat16),
+            pltpu.VMEM((planes, BLK, part, 2 * BLOCK), jnp.bfloat16),
+            pltpu.VMEM((BLK, part, 2 * BLOCK), jnp.bfloat16),
+            pltpu.VMEM((planes, group - 1, CAP, part, 2 * BLOCK), jnp.bfloat16),
+            pltpu.VMEM((planes, HEADS, group * CAP, part, PAIR), jnp.bfloat16),
+            pltpu.SMEM((group, 8, 128), jnp.int32),
+            dma(3), dma(3), dma(3, 3), dma(3, 3), dma(group - 1), dma(group - 1),
+            dma(2, planes // 2), dma(2, planes // 2),
+            dma(planes, group - 1), dma(planes, group - 1), dma(planes, 3), dma(planes, 3),
+            pltpu.SemaphoreType.DMA,
+        ],
+        compiler_params=pltpu.CompilerParams(
+            collective_id=2, has_side_effects=True, vmem_limit_bytes=48 << 20
+        ),
+        name="fetch",
+    )(own, asked, pairs, mine)
+
+
 def on_device(features, in_weight, out_weight, cotangent, key_slots, block_count, wanted):
     node_count = lax.axis_size("node")
     node_rows = BLK * BLOCK
     total_nodes = node_rows * node_count
-    projected = jnp.dot(features, in_weight, preferred_element_type=jnp.float32).astype(
-        jnp.bfloat16
-    )
-    projected = lax.all_to_all(projected, "head", split_axis=1, concat_axis=0, tiled=True)
-    queries = projected[:, :HD] * jnp.bfloat16(SCALE)
-    paired = projected[:, HD:].reshape(BLK, BLOCK, PAIR)
+    queries, table, rows, asks = fetch(features, in_weight, wanted, node_count)
+    queries = queries.reshape(node_rows, PAIR)
     requests = lax.all_to_all(wanted, "node", split_axis=1, concat_axis=0, tiled=True).reshape(-1)
-    outgoing = paired[requests].reshape(node_count, CAP, BLOCK, PAIR)
-    incoming = lax.all_to_all(outgoing, "node", split_axis=0, concat_axis=0, tiled=True)
-    table = jnp.concatenate([paired, incoming.reshape(node_count * CAP, BLOCK, PAIR)], axis=0)
     slots = key_slots.reshape(-1)
-    padded = jnp.concatenate([queries, jnp.zeros_like(queries)], axis=1)
-    wide, stat = forward(slots, block_count, padded, table)
+    wide, stat = forward(slots, block_count, queries, table)
     attended = wide[:, HD:]
     attended_rows = lax.all_to_all(attended, "head", split_axis=0, concat_axis=1, tiled=True)
     summed = features.astype(jnp.float32) + jnp.dot(
@@ -320,7 +507,7 @@
         jnp.bfloat16
     )
     attended_grad = lax.all_to_all(attended_grad, "head", split_axis=1, concat_axis=0, tiled=True)
-    both = jnp.concatenate([queries, attended_grad], axis=1)
+    both = jnp.concatenate([queries[:, :HD], attended_grad], axis=1)
     dq, own, leaving = backward(slots, block_count, both, wide, stat, table)
     returned = lax.all_to_all(
         leaving.reshape(node_count, CAP, BLOCK, PAIR), "node", split_axis=0, concat_axis=0, tiled=True

time: 404 us -> 352 us (0.87)
  waiting for transfers between devices: 219 us -> 111 us
  Pallas kernels: 86.4 us -> 163 us
  starting transfers between devices: 41.4 us -> 31.4 us
  blocking collectives: 7.92 us -> 0 us
    all_to_all x2 -> x1, waiting for transfers between devices: 104 us -> 4.77 us  [on_device(): lax.all_to_all(attended_grad, 'head', split_axis=1, concat_axis=0, tiled=...]
    pallas_call x0 -> x1, Pallas kernels: none -> 76.6 us  [fetch(): pl.pallas_call(functools.partial(fetch_kernel, planes, group), out_shape=...]
    all_to_all x1 -> x0, blocking collectives: 7.92 us -> none  [on_device(): lax.all_to_all(attended_grad, 'head', split_axis=1, concat_axis=0, tiled=...]
    all_to_all x2 -> x1, starting transfers between devices: 11 us -> 3.41 us  [on_device(): lax.all_to_all(attended_grad, 'head', split_axis=1, concat_axis=0, tiled=...]
    all_to_all x1, waiting for transfers between devices: 6.79 us -> 0.01 us  [on_device(): lax.all_to_all(wanted, 'node', split_axis=1, concat_axis=0, tiled=True)]
    unnamed x29 -> x34, local copies, waits for them, and re-layouts: 6.55 us -> 8.87 us
  transfers between devices with their start and end apart: 6 -> 5, of which waited for: 6 -> 4; matrix products, arithmetic and copies ran while one was open for 1% -> 1% of each run, Pallas kernels for 0% -> 9%
where the time goes in v3:
time: 352 us; the launch traced here: 351 us
  Pallas kernels  163 us (46%)
  waiting for transfers between devices  111 us (32%)
  starting transfers between devices  31.4 us (9%)
  other arithmetic  28.8 us (8%)
  local copies, waits for them, and re-layouts  13.4 us (4%)
    all_to_all x1, waiting for transfers between devices, on_device(): lax.all_to_all(leaving.reshape(node_count, CAP, BLOCK, PAIR), 'node', spl...  92.8 us
    pallas_call x1, Pallas kernels, fetch(): pl.pallas_call(functools.partial(fetch_kernel, planes, group), out_shape=...  76.6 us
    pallas_call x1, Pallas kernels, sum_weights(): pl.pallas_call(functools.partial(weights_kernel, planes, group), out_shap...  43.6 us
    pallas_call x1, Pallas kernels, backward(): pl.pallas_call(backward_kernel, grid_spec=grid_spec, out_shape=(jax.Shape...  32 us
    scatter-add x1, other arithmetic, on_device(): own.at[requests].add(returned).astype(jnp.bfloat16).reshape(node_rows, PAIR)  17 us
    pallas_call x1, Pallas kernels, forward(): pl.pallas_call(forward_kernel, grid_spec=grid_spec, out_shape=(jax.ShapeD...  10.7 us
    all_to_all x1, starting transfers between devices, on_device(): lax.all_to_all(leaving.reshape(node_count, CAP, BLOCK, PAIR), 'node', spl...  10.6 us
    all_to_all x1, starting transfers between devices, on_device(): lax.all_to_all(wanted, 'node', split_axis=1, concat_axis=0, tiled=True)  10.4 us
  transfers between devices with their start and end apart: 5, of which 4 were waited for; matrix products, arithmetic and copies ran while one was open for 1% of the time, Pallas kernels for 9%

profile of v3, /device:TPU:1, one launch (start us, length us, event | category | flops | bytes accessed | tf_op | source)
XLA Modules:
  0.0 351.1 jit_solution(11688889912497068471)
XLA Ops:
  0.6 1.2 copy.43
  1.9 0.1 copy.45
  2.1 0.8 reshape.108.slots_ref
  2.9 0.8 reshape.110
  3.8 0.1 copy.58.pairs_ref
  4.1 0.9 copy-done.1
  5.0 76.6 %fetch.1 = (bf16[16,128,128]{2,1,0:T(8,128)(2,1)S(1)}, bf16[144,128,128]{2,1,0:T(8,128)(2,1)}, bf16[8,8,2,32,256]{4,3,2,1,0:T(8,128)(2,1)}, s32[8,8,128]{2,1,0:T(8,128)}) custom-call(bf16[4,128,256]{2,1,0:T(8,128)(2,1)S(1)} %bitcast.53, s32[8,8,128]{2,1,0:T(8,128)S(1)} %pad.4.asked_ref, bf16[256,512]{1,0:T(8,128)(2,1)S(1)} %copy.58.pairs_ref, ...), custom_call_target="tpu_custom_call" | custom-call | tf_op jit(solution)/shard_map/fetch/pallas_call | solution.py:454
  81.7 2.4 copy-done.5
  84.0 0.7 copy-done.6
  84.7 10.7 %attend.1 = (bf16[2048,128]{1,0:T(8,128)(2,1)S(1)}, f32[2048,128]{1,0:T(8,128)S(1)}) custom-call(s32[192]{0:T(256)S(1)} %reshape.108.slots_ref, s32[16]{0:T(128)S(1)} %copy-done.6, bf16[2048,128]{1,0:T(8,128)(2,1)S(1)} %bitcast.56, bf16[144,128,128]{2,1,0:T(8,128)(2,1)S(1)} %copy-done.5), custom_call_target="tpu_custom_call" | custom-call | flops 1610612736 | bytes 8388608 | tf_op jit(solution)/shard_map/attend/pallas_call | solution.py:69
  95.5 1.0 copy-done.7
  96.4 0.2 slice.29
  96.7 0.9 copy.46
  97.6 3.4 all-to-all-start
  101.0 0.1 copy.40
  101.1 0.1 copy.47
  101.3 5.2 %all-to-all-done = bf16[4,512,64]{1,2,0:T(8,128)(2,1)S(1)} async-done(((bf16[4,512,64]{1,2,0:T(8,128)(2,1)}), bf16[4,512,64]{1,2,0:T(8,128)(2,1)S(1)}, u32[]{:S(2)}, u32[]{:S(2)}) %all-to-all-start) | async-done | bytes 262176 | tf_op jit(solution)/shard_map/all_to_all | solution.py:493
  106.5 0.3 multiply_reduce_fusion
  106.8 0.1 fusion.1
  106.9 0.8 fusion.2
  107.7 0.9 convolution_convert_fusion
  108.7 3.4 all-to-all-start.1
  112.1 0.7 copy.49
  112.8 4.8 %all-to-all-done.1 = bf16[512,4,64]{0,2,1:T(8,128)(2,1)S(1)} async-done(((bf16[512,4,64]{0,2,1:T(8,128)(2,1)}), bf16[512,4,64]{0,2,1:T(8,128)(2,1)S(1)}, u32[]{:S(2)}, u32[]{:S(2)}) %all-to-all-start.1) | async-done | bytes 262176 | tf_op jit(solution)/shard_map/all_to_all | solution.py:509
  117.6 10.4 %all-to-all-start.2 = ((s32[1,64,2]{2,0,1:T(1,128)}), s32[1,64,2]{2,0,1:T(1,128)S(1)}, u32[]{:S(2)}, u32[]{:S(2)}) async-start(s32[1,64,2]{2,0,1:T(1,128)} %copy.49), calls=%async_computation.2 | async-start | bytes 65536 | tf_op jit(solution)/shard_map/all_to_all | solution.py:489
  128.0 0.3 copy.48
  128.3 1.1 pad_maximum_fusion.1.qg_ref
  129.4 32.0 %attend_back.1 = (bf16[2048,128]{1,0:T(8,128)(2,1)}, f32[16,128,128]{2,1,0:T(8,128)}, bf16[128,128,128]{2,1,0:T(8,128)(2,1)}) custom-call(s32[192]{0:T(256)} %copy-done.4, s32[16]{0:T(128)} %count_ref.3, bf16[2048,128]{1,0:T(8,128)(2,1)} %pad_maximum_fusion.1.qg_ref, bf16[2048,128]{1,0:T(8,128)(2,1)} %copy-done.3, f32[2048,128]{1,0:T(8,128)} %copy-done.7, ...), custom_call_target="tpu_custom_call" | custom-call | flops 4026531840 | bytes 16777216 | tf_op jit(solution)/shard_map/attend_back/pallas_call | solution.py:142
  161.4 10.6 %all-to-all-start.3 = ((bf16[64,2,128,128]{3,2,1,0:T(8,128)(2,1)}), bf16[64,2,128,128]{3,2,1,0:T(8,128)(2,1)}, u32[]{:S(2)}, u32[]{:S(2)}) async-start(bf16[64,2,128,128]{3,2,1,0:T(8,128)(2,1)} %bitcast.60), calls=%async_computation.3 | async-start | bytes 8388608 | tf_op jit(solution)/shard_map/all_to_all | solution.py:512
  172.0 0.5 broadcast.50
  172.5 0.7 reduce.3
  173.3 0.1 reshape.115
  173.4 0.2 copy.50
  173.7 92.8 %all-to-all-done.3 = bf16[64,2,128,128]{3,2,1,0:T(8,128)(2,1)} async-done(((bf16[64,2,128,128]{3,2,1,0:T(8,128)(2,1)}), bf16[64,2,128,128]{3,2,1,0:T(8,128)(2,1)}, u32[]{:S(2)}, u32[]{:S(2)}) %all-to-all-start.3) | async-done | bytes 4194336 | tf_op jit(solution)/shard_map/all_to_all | solution.py:512
  266.4 6.6 %bitcast_convert_fusion = f32[128,128,128]{2,1,0:T(8,128)} fusion(bf16[64,2,128,128]{3,2,1,0:T(8,128)(2,1)} %all-to-all-done.3), kind=kLoop, calls=%fused_computation.1 | loop fusion | flops 2097152 | bytes 12582912 | tf_op jit(solution)/shard_map/reshape | solution.py:515
  273.0 17.0 %scatter_fusion = f32[16,128,128]{2,1,0:T(8,128)S(1)} fusion(f32[16,128,128]{2,1,0:T(8,128)S(1)} %copy-done.8, s32[128]{0:T(128)S(1)} %fusion.8, f32[128,128,128]{2,1,0:T(8,128)} %bitcast_convert_fusion), kind=kCustom, calls=%fused_computation | custom fusion | flops 2097152 | bytes 25166336 | tf_op jit(solution)/shard_map/scatter-add | solution.py:516
  290.2 0.2 copy.51
  290.4 0.9 pad_maximum_fusion
  291.4 3.5 all-to-all-start.4
  294.9 0.8 copy.55
  295.7 0.3 fusion.4.out_ref
  296.0 8.5 %all-to-all-done.4 = bf16[4,512,192]{1,2,0:T(8,128)(2,1)S(1)} async-done(((bf16[4,512,192]{1,2,0:T(8,128)(2,1)}), bf16[4,512,192]{1,2,0:T(8,128)(2,1)S(1)}, u32[]{:S(2)}, u32[]{:S(2)}) %all-to-all-start.4) | async-done | bytes 786464 | tf_op jit(solution)/shard_map/all_to_all | solution.py:518
  304.5 0.4 fusion
  304.9 0.4 fusion.10.in_ref
  305.3 43.6 %sum_weights.1 = f32[8,8,8,128]{3,2,1,0:T(8,128)S(1)} custom-call(f32[768,256]{1,0:T(8,128)S(1)} %fusion.10.in_ref, f32[256,256]{1,0:T(8,128)S(1)} %fusion.4.out_ref), custom_call_target="tpu_custom_call" | custom-call | tf_op jit(solution)/shard_map/sum_weights/pallas_call | solution.py:260
  348.9 0.6 copy_bitcast_fusion
  349.5 0.7 bitcast_bitcast_fusion
  350.2 0.8 copy.56
  (39 shorter events, 0.5 us)
Async XLA Ops:
  0.6 105.8 %copy-start = (bf16[256,256]{1,0:T(8,128)(2,1)S(1)}, bf16[256,256]{1,0:T(8,128)(2,1)}, u32[]{:S(2)}) copy-start(bf16[256,256]{1,0:T(8,128)(2,1)} %param.9) | copy-start | bytes 393220
  2.9 93.7 %copy-start.4 = (s32[192]{0:T(256)}, s32[192]{0:T(256)S(1)}, u32[]{:S(2)}) copy-start(s32[192]{0:T(256)S(1)} %reshape.108.slots_ref) | copy-start | bytes 2308
  4.0 1.0 copy-start.1
  81.6 19.3 %copy-start.2 = (bf16[512,256]{1,0:T(8,128)(2,1)S(1)}, bf16[512,256]{1,0:T(8,128)(2,1)}, u32[]{:S(2)}) copy-start(bf16[512,256]{1,0:T(8,128)(2,1)} %param.7) | copy-start | bytes 786436
  81.7 2.4 copy-start.5
  84.0 0.7 copy-start.6
  84.7 16.4 %copy-start.12 = (bf16[512,256]{1,0:T(8,128)(2,1)S(1)}, bf16[512,256]{1,0:T(8,128)(2,1)}, u32[]{:S(2)}) copy-start(bf16[512,256]{1,0:T(8,128)(2,1)} %param.10) | copy-start | bytes 786436
  95.5 1.0 copy-start.7
  96.4 12.2 %copy-start.3 = (bf16[2048,128]{1,0:T(8,128)(2,1)}, bf16[2048,128]{1,0:T(8,128)(2,1)S(1)}, u32[]{:S(2)}) copy-start(bf16[2048,128]{1,0:T(8,128)(2,1)S(1)} %get-tuple-element.13.att_ref) | copy-start | bytes 1572868
  96.4 15.6 %copy-start.13 = (s32[1,64,2]{1,2,0:T(2,128)S(1)}, s32[1,64,2]{1,2,0:T(2,128)}, u32[]{:S(2)}) copy-start(s32[1,64,2]{1,2,0:T(2,128)} %param.13) | copy-start | bytes 1540
  97.6 8.9 %all-to-all-start = ((bf16[4,512,64]{1,2,0:T(8,128)(2,1)}), bf16[4,512,64]{1,2,0:T(8,128)(2,1)S(1)}, u32[]{:S(2)}, u32[]{:S(2)}) async-start(bf16[4,512,64]{1,2,0:T(8,128)(2,1)} %copy.46), calls=%async_computation | async-start | bytes 524288 | tf_op jit(solution)/shard_map/all_to_all | solution.py:493
  108.7 8.9 %all-to-all-start.1 = ((bf16[512,4,64]{0,2,1:T(8,128)(2,1)}), bf16[512,4,64]{0,2,1:T(8,128)(2,1)S(1)}, u32[]{:S(2)}, u32[]{:S(2)}) async-start(bf16[512,4,64]{0,2,1:T(8,128)(2,1)} %bitcast.10), calls=%async_computation.1 | async-start | bytes 524288 | tf_op jit(solution)/shard_map/all_to_all | solution.py:509
  117.6 43.8 %all-to-all-start.2 = ((s32[1,64,2]{2,0,1:T(1,128)}), s32[1,64,2]{2,0,1:T(1,128)S(1)}, u32[]{:S(2)}, u32[]{:S(2)}) async-start(s32[1,64,2]{2,0,1:T(1,128)} %copy.49), calls=%async_computation.2 | async-start | bytes 65536 | tf_op jit(solution)/shard_map/all_to_all | solution.py:489
  161.4 12.1 %copy-start.11 = (bf16[2048,128]{1,0:T(8,128)(2,1)S(1)}, bf16[2048,128]{1,0:T(8,128)(2,1)}, u32[]{:S(2)}) copy-start(bf16[2048,128]{1,0:T(8,128)(2,1)} %get-tuple-element.15) | copy-start | bytes 1572868
  161.4 105.0 %all-to-all-start.3 = ((bf16[64,2,128,128]{3,2,1,0:T(8,128)(2,1)}), bf16[64,2,128,128]{3,2,1,0:T(8,128)(2,1)}, u32[]{:S(2)}, u32[]{:S(2)}) async-start(bf16[64,2,128,128]{3,2,1,0:T(8,128)(2,1)} %bitcast.60), calls=%async_computation.3 | async-start | bytes 8388608 | tf_op jit(solution)/shard_map/all_to_all | solution.py:512
  173.6 99.4 %copy-start.8 = (f32[16,128,128]{2,1,0:T(8,128)S(1)}, f32[16,128,128]{2,1,0:T(8,128)}, u32[]{:S(2)}) copy-start(f32[16,128,128]{2,1,0:T(8,128)} %get-tuple-element.16) | copy-start | bytes 3145732
  290.1 14.4 %copy-start.9 = (bf16[256,768]{1,0:T(8,128)(2,1)S(1)}, bf16[256,768]{1,0:T(8,128)(2,1)}, u32[]{:S(2)}) copy-start(bf16[256,768]{1,0:T(8,128)(2,1)} %param.8) | copy-start | bytes 1179652
  290.2 4.7 %copy-start.10 = (bf16[512,256]{0,1:T(8,128)(2,1)S(1)}, bf16[512,256]{0,1:T(8,128)(2,1)}, u32[]{:S(2)}) copy-start(bf16[512,256]{0,1:T(8,128)(2,1)} %get-tuple-element.31) | copy-start | bytes 786436
  291.4 13.1 %all-to-all-start.4 = ((bf16[4,512,192]{1,2,0:T(8,128)(2,1)}), bf16[4,512,192]{1,2,0:T(8,128)(2,1)S(1)}, u32[]{:S(2)}, u32[]{:S(2)}) async-start(bf16[4,512,192]{1,2,0:T(8,128)(2,1)} %pad_maximum_fusion), calls=%async_computation.4 | async-start | bytes 1572864 | tf_op jit(solution)/shard_map/all_to_all | solution.py:518

commit v4 on v3

--- a/solution.py
+++ b/solution.py
@@ -82,10 +82,9 @@
 
 
 def backward_kernel(
-    slots_ref, count_ref, qg_ref, att_ref, stat_ref, table_ref, dq_ref, own_ref, far_ref, acc_ref
+    slots_ref, count_ref, qg_ref, att_ref, stat_ref, table_ref, dq_ref, grads_ref, acc_ref
 ):
     b = pl.program_id(0)
-    own_slots = own_ref.shape[0]
 
     @pl.when(b == 0)
     def _():
@@ -119,33 +118,30 @@
         grads = dot(pair, stacked, TN)
         for i in range(2):
             acc_ref[slots[i]] += grads[i * BLOCK : (i + 1) * BLOCK]
-    dq_ref[...] = (dq * SCALE).astype(jnp.bfloat16)
+    dq = (dq * SCALE).astype(jnp.bfloat16)
+    dq_ref[0] = jnp.concatenate([dq[:HD, :HD], dq[HD:, :HD]], axis=1)
 
     @pl.when(b == pl.num_programs(0) - 1)
     def _():
-        own_ref[...] = acc_ref[:own_slots]
-        far_ref[...] = acc_ref[own_slots:].astype(jnp.bfloat16)
+        grads_ref[...] = acc_ref[...].astype(jnp.bfloat16)
 
 
 def backward(slots, count, query_grad, attended, stat, table):
-    rows = BLK * BLOCK
-    far = table.shape[0] - BLK
     whole = lambda shape: pl.BlockSpec(shape, lambda b, *_: (0,) * len(shape))
     rowwise = pl.BlockSpec((BLOCK, PAIR), lambda b, *_: (b, 0))
     grid_spec = pltpu.PrefetchScalarGridSpec(
         num_scalar_prefetch=2,
         grid=(BLK,),
         in_specs=[rowwise, rowwise, rowwise, whole(table.shape)],
-        out_specs=[rowwise, whole((BLK, BLOCK, PAIR)), whole((far, BLOCK, PAIR))],
+        out_specs=[pl.BlockSpec((1, HD, PAIR), lambda b, *_: (b, 0, 0)), whole(table.shape)],
         scratch_shapes=[pltpu.VMEM(table.shape, jnp.float32)],
     )
     return pl.pallas_call(
         backward_kernel,
         grid_spec=grid_spec,
         out_shape=(
-            jax.ShapeDtypeStruct((rows, PAIR), jnp.bfloat16),
-            jax.ShapeDtypeStruct((BLK, BLOCK, PAIR), jnp.float32),
-            jax.ShapeDtypeStruct((far, BLOCK, PAIR), jnp.bfloat16),
+            jax.ShapeDtypeStruct((BLK, HD, PAIR), jnp.bfloat16),
+            jax.ShapeDtypeStruct(table.shape, jnp.bfloat16),
         ),
         compiler_params=pltpu.CompilerParams(vmem_limit_bytes=56 << 20),
         cost_estimate=pl.CostEstimate(
@@ -480,13 +476,232 @@
     )(own, asked, pairs, mine)
 
 
+def return_kernel(
+    planes, group, grads_ref, dq_ref, rows_ref, features_ref, norm_ref, pair_ref, single_ref, asks_ref,
+    feature_ref, weight_ref,
+    own_pairs, own_queries, heads, leaving, answers, partial, ring, summed, quarters, acc,
+    o_send, o_recv, q_send, q_recv, x_send, x_recv, g_send, g_recv, r_send, r_recv, f_send, f_recv,
+):
+    node, head = lax.axis_index("node"), lax.axis_index("head")
+    z, g = node // group, node % group
+    half = planes // 2
+    part = BLOCK // HEADS
+    width = group * CAP
+    x_peers = [(node, (head + d) % HEADS) for d in range(1, HEADS)]
+    g_peers = [(z * group + (g + d) % group, head) for d in range(1, group)]
+    right = (((z + 1) % planes) * group + g, head)
+    left = (((z + planes - 1) % planes) * group + g, head)
+
+    def remote(source, target, send, recv, peer):
+        return pltpu.make_async_remote_copy(
+            source, target, send, recv, device_id=peer, device_id_type=MESH
+        )
+
+    def quarter(h):
+        return pl.ds(pl.multiple_of(h * part, part), part)
+
+    barrier = pltpu.get_barrier_semaphore()
+    for peer in x_peers + g_peers + [left, right]:
+        pl.semaphore_signal(barrier, inc=1, device_id=peer, device_id_type=MESH)
+    pl.semaphore_wait(barrier, len(x_peers + g_peers) + 2)
+
+    order = list(reversed(ring_order(planes)))
+    planes_in_order = [(z + offset + planes) % planes for offset in order]
+    sent = []
+    far = [
+        [
+            remote(
+                grads_ref.at[pl.ds(BLK + at * width, width), quarter(peer[1])], heads.at[at, head],
+                x_send.at[at, d], x_recv.at[at, d], peer,
+            )
+            for d, peer in enumerate(x_peers)
+        ]
+        for at in planes_in_order
+    ]
+    own = []
+    for d, peer in enumerate(x_peers):
+        blocks = pl.ds(peer[1] * HEADS, HEADS)
+        own.append(remote(grads_ref.at[blocks], own_pairs.at[head], o_send.at[d], o_recv.at[d], peer))
+        own.append(remote(dq_ref.at[blocks], own_queries.at[head], q_send.at[d], q_recv.at[d], peer))
+
+    def begin(copies):
+        for copy in copies:
+            copy.start()
+            sent.append(copy)
+
+    for t in range(min(3, planes)):
+        begin(far[t])
+    acc[...] = jnp.zeros_like(acc)
+    own_blocks = pl.ds(head * HEADS, HEADS)
+    own_pairs[head] = grads_ref[own_blocks]
+    own_queries[head] = dq_ref[own_blocks]
+
+    def spread(t):
+        at = planes_in_order[t]
+        heads[at, head] = grads_ref[pl.ds(BLK + at * width, width), quarter(head)]
+        for copy in far[t]:
+            copy.wait_recv()
+        if t + 3 < planes:
+            begin(far[t + 3])
+        if t == max(planes - 4, 0):
+            begin(own)
+        pairs = jnp.concatenate(
+            [heads[at, h].reshape(width * part, PAIR) for h in range(HEADS)], axis=1
+        )
+        back = dot(pairs, pair_ref[...]).astype(jnp.bfloat16)
+        leaving[at] = back.reshape(group, CAP, part, 2 * BLOCK)
+        copies = [
+            remote(
+                leaving.at[at, peer[0] % group], answers.at[at, g], g_send.at[at, d], g_recv.at[at, d], peer
+            )
+            for d, peer in enumerate(g_peers)
+        ]
+        begin(copies)
+        answers[at, g] = leaving[at, g]
+        acc[...] += dot(pairs, rows_ref[at].reshape(width * part, 2 * BLOCK), TN)
+        return copies
+
+    def hop(way, step, at):
+        source, target = partial.at[at], ring.at[way, step]
+        if step == 0:
+            blocks = pl.ds(way * (BLK // 2), BLK // 2)
+            source, target = source.at[blocks], target.at[blocks]
+        return remote(
+            source, target, r_send.at[way, step], r_recv.at[way, step], left if way else right
+        )
+
+    def gather(t, copies):
+        at, offset = planes_in_order[t], order[t]
+        for copy in copies:
+            copy.wait_recv()
+        side = width * part
+        column = lax.broadcasted_iota(jnp.int32, (1, side), 1)
+        target = column % part
+        for j in range(width):
+            block = asks_ref[j // CAP, 0, at * CAP + j % CAP]
+            target = target + jnp.where(column // part == j, block * part, 0)
+        row = lax.broadcasted_iota(jnp.int32, (BLK * part, side), 0)
+        chosen = jnp.where(row == target, 1.0, 0.0).astype(jnp.bfloat16)
+        total = dot(chosen, answers[at].reshape(side, 2 * BLOCK)).reshape(BLK, part, 2 * BLOCK)
+        if offset == half:
+            partial[at] = total.astype(jnp.bfloat16)
+            for way in range(2):
+                begin([hop(way, 0, at)])
+            return
+        step = half - 1 - abs(offset)
+        ways = [0] if offset > 0 else [1] if offset < 0 else [0, 1]
+        for way in ways:
+            hop(way, step, at).wait_recv()
+            if step == 0:
+                mid = BLK // 2
+                if way == 0:
+                    total = jnp.concatenate(
+                        [total[:mid] + ring[way, step, :mid].astype(jnp.float32), total[mid:]], axis=0
+                    )
+                else:
+                    total = jnp.concatenate(
+                        [total[:mid], total[mid:] + ring[way, step, mid:].astype(jnp.float32)], axis=0
+                    )
+            else:
+                total = total + ring[way, step].astype(jnp.float32)
+        if offset:
+            partial[at] = total.astype(jnp.bfloat16)
+            begin([hop(ways[0], step + 1, at)])
+        else:
+            summed[...] = total.astype(jnp.bfloat16)
+
+    waiting = None
+    for t in range(planes):
+        copies = spread(t)
+        if t:
+            gather(t - 1, waiting)
+        waiting = copies
+    gather(planes - 1, waiting)
+    final = [
+        remote(
+            summed.at[pl.ds(peer[1] * HEADS, HEADS)], quarters.at[head], f_send.at[d], f_recv.at[d], peer
+        )
+        for d, peer in enumerate(x_peers)
+    ]
+    begin(final)
+    quarters[head] = summed[own_blocks]
+
+    for copy in own:
+        copy.wait_recv()
+    rows = HEADS * BLOCK
+    pairs = jnp.concatenate([own_pairs[h].reshape(rows, PAIR) for h in range(HEADS)], axis=1)
+    queries = jnp.concatenate(
+        [
+            jnp.concatenate(
+                [own_queries[h, :, :, :HD], own_queries[h, :, :, HD:]], axis=1
+            ).reshape(rows, HD)
+            for h in range(HEADS)
+        ],
+        axis=1,
+    )
+    features = features_ref[...]
+    pair_weight = acc[...] + dot(pairs, features, TN)
+    single_weight = dot(queries, features, TN)
+    for h in range(HEADS):
+        weight_ref[h, :HD] = single_weight[h * HD : (h + 1) * HD]
+        weight_ref[h, HD:] = pair_weight[h * PAIR : (h + 1) * PAIR]
+    base = norm_ref[...] + dot(pairs, pair_ref[...]) + dot(queries, single_ref[...])
+    base = base.reshape(HEADS, HEADS, part, 2 * BLOCK)
+    for copy in final:
+        copy.wait_recv()
+    for h in range(HEADS):
+        feature_ref[:, h] = (base[:, h] + quarters[h].astype(jnp.float32)).astype(jnp.bfloat16)
+    for copy in sent:
+        copy.wait_send()
+
+
+def give_back(grads, dq, rows, features, norm_grad, in_weight, asks, node_count):
+    planes, group = torus(node_count)
+    part = BLOCK // HEADS
+    wide = 2 * BLOCK
+    columns = in_weight.T.reshape(HEADS, 3 * HD, wide)
+    pair = columns[:, HD:].reshape(HEADS * PAIR, wide)
+    single = columns[:, :HD].reshape(HEADS * HD, wide)
+    dma = lambda *shape: pltpu.SemaphoreType.DMA(shape)
+    vmem = pl.BlockSpec(memory_space=pltpu.VMEM)
+    low = lambda *shape: pltpu.VMEM(shape, jnp.bfloat16)
+    feature_grad, weight = pl.pallas_call(
+        functools.partial(return_kernel, planes, group),
+        out_shape=(
+            jax.ShapeDtypeStruct((HEADS, HEADS, part, wide), jnp.bfloat16),
+            jax.ShapeDtypeStruct((HEADS, 3 * HD, wide), jnp.float32),
+        ),
+        in_specs=[vmem] * 7 + [pl.BlockSpec(memory_space=pltpu.SMEM)],
+        out_specs=(vmem,) * 2,
+        scratch_shapes=[
+            low(HEADS, HEADS, BLOCK, PAIR),
+            low(HEADS, HEADS, HD, PAIR),
+            low(planes, HEADS, group * CAP, part, PAIR),
+            low(planes, group, CAP, part, wide),
+            low(planes, group, CAP, part, wide),
+            low(planes, BLK, part, wide),
+            low(2, planes // 2, BLK, part, wide),
+            low(BLK, part, wide),
+            low(HEADS, HEADS, part, wide),
+            pltpu.VMEM((HEADS * PAIR, wide), jnp.float32),
+            dma(3), dma(3), dma(3), dma(3), dma(planes, 3), dma(planes, 3),
+            dma(planes, group - 1), dma(planes, group - 1),
+            dma(2, planes // 2), dma(2, planes // 2), dma(3), dma(3),
+        ],
+        compiler_params=pltpu.CompilerParams(
+            collective_id=3, has_side_effects=True, vmem_limit_bytes=56 << 20
+        ),
+        name="give_back",
+    )(grads, dq, rows, features, norm_grad, pair, single, asks)
+    return feature_grad.reshape(HEADS * BLOCK, wide), weight.reshape(HEADS * 3 * HD, wide)
+
+
 def on_device(features, in_weight, out_weight, cotangent, key_slots, block_count, wanted):
     node_count = lax.axis_size("node")
     node_rows = BLK * BLOCK
     total_nodes = node_rows * node_count
     queries, table, rows, asks = fetch(features, in_weight, wanted, node_count)
     queries = queries.reshape(node_rows, PAIR)
-    requests = lax.all_to_all(wanted, "node", split_axis=1, concat_axis=0, tiled=True).reshape(-1)
     slots = key_slots.reshape(-1)
     wide, stat = forward(slots, block_count, queries, table)
     attended = wide[:, HD:]
@@ -508,25 +723,15 @@
     )
     attended_grad = lax.all_to_all(attended_grad, "head", split_axis=1, concat_axis=0, tiled=True)
     both = jnp.concatenate([queries[:, :HD], attended_grad], axis=1)
-    dq, own, leaving = backward(slots, block_count, both, wide, stat, table)
-    returned = lax.all_to_all(
-        leaving.reshape(node_count, CAP, BLOCK, PAIR), "node", split_axis=0, concat_axis=0, tiled=True
-    )
-    returned = returned.astype(jnp.float32).reshape(node_count * CAP, BLOCK, PAIR)
-    pair_grads = own.at[requests].add(returned).astype(jnp.bfloat16).reshape(node_rows, PAIR)
-    projected_grad = jnp.concatenate([dq[:, :HD], pair_grads], axis=1)
-    grad_rows_back = lax.all_to_all(projected_grad, "head", split_axis=0, concat_axis=1, tiled=True)
-    feature_grad = norm_grad + jnp.dot(
-        grad_rows_back, in_weight.T, preferred_element_type=jnp.float32
-    )
-    in_weight_grad = lax.dot_general(
-        grad_rows_back, features, TN, preferred_element_type=jnp.float32
+    dq, grads = backward(slots, block_count, both, wide, stat, table)
+    feature_grad, in_weight_grad = give_back(
+        grads, dq, rows, features, norm_grad, in_weight, asks, node_count
     )
     in_weight_grad, out_weight_grad = sum_weights(in_weight_grad, out_weight_grad, node_count)
     grad_factor = total_nodes ** (-0.5)
     return (
         output,
-        feature_grad.astype(jnp.bfloat16),
+        feature_grad,
         in_weight_grad * grad_factor,
         out_weight_grad * grad_factor,
     )

time: 352 us -> 270 us (0.77)
  waiting for transfers between devices: 111 us -> 9.18 us
  Pallas kernels: 163 us -> 231 us
  other arithmetic: 28.8 us -> 3.64 us
  starting transfers between devices: 31.4 us -> 6.99 us
    all_to_all x3 -> x0, waiting for transfers between devices: 101 us -> none  [the longest x1 92.8 us: on_device(): lax.all_to_all(leaving.reshape(node_count, CAP, BLOCK, PAIR), 'node', spl...]
    pallas_call x0 -> x1, Pallas kernels: none -> 70.3 us  [give_back(): pl.pallas_call(functools.partial(return_kernel, planes, group), out_shape...]
    all_to_all x3 -> x0, starting transfers between devices: 24.6 us -> none  [the longest x1 10.6 us: on_device(): lax.all_to_all(leaving.reshape(node_count, CAP, BLOCK, PAIR), 'node', spl...]
    scatter-add x1 -> x0, other arithmetic: 17 us -> none  [on_device(): own.at[requests].add(returned).astype(jnp.bfloat16).reshape(node_rows, PAIR)]
    reshape x1 -> x0, other arithmetic: 6.6 us -> none  [on_device(): returned.astype(jnp.float32).reshape(node_count * CAP, BLOCK, PAIR)]
    unnamed x34 -> x28, local copies, waits for them, and re-layouts: 8.87 us -> 10.9 us
  transfers between devices with their start and end apart: 5 -> 2, of which waited for: 4 -> 2; matrix products, arithmetic and copies ran while one was open for 1% -> 1% of each run, Pallas kernels for 9% -> 0%
where the time goes in v4:
time: 270 us; the launch traced here: 269 us
  Pallas kernels  231 us (86%)
  local copies, waits for them, and re-layouts  15.8 us (6%)
  waiting for transfers between devices  9.18 us (3%)
  starting transfers between devices  6.99 us (3%)
  other arithmetic  3.64 us (1%)
    pallas_call x1, Pallas kernels, fetch(): pl.pallas_call(functools.partial(fetch_kernel, planes, group), out_shape=...  76 us
    pallas_call x1, Pallas kernels, give_back(): pl.pallas_call(functools.partial(return_kernel, planes, group), out_shape...  70.3 us
    pallas_call x1, Pallas kernels, sum_weights(): pl.pallas_call(functools.partial(weights_kernel, planes, group), out_shap...  42.6 us
    pallas_call x1, Pallas kernels, backward(): pl.pallas_call(backward_kernel, grid_spec=grid_spec, out_shape=(jax.Shape...  31.7 us
    unnamed x28, local copies, waits for them, and re-layouts  10.9 us
    pallas_call x1, Pallas kernels, forward(): pl.pallas_call(forward_kernel, grid_spec=grid_spec, out_shape=(jax.ShapeD...  10.7 us
  transfers between devices with their start and end apart: 2, of which 2 were waited for; matrix products, arithmetic and copies ran while one was open for 1% of the time, Pallas kernels for 0%

profile of v4, /device:TPU:1, one launch (start us, length us, event | category | flops | bytes accessed | tf_op | source)
XLA Modules:
  0.0 269.3 jit_solution(13285916522267852060)
XLA Ops:
  0.6 0.0 copy-start
  0.7 1.2 copy.33
  1.9 0.1 copy.35
  2.0 0.1 slice.40
  2.1 0.8 reshape.72.slots_ref
  2.9 0.0 copy-start.7
  2.9 0.8 reshape.74
  3.7 0.1 copy.32
  3.8 0.1 copy.43.pairs_ref
  3.9 0.1 pad.8.clone
  4.0 0.0 copy-start.1
  4.0 0.9 copy-done.1
  5.0 76.0 %fetch.1 = (bf16[16,128,128]{2,1,0:T(8,128)(2,1)S(1)}, bf16[144,128,128]{2,1,0:T(8,128)(2,1)}, bf16[8,8,2,32,256]{4,3,2,1,0:T(8,128)(2,1)S(1)}, s32[8,8,128]{2,1,0:T(8,128)S(1)}) custom-call(bf16[4,128,256]{2,1,0:T(8,128)(2,1)S(1)} %bitcast.43, s32[8,8,128]{2,1,0:T(8,128)S(1)} %pad.4.asked_ref, bf16[256,512]{1,0:T(8,128)(2,1)S(1)} %copy.43.pairs_ref, ...), custom_call_target="tpu_custom_call" | custom-call | tf_op jit(solution)/shard_map/fetch/pallas_call | solution.py:450
  81.0 0.0 copy-start.3
  81.0 1.3 copy-done.3
  82.3 0.6 copy-done.6
  82.9 2.4 copy-done.8
  85.3 0.7 copy-done.9
  86.0 10.7 %attend.1 = (bf16[2048,128]{1,0:T(8,128)(2,1)S(1)}, f32[2048,128]{1,0:T(8,128)S(1)}) custom-call(s32[192]{0:T(256)S(1)} %reshape.72.slots_ref, s32[16]{0:T(128)S(1)} %copy-done.9, bf16[2048,128]{1,0:T(8,128)(2,1)S(1)} %bitcast.47, bf16[144,128,128]{2,1,0:T(8,128)(2,1)S(1)} %copy-done.8), custom_call_target="tpu_custom_call" | custom-call | flops 1610612736 | bytes 8388608 | tf_op jit(solution)/shard_map/attend/pallas_call | solution.py:69
  96.7 0.0 copy-start.10
  96.7 1.0 copy-done.10
  97.7 0.2 slice.32
  97.9 0.9 copy.36
  98.9 0.0 copy-done.7
  98.9 3.4 %all-to-all-start = ((bf16[4,512,64]{1,2,0:T(8,128)(2,1)}), bf16[4,512,64]{1,2,0:T(8,128)(2,1)S(1)}, u32[]{:S(2)}, u32[]{:S(2)}) async-start(bf16[4,512,64]{1,2,0:T(8,128)(2,1)} %copy.36), calls=%async_computation | async-start | bytes 524288 | tf_op jit(solution)/shard_map/all_to_all | solution.py:708
  102.3 0.7 slice.43
  102.9 0.7 slice.42
  103.7 4.1 %all-to-all-done = bf16[4,512,64]{1,2,0:T(8,128)(2,1)S(1)} async-done(((bf16[4,512,64]{1,2,0:T(8,128)(2,1)}), bf16[4,512,64]{1,2,0:T(8,128)(2,1)S(1)}, u32[]{:S(2)}, u32[]{:S(2)}) %all-to-all-start) | async-done | bytes 262176 | tf_op jit(solution)/shard_map/all_to_all | solution.py:708
  107.8 0.0 copy-done
  107.8 0.0 copy-done.2
  107.8 0.4 multiply_reduce_fusion
  108.2 0.0 copy-done.12
  108.2 0.2 fusion
  108.4 0.9 fusion.1
  109.3 1.0 convolution_convert_fusion
  110.3 3.6 %all-to-all-start.1 = ((bf16[512,4,64]{0,2,1:T(8,128)(2,1)}), bf16[512,4,64]{0,2,1:T(8,128)(2,1)S(1)}, u32[]{:S(2)}, u32[]{:S(2)}) async-start(bf16[512,4,64]{0,2,1:T(8,128)(2,1)} %bitcast.10), calls=%async_computation.1 | async-start | bytes 524288 | tf_op jit(solution)/shard_map/all_to_all | solution.py:724
  113.9 0.2 fusion.3.out_ref
  114.1 5.1 %all-to-all-done.1 = bf16[512,4,64]{0,2,1:T(8,128)(2,1)S(1)} async-done(((bf16[512,4,64]{0,2,1:T(8,128)(2,1)}), bf16[512,4,64]{0,2,1:T(8,128)(2,1)S(1)}, u32[]{:S(2)}, u32[]{:S(2)}) %all-to-all-start.1) | async-done | bytes 262176 | tf_op jit(solution)/shard_map/all_to_all | solution.py:724
  119.2 0.3 copy.38
  119.5 0.0 copy-done.5
  119.5 1.1 pad_maximum_fusion.qg_ref
  120.6 31.7 %attend_back.1 = (bf16[16,64,128]{2,1,0:T(8,128)(2,1)}, bf16[144,128,128]{2,1,0:T(8,128)(2,1)}) custom-call(s32[192]{0:T(256)} %copy-done.7, s32[16]{0:T(128)} %count_ref.3, bf16[2048,128]{1,0:T(8,128)(2,1)} %pad_maximum_fusion.qg_ref, bf16[2048,128]{1,0:T(8,128)(2,1)} %copy-done.5, f32[2048,128]{1,0:T(8,128)} %copy-done.10, ...), custom_call_target="tpu_custom_call" | custom-call | flops 4026531840 | bytes 16777216 | tf_op jit(solution)/shard_map/attend_back/pallas_call | solution.py:139
  152.3 70.3 %give_back.1 = (bf16[4,4,32,256]{3,2,1,0:T(8,128)(2,1)}, f32[4,192,256]{2,1,0:T(8,128)}) custom-call(bf16[144,128,128]{2,1,0:T(8,128)(2,1)} %get-tuple-element.18.grads_ref, bf16[16,64,128]{2,1,0:T(8,128)(2,1)} %get-tuple-element.19.dq_ref, bf16[8,8,2,32,256]{4,3,2,1,0:T(8,128)(2,1)} %copy-done.3, bf16[512,256]{1,0:T(8,128)(2,1)} %features_ref.1, ...), custom_call_target="tpu_custom_call" | custom-call | tf_op jit(solution)/shard_map/give_back/pallas_call | solution.py:668
  222.6 1.1 copy-done.4
  223.8 42.6 %sum_weights.1 = f32[8,8,8,128]{3,2,1,0:T(8,128)S(1)} custom-call(f32[768,256]{1,0:T(8,128)S(1)} %bitcast.46, f32[256,256]{1,0:T(8,128)S(1)} %fusion.3.out_ref), custom_call_target="tpu_custom_call" | custom-call | tf_op jit(solution)/shard_map/sum_weights/pallas_call | solution.py:256
  266.3 0.6 copy_bitcast_fusion
  267.0 0.7 bitcast_bitcast_fusion
  267.7 1.7 copy.49
  (18 shorter events, 0.1 us)
Async XLA Ops:
  0.6 107.1 %copy-start = (bf16[256,256]{1,0:T(8,128)(2,1)S(1)}, bf16[256,256]{1,0:T(8,128)(2,1)}, u32[]{:S(2)}) copy-start(bf16[256,256]{1,0:T(8,128)(2,1)} %param.9) | copy-start | bytes 393220
  2.9 95.9 %copy-start.7 = (s32[192]{0:T(256)}, s32[192]{0:T(256)S(1)}, u32[]{:S(2)}) copy-start(s32[192]{0:T(256)S(1)} %reshape.72.slots_ref) | copy-start | bytes 2308
  4.0 1.0 copy-start.1
  81.0 1.3 copy-start.3
  82.3 0.6 copy-start.6
  82.9 24.8 %copy-start.2 = (bf16[512,256]{1,0:T(8,128)(2,1)S(1)}, bf16[512,256]{1,0:T(8,128)(2,1)}, u32[]{:S(2)}) copy-start(bf16[512,256]{1,0:T(8,128)(2,1)} %features_ref.1) | copy-start | bytes 786436
  82.9 2.4 copy-start.8
  85.3 0.7 copy-start.9
  86.0 22.2 %copy-start.12 = (bf16[512,256]{1,0:T(8,128)(2,1)S(1)}, bf16[512,256]{1,0:T(8,128)(2,1)}, u32[]{:S(2)}) copy-start(bf16[512,256]{1,0:T(8,128)(2,1)} %param.10) | copy-start | bytes 786436
  96.7 1.0 copy-start.10
  97.7 21.8 %copy-start.5 = (bf16[2048,128]{1,0:T(8,128)(2,1)}, bf16[2048,128]{1,0:T(8,128)(2,1)S(1)}, u32[]{:S(2)}) copy-start(bf16[2048,128]{1,0:T(8,128)(2,1)S(1)} %get-tuple-element.16.att_ref) | copy-start | bytes 1572868
  98.9 8.9 %all-to-all-start = ((bf16[4,512,64]{1,2,0:T(8,128)(2,1)}), bf16[4,512,64]{1,2,0:T(8,128)(2,1)S(1)}, u32[]{:S(2)}, u32[]{:S(2)}) async-start(bf16[4,512,64]{1,2,0:T(8,128)(2,1)} %copy.36), calls=%async_computation | async-start | bytes 524288 | tf_op jit(solution)/shard_map/all_to_all | solution.py:708
  109.3 43.0 %copy-start.11 = (f32[512,256]{1,0:T(8,128)}, f32[512,256]{1,0:T(8,128)S(1)}, u32[]{:S(2)}) copy-start(f32[512,256]{1,0:T(8,128)S(1)} %get-tuple-element.24.norm_ref) | copy-start | bytes 1572868
  110.3 8.9 %all-to-all-start.1 = ((bf16[512,4,64]{0,2,1:T(8,128)(2,1)}), bf16[512,4,64]{0,2,1:T(8,128)(2,1)S(1)}, u32[]{:S(2)}, u32[]{:S(2)}) async-start(bf16[512,4,64]{0,2,1:T(8,128)(2,1)} %bitcast.10), calls=%async_computation.1 | async-start | bytes 524288 | tf_op jit(solution)/shard_map/all_to_all | solution.py:724
  222.6 1.1 copy-start.4

commit v5 on v4

--- a/solution.py
+++ b/solution.py
@@ -32,19 +32,21 @@
     scores = []
     for j in range(0, PER, 2):
         pair = dot(query, jnp.concatenate(chosen[j : j + 2], axis=0), NT)
-        key = lax.broadcasted_iota(jnp.int32, pair.shape, 1) + j * BLOCK
-        scores.append(jnp.where(key < count * BLOCK, pair, -1e30))
+        for i in range(2):
+            dead = jnp.where(j + i < count, 0.0, -1e30)
+            scores.append(pair[:, i * BLOCK : (i + 1) * BLOCK] + dead)
     highest = scores[0]
     for part in scores[1:]:
         highest = jnp.maximum(highest, part)
     highest = jnp.max(highest, axis=1, keepdims=True)
-    total = jnp.zeros((BLOCK, 2 * BLOCK), jnp.float32)
+    total = jnp.zeros((BLOCK, BLOCK), jnp.float32)
     result = jnp.zeros((BLOCK, PAIR), jnp.float32)
-    for j, part in enumerate(scores):
-        raised = jnp.exp(part - highest)
-        total = total + raised
+    for j in range(0, PER, 2):
+        raised = [jnp.exp(part - highest) for part in scores[j : j + 2]]
+        total = total + raised[0] + raised[1]
         result = result + dot(
-            raised.astype(jnp.bfloat16), jnp.concatenate(chosen[2 * j : 2 * j + 2], axis=0)
+            jnp.concatenate([x.astype(jnp.bfloat16) for x in raised], axis=1),
+            jnp.concatenate(chosen[j : j + 2], axis=0),
         )
     total = jnp.sum(total, axis=1, keepdims=True)
     out_ref[...] = (result / total).astype(jnp.bfloat16)
@@ -102,23 +104,27 @@
         axis=1,
         keepdims=True,
     )
-    highest = stat_ref[:, 0:1]
-    inverse = stat_ref[:, HD : HD + 1]
-    dq = jnp.zeros((BLOCK, PAIR), jnp.float32)
+    flipped = jnp.where((lane >= 32) & (lane < HD), dots, stat_ref[...]).T
+    highest, dots, inverse = flipped[0:1], flipped[32:33], flipped[HD : HD + 1]
+    dq = jnp.zeros((PAIR, BLOCK), jnp.float32)
     for j in range(0, PER, 2):
         slots = [slots_ref[b * PER + j + i] for i in range(2)]
         chosen = jnp.concatenate([table_ref[s] for s in slots], axis=0)
-        products = dot(stacked, chosen, NT)
-        key = lax.broadcasted_iota(jnp.int32, (BLOCK, 2 * BLOCK), 1) + j * BLOCK
-        scores = jnp.where(key < count * BLOCK, products[:BLOCK], -1e30)
-        attention = jnp.exp(scores - highest) * inverse
-        score_grad = (attention * (products[BLOCK:] - dots)).astype(jnp.bfloat16)
-        dq = dq + dot(score_grad, chosen)
-        pair = jnp.concatenate([score_grad, attention.astype(jnp.bfloat16)], axis=0)
-        grads = dot(pair, stacked, TN)
+        products = dot(chosen, stacked, NT)
+        terms = []
+        for i in range(2):
+            rows = slice(i * BLOCK, (i + 1) * BLOCK)
+            top = highest + jnp.where(j + i < count, 0.0, 1e30)
+            attention = jnp.exp(products[rows, :BLOCK] - top) * inverse
+            terms.append((attention * (products[rows, BLOCK:] - dots), attention))
+        score_grad, attention = [
+            jnp.concatenate([x.astype(jnp.bfloat16) for x in pair], axis=0) for pair in zip(*terms)
+        ]
+        dq = dq + dot(chosen, score_grad, TN)
+        grads = dot(jnp.concatenate([score_grad, attention], axis=1), stacked)
         for i in range(2):
             acc_ref[slots[i]] += grads[i * BLOCK : (i + 1) * BLOCK]
-    dq = (dq * SCALE).astype(jnp.bfloat16)
+    dq = (dq.T * SCALE).astype(jnp.bfloat16)
     dq_ref[0] = jnp.concatenate([dq[:HD, :HD], dq[HD:, :HD]], axis=1)
 
     @pl.when(b == pl.num_programs(0) - 1)

time: 270 us -> 271 us (level)
  no operation moved by 1% of the time
where the time goes in v5:
time: 271 us
  Pallas kernels  233 us (86%)
  local copies, waits for them, and re-layouts  15.8 us (6%)
  waiting for transfers between devices  9.18 us (3%)
  starting transfers between devices  6.99 us (3%)
  other arithmetic  3.64 us (1%)
    pallas_call x1, Pallas kernels, fetch(): pl.pallas_call(functools.partial(fetch_kernel, planes, group), out_shape=...  76 us
    pallas_call x1, Pallas kernels, give_back(): pl.pallas_call(functools.partial(return_kernel, planes, group), out_shape...  70.2 us
    pallas_call x1, Pallas kernels, sum_weights(): pl.pallas_call(functools.partial(weights_kernel, planes, group), out_shap...  42.6 us
    pallas_call x1, Pallas kernels, backward(): pl.pallas_call(backward_kernel, grid_spec=grid_spec, out_shape=(jax.Shape...  33.2 us
    unnamed x28, local copies, waits for them, and re-layouts  10.9 us
    pallas_call x1, Pallas kernels, forward(): pl.pallas_call(forward_kernel, grid_spec=grid_spec, out_shape=(jax.ShapeD...  10.7 us
  transfers between devices with their start and end apart: 2, of which 2 were waited for; matrix products, arithmetic and copies ran while one was open for 1% of the time, Pallas kernels for 0%

profile of v5, /device:TPU:1, one launch (start us, length us, event | category | flops | bytes accessed | tf_op | source)
XLA Modules:
  0.0 270.8 jit_solution(17070424106110098971)
XLA Ops:
  0.6 0.0 copy-start
  0.7 1.2 copy.33
  1.9 0.1 copy.35
  2.0 0.1 slice.40
  2.1 0.8 reshape.72.slots_ref
  2.9 0.0 copy-start.7
  2.9 0.8 reshape.74
  3.7 0.1 copy.32
  3.8 0.1 copy.43.pairs_ref
  3.9 0.1 pad.8.clone
  4.0 0.0 copy-start.1
  4.0 0.9 copy-done.1
  5.0 76.0 %fetch.1 = (bf16[16,128,128]{2,1,0:T(8,128)(2,1)S(1)}, bf16[144,128,128]{2,1,0:T(8,128)(2,1)}, bf16[8,8,2,32,256]{4,3,2,1,0:T(8,128)(2,1)S(1)}, s32[8,8,128]{2,1,0:T(8,128)S(1)}) custom-call(bf16[4,128,256]{2,1,0:T(8,128)(2,1)S(1)} %bitcast.43, s32[8,8,128]{2,1,0:T(8,128)S(1)} %pad.4.asked_ref, bf16[256,512]{1,0:T(8,128)(2,1)S(1)} %copy.43.pairs_ref, ...), custom_call_target="tpu_custom_call" | custom-call | tf_op jit(solution)/shard_map/fetch/pallas_call | solution.py:456
  81.0 0.0 copy-start.3
  81.0 1.3 copy-done.3
  82.3 0.6 copy-done.6
  82.9 2.4 copy-done.8
  85.3 0.7 copy-done.9
  86.0 10.7 %attend.1 = (bf16[2048,128]{1,0:T(8,128)(2,1)S(1)}, f32[2048,128]{1,0:T(8,128)S(1)}) custom-call(s32[192]{0:T(256)S(1)} %reshape.72.slots_ref, s32[16]{0:T(128)S(1)} %copy-done.9, bf16[2048,128]{1,0:T(8,128)(2,1)S(1)} %bitcast.47, bf16[144,128,128]{2,1,0:T(8,128)(2,1)S(1)} %copy-done.8), custom_call_target="tpu_custom_call" | custom-call | flops 1610612736 | bytes 8388608 | tf_op jit(solution)/shard_map/attend/pallas_call | solution.py:71
  96.7 0.0 copy-start.10
  96.7 1.0 copy-done.10
  97.7 0.2 slice.32
  97.9 0.9 copy.36
  98.8 0.0 copy-done.7
  98.8 3.4 %all-to-all-start = ((bf16[4,512,64]{1,2,0:T(8,128)(2,1)}), bf16[4,512,64]{1,2,0:T(8,128)(2,1)S(1)}, u32[]{:S(2)}, u32[]{:S(2)}) async-start(bf16[4,512,64]{1,2,0:T(8,128)(2,1)} %copy.36), calls=%async_computation | async-start | bytes 524288 | tf_op jit(solution)/shard_map/all_to_all | solution.py:714
  102.2 0.7 slice.43
  102.9 0.7 slice.42
  103.6 4.1 %all-to-all-done = bf16[4,512,64]{1,2,0:T(8,128)(2,1)S(1)} async-done(((bf16[4,512,64]{1,2,0:T(8,128)(2,1)}), bf16[4,512,64]{1,2,0:T(8,128)(2,1)S(1)}, u32[]{:S(2)}, u32[]{:S(2)}) %all-to-all-start) | async-done | bytes 262176 | tf_op jit(solution)/shard_map/all_to_all | solution.py:714
  107.7 0.0 copy-done
  107.7 0.0 copy-done.2
  107.7 0.4 multiply_reduce_fusion
  108.1 0.0 copy-done.12
  108.1 0.2 fusion
  108.4 0.9 fusion.1
  109.3 1.0 convolution_convert_fusion
  110.2 3.6 %all-to-all-start.1 = ((bf16[512,4,64]{0,2,1:T(8,128)(2,1)}), bf16[512,4,64]{0,2,1:T(8,128)(2,1)S(1)}, u32[]{:S(2)}, u32[]{:S(2)}) async-start(bf16[512,4,64]{0,2,1:T(8,128)(2,1)} %bitcast.10), calls=%async_computation.1 | async-start | bytes 524288 | tf_op jit(solution)/shard_map/all_to_all | solution.py:730
  113.8 0.2 fusion.3.out_ref
  114.1 5.1 %all-to-all-done.1 = bf16[512,4,64]{0,2,1:T(8,128)(2,1)S(1)} async-done(((bf16[512,4,64]{0,2,1:T(8,128)(2,1)}), bf16[512,4,64]{0,2,1:T(8,128)(2,1)S(1)}, u32[]{:S(2)}, u32[]{:S(2)}) %all-to-all-start.1) | async-done | bytes 262176 | tf_op jit(solution)/shard_map/all_to_all | solution.py:730
  119.1 0.3 copy.38
  119.4 1.1 pad_maximum_fusion.qg_ref
  120.5 33.2 %attend_back.1 = (bf16[16,64,128]{2,1,0:T(8,128)(2,1)}, bf16[144,128,128]{2,1,0:T(8,128)(2,1)}) custom-call(s32[192]{0:T(256)} %copy-done.7, s32[16]{0:T(128)} %count_ref.3, bf16[2048,128]{1,0:T(8,128)(2,1)} %pad_maximum_fusion.qg_ref, bf16[2048,128]{1,0:T(8,128)(2,1)} %copy-done.5, f32[2048,128]{1,0:T(8,128)} %copy-done.10, ...), custom_call_target="tpu_custom_call" | custom-call | flops 4026531840 | bytes 16777216 | tf_op jit(solution)/shard_map/attend_back/pallas_call | solution.py:145
  153.8 0.0 copy-done.11
  153.8 70.2 %give_back.1 = (bf16[4,4,32,256]{3,2,1,0:T(8,128)(2,1)}, f32[4,192,256]{2,1,0:T(8,128)}) custom-call(bf16[144,128,128]{2,1,0:T(8,128)(2,1)} %get-tuple-element.18.grads_ref, bf16[16,64,128]{2,1,0:T(8,128)(2,1)} %get-tuple-element.19.dq_ref, bf16[8,8,2,32,256]{4,3,2,1,0:T(8,128)(2,1)} %copy-done.3, bf16[512,256]{1,0:T(8,128)(2,1)} %features_ref.1, ...), custom_call_target="tpu_custom_call" | custom-call | tf_op jit(solution)/shard_map/give_back/pallas_call | solution.py:674
  224.0 1.1 copy-done.4
  225.2 42.6 %sum_weights.1 = f32[8,8,8,128]{3,2,1,0:T(8,128)S(1)} custom-call(f32[768,256]{1,0:T(8,128)S(1)} %bitcast.46, f32[256,256]{1,0:T(8,128)S(1)} %fusion.3.out_ref), custom_call_target="tpu_custom_call" | custom-call | tf_op jit(solution)/shard_map/sum_weights/pallas_call | solution.py:262
  267.8 0.6 copy_bitcast_fusion
  268.4 0.7 bitcast_bitcast_fusion
  269.1 1.7 copy.49
  (18 shorter events, 0.1 us)
Async XLA Ops:
  0.6 107.1 %copy-start = (bf16[256,256]{1,0:T(8,128)(2,1)S(1)}, bf16[256,256]{1,0:T(8,128)(2,1)}, u32[]{:S(2)}) copy-start(bf16[256,256]{1,0:T(8,128)(2,1)} %param.9) | copy-start | bytes 393220
  2.9 95.9 %copy-start.7 = (s32[192]{0:T(256)}, s32[192]{0:T(256)S(1)}, u32[]{:S(2)}) copy-start(s32[192]{0:T(256)S(1)} %reshape.72.slots_ref) | copy-start | bytes 2308
  4.0 1.0 copy-start.1
  81.0 1.3 copy-start.3
  82.3 0.6 copy-start.6
  82.9 24.8 %copy-start.2 = (bf16[512,256]{1,0:T(8,128)(2,1)S(1)}, bf16[512,256]{1,0:T(8,128)(2,1)}, u32[]{:S(2)}) copy-start(bf16[512,256]{1,0:T(8,128)(2,1)} %features_ref.1) | copy-start | bytes 786436
  82.9 2.4 copy-start.8
  85.3 0.7 copy-start.9
  86.0 22.1 %copy-start.12 = (bf16[512,256]{1,0:T(8,128)(2,1)S(1)}, bf16[512,256]{1,0:T(8,128)(2,1)}, u32[]{:S(2)}) copy-start(bf16[512,256]{1,0:T(8,128)(2,1)} %param.10) | copy-start | bytes 786436
  96.7 1.0 copy-start.10
  97.7 21.8 %copy-start.5 = (bf16[2048,128]{1,0:T(8,128)(2,1)}, bf16[2048,128]{1,0:T(8,128)(2,1)S(1)}, u32[]{:S(2)}) copy-start(bf16[2048,128]{1,0:T(8,128)(2,1)S(1)} %get-tuple-element.16.att_ref) | copy-start | bytes 1572868
  98.8 8.9 %all-to-all-start = ((bf16[4,512,64]{1,2,0:T(8,128)(2,1)}), bf16[4,512,64]{1,2,0:T(8,128)(2,1)S(1)}, u32[]{:S(2)}, u32[]{:S(2)}) async-start(bf16[4,512,64]{1,2,0:T(8,128)(2,1)} %copy.36), calls=%async_computation | async-start | bytes 524288 | tf_op jit(solution)/shard_map/all_to_all | solution.py:714
  109.3 44.5 %copy-start.11 = (f32[512,256]{1,0:T(8,128)}, f32[512,256]{1,0:T(8,128)S(1)}, u32[]{:S(2)}) copy-start(f32[512,256]{1,0:T(8,128)S(1)} %get-tuple-element.24.norm_ref) | copy-start | bytes 1572868
  110.2 8.9 %all-to-all-start.1 = ((bf16[512,4,64]{0,2,1:T(8,128)(2,1)}), bf16[512,4,64]{0,2,1:T(8,128)(2,1)S(1)}, u32[]{:S(2)}, u32[]{:S(2)}) async-start(bf16[512,4,64]{0,2,1:T(8,128)(2,1)} %bitcast.10), calls=%async_computation.1 | async-start | bytes 524288 | tf_op jit(solution)/shard_map/all_to_all | solution.py:730
  224.0 1.1 copy-start.4

commit v6 on v5

--- a/solution.py
+++ b/solution.py
@@ -14,6 +14,10 @@
 PER = 12
 CAP = 2
 PAIR = 2 * HD
+WIDE = 2 * BLOCK
+SHARED = BLOCK // 2
+PART = SHARED // HEADS
+LUMP = PART + (BLOCK - SHARED) // 2
 SCALE = HD ** (-0.5)
 NT = (((1,), (1,)), ((), ()))
 TN = (((0,), (0,)), ((), ()))
@@ -84,7 +88,7 @@
 
 
 def backward_kernel(
-    slots_ref, count_ref, qg_ref, att_ref, stat_ref, table_ref, dq_ref, grads_ref, acc_ref
+    slots_ref, count_ref, qg_ref, att_ref, stat_ref, table_ref, dq_ref, grads_ref, acc_ref, keys_ref, terms_ref
 ):
     b = pl.program_id(0)
 
@@ -106,24 +110,24 @@
     )
     flipped = jnp.where((lane >= 32) & (lane < HD), dots, stat_ref[...]).T
     highest, dots, inverse = flipped[0:1], flipped[32:33], flipped[HD : HD + 1]
-    dq = jnp.zeros((PAIR, BLOCK), jnp.float32)
+    slots = [slots_ref[b * PER + j] for j in range(PER)]
+    for j in range(PER):
+        keys_ref[j * BLOCK : (j + 1) * BLOCK] = table_ref[slots[j]]
     for j in range(0, PER, 2):
-        slots = [slots_ref[b * PER + j + i] for i in range(2)]
-        chosen = jnp.concatenate([table_ref[s] for s in slots], axis=0)
-        products = dot(chosen, stacked, NT)
-        terms = []
+        products = dot(keys_ref[j * BLOCK : (j + 2) * BLOCK], stacked, NT)
         for i in range(2):
             rows = slice(i * BLOCK, (i + 1) * BLOCK)
             top = highest + jnp.where(j + i < count, 0.0, 1e30)
             attention = jnp.exp(products[rows, :BLOCK] - top) * inverse
-            terms.append((attention * (products[rows, BLOCK:] - dots), attention))
-        score_grad, attention = [
-            jnp.concatenate([x.astype(jnp.bfloat16) for x in pair], axis=0) for pair in zip(*terms)
-        ]
-        dq = dq + dot(chosen, score_grad, TN)
-        grads = dot(jnp.concatenate([score_grad, attention], axis=1), stacked)
+            score_grad = attention * (products[rows, BLOCK:] - dots)
+            terms_ref[(j + i) * BLOCK : (j + i + 1) * BLOCK] = jnp.concatenate(
+                [score_grad.astype(jnp.bfloat16), attention.astype(jnp.bfloat16)], axis=1
+            )
+    dq = dot(keys_ref[...], terms_ref[:, :BLOCK], TN)
+    for j in range(0, PER, 2):
+        grads = dot(terms_ref[j * BLOCK : (j + 2) * BLOCK], stacked)
         for i in range(2):
-            acc_ref[slots[i]] += grads[i * BLOCK : (i + 1) * BLOCK]
+            acc_ref[slots[j + i]] += grads[i * BLOCK : (i + 1) * BLOCK]
     dq = (dq.T * SCALE).astype(jnp.bfloat16)
     dq_ref[0] = jnp.concatenate([dq[:HD, :HD], dq[HD:, :HD]], axis=1)
 
@@ -140,7 +144,11 @@
         grid=(BLK,),
         in_specs=[rowwise, rowwise, rowwise, whole(table.shape)],
         out_specs=[pl.BlockSpec((1, HD, PAIR), lambda b, *_: (b, 0, 0)), whole(table.shape)],
-        scratch_shapes=[pltpu.VMEM(table.shape, jnp.float32)],
+        scratch_shapes=[
+            pltpu.VMEM(table.shape, jnp.float32),
+            pltpu.VMEM((PER * BLOCK, PAIR), jnp.bfloat16),
+            pltpu.VMEM((PER * BLOCK, 2 * BLOCK), jnp.bfloat16),
+        ],
     )
     return pl.pallas_call(
         backward_kernel,
@@ -293,14 +301,14 @@
 
 
 def fetch_kernel(
-    planes, group, own_ref, asked_ref, pairs_ref, mine_ref, query_ref, table_ref, rows_ref, asks_ref,
-    whole, ring, chunk, picked, made, asks,
-    a_send, a_recv, b_send, b_recv, q_send, q_recv, r_send, r_recv, g_send, g_recv, x_send, x_recv, asks_sem,
+    planes, group, own_ref, asked_ref, pairs_ref, mine_ref, query_ref, table_ref, shared_ref, asks_ref,
+    whole, ring, chunk, picked, landed, made, asks,
+    b_send, b_recv, q_send, q_recv, r_send, r_recv, g_send, g_recv, x_send, x_recv, asks_sem,
 ):
     node, head = lax.axis_index("node"), lax.axis_index("head")
     z, g = node // group, node % group
     half = planes // 2
-    part = BLOCK // HEADS
+    part = PART
     x_peers = [(node, (head + d) % HEADS) for d in range(1, HEADS)]
     g_peers = [(z * group + (g + d) % group, head) for d in range(1, group)]
     right = (((z + 1) % planes) * group + g, head)
@@ -322,17 +330,11 @@
     own_blocks = pl.ds(head * HEADS, HEADS)
     first, rest = [], []
     for d, peer in enumerate(x_peers):
-        rows = quarter(peer[1])
-        first.append(
-            remote(own_ref.at[:, rows], whole.at[own_blocks, rows], a_send.at[d], a_recv.at[d], peer)
-        )
-    for e in range(1, HEADS):
-        for d, peer in enumerate(x_peers):
-            rows = quarter((peer[1] + e) % HEADS)
-            rest.append(
+        for e in range(HEADS + 1):
+            rows = pl.ds(SHARED, BLOCK - SHARED) if e == 1 else quarter((peer[1] + max(e - 1, 0)) % HEADS)
+            (first if e < 2 else rest).append(
                 remote(
-                    own_ref.at[:, rows], whole.at[own_blocks, rows],
-                    b_send.at[d, e - 1], b_recv.at[d, e - 1], peer,
+                    own_ref.at[:, rows], whole.at[own_blocks, rows], b_send.at[d, e], b_recv.at[d, e], peer
                 )
             )
     questions = [
@@ -345,7 +347,15 @@
     asks_ref[g] = asked_ref[g]
     for copy in first:
         copy.wait_recv()
-    ring[z] = whole[:, quarter(head)]
+    ring[z, :, :PART] = whole[:, quarter(head)]
+    low = (BLOCK - SHARED) // 2
+
+    @pl.loop(0, BLK)
+    def _(b):
+        pairs = dot(whole[b, SHARED:], mine_ref[:, PAIR:]).astype(jnp.bfloat16)
+        table_ref[b, SHARED:] = pairs
+        ring[z, b, PART:] = jnp.concatenate([pairs[:low], pairs[low:]], axis=1)
+
 
     def hop(way, k):
         at = (z - k + planes) % planes if way == 0 else (z + k) % planes
@@ -386,10 +396,10 @@
                 if d:
                     picked[at, d - 1, c] = block
                 else:
-                    rows_ref[at, g, c] = block
+                    landed[at, g, c] = block
             if d:
                 copy = remote(
-                    picked.at[at, d - 1], rows_ref.at[at, g], g_send.at[at, d - 1], g_recv.at[at, d - 1],
+                    picked.at[at, d - 1], landed.at[at, g], g_send.at[at, d - 1], g_recv.at[at, d - 1],
                     g_peers[d - 1],
                 )
                 copy.start()
@@ -401,11 +411,13 @@
         at = (z + order[t] + planes) % planes
         for d in range(1, group):
             remote(
-                picked.at[at, d - 1], rows_ref.at[at, g], g_send.at[at, d - 1], g_recv.at[at, d - 1],
+                picked.at[at, d - 1], landed.at[at, g], g_send.at[at, d - 1], g_recv.at[at, d - 1],
                 g_peers[d - 1],
             ).wait_recv()
-        rows = rows_ref[at].reshape(group * CAP * part, 2 * BLOCK)
-        pairs = dot(rows, pairs_ref[...]).astype(jnp.bfloat16)
+        rows = landed[at].reshape(group * CAP, LUMP, WIDE)
+        shared = rows[:, :PART].reshape(group * CAP * PART, WIDE)
+        shared_ref[at] = shared
+        pairs = dot(shared, pairs_ref[...]).astype(jnp.bfloat16)
         for h in range(HEADS):
             made[at, h] = pairs[:, h * PAIR : (h + 1) * PAIR].reshape(group * CAP, part, PAIR)
         slots = pl.ds(BLK + at * group * CAP, group * CAP)
@@ -418,6 +430,8 @@
             sent.append(copy)
             arriving.append(copy)
         table_ref[slots, quarter(head)] = made[at, head]
+        table_ref[slots, SHARED : SHARED + low] = rows[:, PART:, :PAIR]
+        table_ref[slots, SHARED + low :] = rows[:, PART:, PAIR:]
 
     bring(0)
     for copy in rest:
@@ -427,7 +441,7 @@
     def _(b):
         both = dot(whole[b], mine_ref[...])
         query_ref[b] = (both[:, :PAIR] * SCALE).astype(jnp.bfloat16)
-        table_ref[b] = both[:, PAIR:].astype(jnp.bfloat16)
+        table_ref[b, :SHARED] = both[:SHARED, PAIR:].astype(jnp.bfloat16)
 
     for t in range(1, planes):
         bring(t)
@@ -441,7 +455,7 @@
 
 def fetch(features, in_weight, wanted, node_count):
     planes, group = torus(node_count)
-    part = BLOCK // HEADS
+    part = PART
     head = lax.axis_index("head")
     own = features.reshape(HEADS, BLOCK, 2 * BLOCK)
     asked = wanted.reshape(planes, group, CAP).transpose(1, 0, 2).reshape(group, 1, planes * CAP)
@@ -458,19 +472,20 @@
         out_shape=(
             jax.ShapeDtypeStruct((BLK, BLOCK, PAIR), jnp.bfloat16),
             jax.ShapeDtypeStruct((slots, BLOCK, PAIR), jnp.bfloat16),
-            jax.ShapeDtypeStruct((planes, group, CAP, part, 2 * BLOCK), jnp.bfloat16),
+            jax.ShapeDtypeStruct((planes, group * CAP * PART, WIDE), jnp.bfloat16),
             jax.ShapeDtypeStruct((group, 8, 128), jnp.int32),
         ),
         in_specs=[vmem] * 4,
         out_specs=(vmem,) * 4,
         scratch_shapes=[
             pltpu.VMEM((BLK, BLOCK, 2 * BLOCK), jnp.bfloat16),
-            pltpu.VMEM((planes, BLK, part, 2 * BLOCK), jnp.bfloat16),
-            pltpu.VMEM((BLK, part, 2 * BLOCK), jnp.bfloat16),
-            pltpu.VMEM((planes, group - 1, CAP, part, 2 * BLOCK), jnp.bfloat16),
+            pltpu.VMEM((planes, BLK, LUMP, WIDE), jnp.bfloat16),
+            pltpu.VMEM((BLK, LUMP, WIDE), jnp.bfloat16),
+            pltpu.VMEM((planes, group - 1, CAP, LUMP, WIDE), jnp.bfloat16),
+            pltpu.VMEM((planes, group, CAP, LUMP, WIDE), jnp.bfloat16),
             pltpu.VMEM((planes, HEADS, group * CAP, part, PAIR), jnp.bfloat16),
             pltpu.SMEM((group, 8, 128), jnp.int32),
-            dma(3), dma(3), dma(3, 3), dma(3, 3), dma(group - 1), dma(group - 1),
+            dma(3, HEADS + 1), dma(3, HEADS + 1), dma(group - 1), dma(group - 1),
             dma(2, planes // 2), dma(2, planes // 2),
             dma(planes, group - 1), dma(planes, group - 1), dma(planes, 3), dma(planes, 3),
             pltpu.SemaphoreType.DMA,
@@ -483,15 +498,16 @@
 
 
 def return_kernel(
-    planes, group, grads_ref, dq_ref, rows_ref, features_ref, norm_ref, pair_ref, single_ref, asks_ref,
+    planes, group, grads_ref, dq_ref, shared_ref, features_ref, norm_ref, pair_ref, single_ref, asks_ref,
     feature_ref, weight_ref,
-    own_pairs, own_queries, heads, leaving, answers, partial, ring, summed, quarters, acc,
-    o_send, o_recv, q_send, q_recv, x_send, x_recv, g_send, g_recv, r_send, r_recv, f_send, f_recv,
+    own_pairs, own_queries, heads, leaving, answers, partial, ring, summed, late, quarters, acc,
+    o_send, o_recv, l_send, l_recv, q_send, q_recv, x_send, x_recv, g_send, g_recv, r_send, r_recv, f_send, f_recv,
 ):
     node, head = lax.axis_index("node"), lax.axis_index("head")
     z, g = node // group, node % group
     half = planes // 2
-    part = BLOCK // HEADS
+    part = PART
+    low = (BLOCK - SHARED) // 2
     width = group * CAP
     x_peers = [(node, (head + d) % HEADS) for d in range(1, HEADS)]
     g_peers = [(z * group + (g + d) % group, head) for d in range(1, group)]
@@ -527,7 +543,12 @@
     own = []
     for d, peer in enumerate(x_peers):
         blocks = pl.ds(peer[1] * HEADS, HEADS)
-        own.append(remote(grads_ref.at[blocks], own_pairs.at[head], o_send.at[d], o_recv.at[d], peer))
+        own.append(
+            remote(
+                grads_ref.at[blocks, pl.ds(0, SHARED)], own_pairs.at[head, :, pl.ds(0, SHARED)],
+                o_send.at[d], o_recv.at[d], peer,
+            )
+        )
         own.append(remote(dq_ref.at[blocks], own_queries.at[head], q_send.at[d], q_recv.at[d], peer))
 
     def begin(copies):
@@ -539,12 +560,13 @@
         begin(far[t])
     acc[...] = jnp.zeros_like(acc)
     own_blocks = pl.ds(head * HEADS, HEADS)
-    own_pairs[head] = grads_ref[own_blocks]
+    own_pairs[head, :, :SHARED] = grads_ref[own_blocks, :SHARED]
     own_queries[head] = dq_ref[own_blocks]
 
     def spread(t):
         at = planes_in_order[t]
-        heads[at, head] = grads_ref[pl.ds(BLK + at * width, width), quarter(head)]
+        slots = pl.ds(BLK + at * width, width)
+        heads[at, head] = grads_ref[slots, quarter(head)]
         for copy in far[t]:
             copy.wait_recv()
         if t + 3 < planes:
@@ -555,7 +577,10 @@
             [heads[at, h].reshape(width * part, PAIR) for h in range(HEADS)], axis=1
         )
         back = dot(pairs, pair_ref[...]).astype(jnp.bfloat16)
-        leaving[at] = back.reshape(group, CAP, part, 2 * BLOCK)
+        leaving[at, :, :, :PART] = back.reshape(group, CAP, part, WIDE)
+        for i in range(2):
+            some = grads_ref[slots, SHARED + i * low : SHARED + (i + 1) * low]
+            leaving[at, :, :, PART:, i * PAIR : (i + 1) * PAIR] = some.reshape(group, CAP, low, PAIR)
         copies = [
             remote(
                 leaving.at[at, peer[0] % group], answers.at[at, g], g_send.at[at, d], g_recv.at[at, d], peer
@@ -564,7 +589,7 @@
         ]
         begin(copies)
         answers[at, g] = leaving[at, g]
-        acc[...] += dot(pairs, rows_ref[at].reshape(width * part, 2 * BLOCK), TN)
+        acc[...] += dot(pairs, shared_ref[at], TN)
         return copies
 
     def hop(way, step, at):
@@ -588,7 +613,15 @@
             target = target + jnp.where(column // part == j, block * part, 0)
         row = lax.broadcasted_iota(jnp.int32, (BLK * part, side), 0)
         chosen = jnp.where(row == target, 1.0, 0.0).astype(jnp.bfloat16)
-        total = dot(chosen, answers[at].reshape(side, 2 * BLOCK)).reshape(BLK, part, 2 * BLOCK)
+        total = jnp.concatenate(
+            [
+                dot(
+                    chosen, answers[at, :, :, i * part : (i + 1) * part].reshape(side, WIDE)
+                ).reshape(BLK, part, WIDE)
+                for i in range(LUMP // part)
+            ],
+            axis=1,
+        )
         if offset == half:
             partial[at] = total.astype(jnp.bfloat16)
             for way in range(2):
@@ -614,7 +647,13 @@
             partial[at] = total.astype(jnp.bfloat16)
             begin([hop(ways[0], step + 1, at)])
         else:
-            summed[...] = total.astype(jnp.bfloat16)
+            summed[...] = total[:, :PART].astype(jnp.bfloat16)
+            for i in range(2):
+                rows = slice(SHARED + i * low, SHARED + (i + 1) * low)
+                fetched = total[:, PART:, i * PAIR : (i + 1) * PAIR]
+                late[:, i * low : (i + 1) * low] = (
+                    grads_ref[:BLK, rows].astype(jnp.float32) + fetched
+                ).astype(jnp.bfloat16)
 
     waiting = None
     for t in range(planes):
@@ -629,10 +668,18 @@
         )
         for d, peer in enumerate(x_peers)
     ]
-    begin(final)
+    tail = [
+        remote(
+            late.at[pl.ds(peer[1] * HEADS, HEADS)], own_pairs.at[head, :, pl.ds(SHARED, BLOCK - SHARED)],
+            l_send.at[d], l_recv.at[d], peer,
+        )
+        for d, peer in enumerate(x_peers)
+    ]
+    begin(tail + final)
+    own_pairs[head, :, SHARED:] = late[own_blocks]
     quarters[head] = summed[own_blocks]
 
-    for copy in own:
+    for copy in own + tail:
         copy.wait_recv()
     rows = HEADS * BLOCK
     pairs = jnp.concatenate([own_pairs[h].reshape(rows, PAIR) for h in range(HEADS)], axis=1)
@@ -652,18 +699,20 @@
         weight_ref[h, :HD] = single_weight[h * HD : (h + 1) * HD]
         weight_ref[h, HD:] = pair_weight[h * PAIR : (h + 1) * PAIR]
     base = norm_ref[...] + dot(pairs, pair_ref[...]) + dot(queries, single_ref[...])
-    base = base.reshape(HEADS, HEADS, part, 2 * BLOCK)
+    base = base.reshape(HEADS, BLOCK, WIDE)
+    feature_ref[:, SHARED:] = base[:, SHARED:].astype(jnp.bfloat16)
     for copy in final:
         copy.wait_recv()
     for h in range(HEADS):
-        feature_ref[:, h] = (base[:, h] + quarters[h].astype(jnp.float32)).astype(jnp.bfloat16)
+        rows = slice(h * part, (h + 1) * part)
+        feature_ref[:, rows] = (base[:, rows] + quarters[h].astype(jnp.float32)).astype(jnp.bfloat16)
     for copy in sent:
         copy.wait_send()
 
 
-def give_back(grads, dq, rows, features, norm_grad, in_weight, asks, node_count):
+def give_back(grads, dq, shared, features, norm_grad, in_weight, asks, node_count):
     planes, group = torus(node_count)
-    part = BLOCK // HEADS
+    part = PART
     wide = 2 * BLOCK
     columns = in_weight.T.reshape(HEADS, 3 * HD, wide)
     pair = columns[:, HD:].reshape(HEADS * PAIR, wide)
@@ -674,7 +723,7 @@
     feature_grad, weight = pl.pallas_call(
         functools.partial(return_kernel, planes, group),
         out_shape=(
-            jax.ShapeDtypeStruct((HEADS, HEADS, part, wide), jnp.bfloat16),
+            jax.ShapeDtypeStruct((HEADS, BLOCK, wide), jnp.bfloat16),
             jax.ShapeDtypeStruct((HEADS, 3 * HD, wide), jnp.float32),
         ),
         in_specs=[vmem] * 7 + [pl.BlockSpec(memory_space=pltpu.SMEM)],
@@ -683,14 +732,15 @@
             low(HEADS, HEADS, BLOCK, PAIR),
             low(HEADS, HEADS, HD, PAIR),
             low(planes, HEADS, group * CAP, part, PAIR),
-            low(planes, group, CAP, part, wide),
-            low(planes, group, CAP, part, wide),
-            low(planes, BLK, part, wide),
-            low(2, planes // 2, BLK, part, wide),
+            low(planes, group, CAP, LUMP, wide),
+            low(planes, group, CAP, LUMP, wide),
+            low(planes, BLK, LUMP, wide),
+            low(2, planes // 2, BLK, LUMP, wide),
             low(BLK, part, wide),
+            low(BLK, BLOCK - SHARED, PAIR),
             low(HEADS, HEADS, part, wide),
             pltpu.VMEM((HEADS * PAIR, wide), jnp.float32),
-            dma(3), dma(3), dma(3), dma(3), dma(planes, 3), dma(planes, 3),
+            dma(3), dma(3), dma(3), dma(3), dma(3), dma(3), dma(planes, 3), dma(planes, 3),
             dma(planes, group - 1), dma(planes, group - 1),
             dma(2, planes // 2), dma(2, planes // 2), dma(3), dma(3),
         ],
@@ -698,7 +748,7 @@
             collective_id=3, has_side_effects=True, vmem_limit_bytes=56 << 20
         ),
         name="give_back",
-    )(grads, dq, rows, features, norm_grad, pair, single, asks)
+    )(grads, dq, shared, features, norm_grad, pair, single, asks)
     return feature_grad.reshape(HEADS * BLOCK, wide), weight.reshape(HEADS * 3 * HD, wide)
 
 
@@ -706,7 +756,7 @@
     node_count = lax.axis_size("node")
     node_rows = BLK * BLOCK
     total_nodes = node_rows * node_count
-    queries, table, rows, asks = fetch(features, in_weight, wanted, node_count)
+    queries, table, shared, asks = fetch(features, in_weight, wanted, node_count)
     queries = queries.reshape(node_rows, PAIR)
     slots = key_slots.reshape(-1)
     wide, stat = forward(slots, block_count, queries, table)
@@ -731,7 +781,7 @@
     both = jnp.concatenate([queries[:, :HD], attended_grad], axis=1)
     dq, grads = backward(slots, block_count, both, wide, stat, table)
     feature_grad, in_weight_grad = give_back(
-        grads, dq, rows, features, norm_grad, in_weight, asks, node_count
+        grads, dq, shared, features, norm_grad, in_weight, asks, node_count
     )
     in_weight_grad, out_weight_grad = sum_weights(in_weight_grad, out_weight_grad, node_count)
     grad_factor = total_nodes ** (-0.5)

time: 271 us -> 251 us (0.926)
  Pallas kernels: 233 us -> 212 us
    pallas_call x1, Pallas kernels: 33.2 us -> 20.2 us  [backward(): pl.pallas_call(backward_kernel, grid_spec=grid_spec, out_shape=(jax.Shape...]
    pallas_call x1, Pallas kernels: 76 us -> 72.5 us  [fetch(): pl.pallas_call(functools.partial(fetch_kernel, planes, group), out_shape=...]
    pallas_call x1, Pallas kernels: 42.6 us -> 39.9 us  [sum_weights(): pl.pallas_call(functools.partial(weights_kernel, planes, group), out_shap...]
where the time goes in v6:
time: 251 us; the launch traced here: 250 us
  Pallas kernels  212 us (84%)
  local copies, waits for them, and re-layouts  15.4 us (6%)
  waiting for transfers between devices  9.18 us (4%)
  starting transfers between devices  6.99 us (3%)
  other arithmetic  3.66 us (1%)
    pallas_call x1, Pallas kernels, fetch(): pl.pallas_call(functools.partial(fetch_kernel, planes, group), out_shape=...  72.5 us
    pallas_call x1, Pallas kernels, give_back(): pl.pallas_call(functools.partial(return_kernel, planes, group), out_shape...  68.7 us
    pallas_call x1, Pallas kernels, sum_weights(): pl.pallas_call(functools.partial(weights_kernel, planes, group), out_shap...  39.9 us
    pallas_call x1, Pallas kernels, backward(): pl.pallas_call(backward_kernel, grid_spec=grid_spec, out_shape=(jax.Shape...  20.2 us
    pallas_call x1, Pallas kernels, forward(): pl.pallas_call(forward_kernel, grid_spec=grid_spec, out_shape=(jax.ShapeD...  10.7 us
    unnamed x28, local copies, waits for them, and re-layouts  10.6 us
    all_to_all x1, waiting for transfers between devices, on_device(): lax.all_to_all(attended_grad, 'head', split_axis=1, concat_axis=0, tiled=...  5.07 us
  transfers between devices with their start and end apart: 2, of which 2 were waited for; matrix products, arithmetic and copies ran while one was open for 1% of the time, Pallas kernels for 0%

profile of v6, /device:TPU:1, one launch (start us, length us, event | category | flops | bytes accessed | tf_op | source)
XLA Modules:
  0.0 249.7 jit_solution(6217997588724587448)
XLA Ops:
  0.6 0.0 copy-start
  0.7 1.2 copy.33
  1.9 0.1 copy.35
  2.0 0.1 slice.40
  2.1 0.8 reshape.72.slots_ref
  2.9 0.0 copy-start.7
  2.9 0.8 reshape.74
  3.7 0.1 copy.32
  3.8 0.1 copy.43.pairs_ref
  3.9 0.1 pad.8.clone
  4.0 0.0 copy-start.1
  4.0 0.9 copy-done.1
  5.0 72.5 %fetch.1 = (bf16[16,128,128]{2,1,0:T(8,128)(2,1)S(1)}, bf16[144,128,128]{2,1,0:T(8,128)(2,1)}, bf16[8,256,256]{2,1,0:T(8,128)(2,1)S(1)}, s32[8,8,128]{2,1,0:T(8,128)S(1)}) custom-call(bf16[4,128,256]{2,1,0:T(8,128)(2,1)S(1)} %bitcast.43, s32[8,8,128]{2,1,0:T(8,128)S(1)} %pad.4.asked_ref, bf16[256,512]{1,0:T(8,128)(2,1)S(1)} %copy.43.pairs_ref, ...), custom_call_target="tpu_custom_call" | custom-call | tf_op jit(solution)/shard_map/fetch/pallas_call | solution.py:470
  77.5 0.0 copy-start.3
  77.5 1.0 copy-done.3
  78.5 0.6 copy-done.6
  79.1 2.4 copy-done.8
  81.5 0.7 copy-done.9
  82.1 10.7 %attend.1 = (bf16[2048,128]{1,0:T(8,128)(2,1)S(1)}, f32[2048,128]{1,0:T(8,128)S(1)}) custom-call(s32[192]{0:T(256)S(1)} %reshape.72.slots_ref, s32[16]{0:T(128)S(1)} %copy-done.9, bf16[2048,128]{1,0:T(8,128)(2,1)S(1)} %bitcast.47, bf16[144,128,128]{2,1,0:T(8,128)(2,1)S(1)} %copy-done.8), custom_call_target="tpu_custom_call" | custom-call | flops 1610612736 | bytes 8388608 | tf_op jit(solution)/shard_map/attend/pallas_call | solution.py:75
  92.8 0.0 copy-start.10
  92.8 1.0 copy-done.10
  93.8 0.2 slice.32
  94.0 0.9 copy.36
  94.9 0.0 copy-done.7
  94.9 3.4 %all-to-all-start = ((bf16[4,512,64]{1,2,0:T(8,128)(2,1)}), bf16[4,512,64]{1,2,0:T(8,128)(2,1)S(1)}, u32[]{:S(2)}, u32[]{:S(2)}) async-start(bf16[4,512,64]{1,2,0:T(8,128)(2,1)} %copy.36), calls=%async_computation | async-start | bytes 524288 | tf_op jit(solution)/shard_map/all_to_all | solution.py:764
  98.3 0.7 slice.43
  99.0 0.7 slice.42
  99.7 4.1 %all-to-all-done = bf16[4,512,64]{1,2,0:T(8,128)(2,1)S(1)} async-done(((bf16[4,512,64]{1,2,0:T(8,128)(2,1)}), bf16[4,512,64]{1,2,0:T(8,128)(2,1)S(1)}, u32[]{:S(2)}, u32[]{:S(2)}) %all-to-all-start) | async-done | bytes 262176 | tf_op jit(solution)/shard_map/all_to_all | solution.py:764
  103.8 0.0 copy-done
  103.8 0.0 copy-done.2
  103.8 0.4 multiply_reduce_fusion
  104.2 0.0 copy-done.12
  104.3 0.2 fusion
  104.5 0.9 fusion.1
  105.4 1.0 convolution_convert_fusion
  106.4 3.6 %all-to-all-start.1 = ((bf16[512,4,64]{0,2,1:T(8,128)(2,1)}), bf16[512,4,64]{0,2,1:T(8,128)(2,1)S(1)}, u32[]{:S(2)}, u32[]{:S(2)}) async-start(bf16[512,4,64]{0,2,1:T(8,128)(2,1)} %bitcast.10), calls=%async_computation.1 | async-start | bytes 524288 | tf_op jit(solution)/shard_map/all_to_all | solution.py:780
  110.0 0.2 fusion.3.out_ref
  110.2 5.1 %all-to-all-done.1 = bf16[512,4,64]{0,2,1:T(8,128)(2,1)S(1)} async-done(((bf16[512,4,64]{0,2,1:T(8,128)(2,1)}), bf16[512,4,64]{0,2,1:T(8,128)(2,1)S(1)}, u32[]{:S(2)}, u32[]{:S(2)}) %all-to-all-start.1) | async-done | bytes 262176 | tf_op jit(solution)/shard_map/all_to_all | solution.py:780
  115.3 0.3 copy.38
  115.6 1.1 pad_maximum_fusion.qg_ref
  116.7 20.2 %attend_back.1 = (bf16[16,64,128]{2,1,0:T(8,128)(2,1)}, bf16[144,128,128]{2,1,0:T(8,128)(2,1)}) custom-call(s32[192]{0:T(256)} %copy-done.7, s32[16]{0:T(128)} %count_ref.3, bf16[2048,128]{1,0:T(8,128)(2,1)} %pad_maximum_fusion.qg_ref, bf16[2048,128]{1,0:T(8,128)(2,1)} %copy-done.5, f32[2048,128]{1,0:T(8,128)} %copy-done.10, ...), custom_call_target="tpu_custom_call" | custom-call | flops 4026531840 | bytes 16777216 | tf_op jit(solution)/shard_map/attend_back/pallas_call | solution.py:153
  136.9 0.0 copy-done.11
  136.9 68.7 %give_back.1 = (bf16[4,128,256]{2,1,0:T(8,128)(2,1)}, f32[4,192,256]{2,1,0:T(8,128)}) custom-call(bf16[144,128,128]{2,1,0:T(8,128)(2,1)} %get-tuple-element.18.grads_ref, bf16[16,64,128]{2,1,0:T(8,128)(2,1)} %get-tuple-element.19.dq_ref, bf16[8,256,256]{2,1,0:T(8,128)(2,1)} %copy-done.3, bf16[512,256]{1,0:T(8,128)(2,1)} %features_ref.1, ...), custom_call_target="tpu_custom_call" | custom-call | tf_op jit(solution)/shard_map/give_back/pallas_call | solution.py:723
  205.7 1.1 copy-done.4
  206.8 39.9 %sum_weights.1 = f32[8,8,8,128]{3,2,1,0:T(8,128)S(1)} custom-call(f32[768,256]{1,0:T(8,128)S(1)} %bitcast.46, f32[256,256]{1,0:T(8,128)S(1)} %fusion.3.out_ref), custom_call_target="tpu_custom_call" | custom-call | tf_op jit(solution)/shard_map/sum_weights/pallas_call | solution.py:270
  246.7 0.6 copy_bitcast_fusion
  247.3 0.7 bitcast_bitcast_fusion
  248.0 1.7 copy.49
  (18 shorter events, 0.1 us)
Async XLA Ops:
  0.6 103.2 %copy-start = (bf16[256,256]{1,0:T(8,128)(2,1)S(1)}, bf16[256,256]{1,0:T(8,128)(2,1)}, u32[]{:S(2)}) copy-start(bf16[256,256]{1,0:T(8,128)(2,1)} %param.9) | copy-start | bytes 393220
  2.9 92.0 %copy-start.7 = (s32[192]{0:T(256)}, s32[192]{0:T(256)S(1)}, u32[]{:S(2)}) copy-start(s32[192]{0:T(256)S(1)} %reshape.72.slots_ref) | copy-start | bytes 2308
  4.0 1.0 copy-start.1
  77.5 1.0 copy-start.3
  78.5 0.6 copy-start.6
  79.1 24.8 %copy-start.2 = (bf16[512,256]{1,0:T(8,128)(2,1)S(1)}, bf16[512,256]{1,0:T(8,128)(2,1)}, u32[]{:S(2)}) copy-start(bf16[512,256]{1,0:T(8,128)(2,1)} %features_ref.1) | copy-start | bytes 786436
  79.1 2.4 copy-start.8
  81.5 0.7 copy-start.9
  82.1 22.1 %copy-start.12 = (bf16[512,256]{1,0:T(8,128)(2,1)S(1)}, bf16[512,256]{1,0:T(8,128)(2,1)}, u32[]{:S(2)}) copy-start(bf16[512,256]{1,0:T(8,128)(2,1)} %param.10) | copy-start | bytes 786436
  92.8 1.0 copy-start.10
  93.8 21.8 %copy-start.5 = (bf16[2048,128]{1,0:T(8,128)(2,1)}, bf16[2048,128]{1,0:T(8,128)(2,1)S(1)}, u32[]{:S(2)}) copy-start(bf16[2048,128]{1,0:T(8,128)(2,1)S(1)} %get-tuple-element.16.att_ref) | copy-start | bytes 1572868
  94.9 8.9 %all-to-all-start = ((bf16[4,512,64]{1,2,0:T(8,128)(2,1)}), bf16[4,512,64]{1,2,0:T(8,128)(2,1)S(1)}, u32[]{:S(2)}, u32[]{:S(2)}) async-start(bf16[4,512,64]{1,2,0:T(8,128)(2,1)} %copy.36), calls=%async_computation | async-start | bytes 524288 | tf_op jit(solution)/shard_map/all_to_all | solution.py:764
  105.4 31.5 %copy-start.11 = (f32[512,256]{1,0:T(8,128)}, f32[512,256]{1,0:T(8,128)S(1)}, u32[]{:S(2)}) copy-start(f32[512,256]{1,0:T(8,128)S(1)} %get-tuple-element.24.norm_ref) | copy-start | bytes 1572868
  106.4 8.9 %all-to-all-start.1 = ((bf16[512,4,64]{0,2,1:T(8,128)(2,1)}), bf16[512,4,64]{0,2,1:T(8,128)(2,1)S(1)}, u32[]{:S(2)}, u32[]{:S(2)}) async-start(bf16[512,4,64]{0,2,1:T(8,128)(2,1)} %bitcast.10), calls=%async_computation.1 | async-start | bytes 524288 | tf_op jit(solution)/shard_map/all_to_all | solution.py:780
  205.6 1.1 copy-start.4

commit v7 on v1

v7 whole, which is shorter than its diff:
```python
import functools

import jax
import jax.numpy as jnp
from jax import lax
from jax.experimental import pallas as pl
from jax.experimental.pallas import tpu as pltpu
from jax.sharding import PartitionSpec as P

HEADS = 4
HD = 64
BLOCK = 128
BLK = 16
PER = 12
CAP = 2
PAIR = 2 * HD
WIDE = 2 * BLOCK
SHARED = BLOCK // 2
PART = SHARED // HEADS
LUMP = PART + (BLOCK - SHARED) // 2
SCALE = HD ** (-0.5)
NT = (((1,), (1,)), ((), ()))
TN = (((0,), (0,)), ((), ()))
MESH = pl.DeviceIdType.MESH


def dot(a, b, dims=(((1,), (0,)), ((), ()))):
    return lax.dot_general(a, b, dims, preferred_element_type=jnp.float32)


def forward_kernel(slots_ref, count_ref, q_ref, table_ref, out_ref, stat_ref):
    b = pl.program_id(0)
    count = count_ref[b]
    packed = q_ref[0]
    query = jnp.concatenate([packed[:, :HD], packed[:, HD:]], axis=0)
    query = jnp.concatenate([query, jnp.zeros_like(query)], axis=1)
    chosen = [table_ref[slots_ref[b * PER + j]] for j in range(PER)]
    scores = []
    for j in range(0, PER, 2):
        pair = dot(query, jnp.concatenate(chosen[j : j + 2], axis=0), NT)
        for i in range(2):
            dead = jnp.where(j + i < count, 0.0, -1e30)
            scores.append(pair[:, i * BLOCK : (i + 1) * BLOCK] + dead)
    highest = scores[0]
    for part in scores[1:]:
        highest = jnp.maximum(highest, part)
    highest = jnp.max(highest, axis=1, keepdims=True)
    total = jnp.zeros((BLOCK, BLOCK), jnp.float32)
    result = jnp.zeros((BLOCK, PAIR), jnp.float32)
    for j in range(0, PER, 2):
        raised = [jnp.exp(part - highest) for part in scores[j : j + 2]]
        total = total + raised[0] + raised[1]
        result = result + dot(
            jnp.concatenate([x.astype(jnp.bfloat16) for x in raised], axis=1),
            jnp.concatenate(chosen[j : j + 2], axis=0),
        )
    total = jnp.sum(total, axis=1, keepdims=True)
    out_ref[...] = (result / total).astype(jnp.bfloat16)
    lane = lax.broadcasted_iota(jnp.int32, stat_ref.shape, 1)
    stat_ref[...] = jnp.where(lane < HD, highest, 1.0 / total)


def forward(slots, count, query, table):
    rows = BLK * BLOCK
    grid_spec = pltpu.PrefetchScalarGridSpec(
        num_scalar_prefetch=2,
        grid=(BLK,),
        in_specs=[
            pl.BlockSpec((1, HD, PAIR), lambda b, *_: (b, 0, 0)),
            pl.BlockSpec(table.shape, lambda b, *_: (0, 0, 0)),
        ],
        out_specs=[
            pl.BlockSpec((BLOCK, PAIR), lambda b, *_: (b, 0)),
            pl.BlockSpec((BLOCK, PAIR), lambda b, *_: (b, 0)),
        ],
    )
    return pl.pallas_call(
        forward_kernel,
        grid_spec=grid_spec,
        out_shape=(
            jax.ShapeDtypeStruct((rows, PAIR), jnp.bfloat16),
            jax.ShapeDtypeStruct((rows, PAIR), jnp.float32),
        ),
        compiler_params=pltpu.CompilerParams(vmem_limit_bytes=40 << 20),
        cost_estimate=pl.CostEstimate(
            flops=4 * BLK * PER * BLOCK**3, bytes_accessed=8 << 20, transcendentals=BLK * PER * BLOCK**2
        ),
        name="attend",
    )(slots, count, query, table)


def backward_kernel(
    slots_ref, count_ref, q_ref, grad_ref, att_ref, stat_ref, table_ref, dq_ref, grads_ref, acc_ref, keys_ref, terms_ref
):
    b = pl.program_id(0)

    @pl.when(b == 0)
    def _():
        acc_ref[...] = jnp.zeros_like(acc_ref)

    count = count_ref[b]
    packed = q_ref[0]
    query = jnp.concatenate([packed[:, :HD], packed[:, HD:]], axis=0)
    both = jnp.concatenate([query, grad_ref[...]], axis=1)
    lane = lax.broadcasted_iota(jnp.int32, both.shape, 1)
    zero = jnp.zeros_like(both)
    stacked = jnp.concatenate(
        [jnp.where(lane < HD, both, zero), jnp.where(lane < HD, zero, both)], axis=0
    )
    dots = jnp.sum(
        jnp.where(lane < HD, 0.0, both.astype(jnp.float32) * att_ref[...].astype(jnp.float32)),
        axis=1,
        keepdims=True,
    )
    flipped = jnp.where((lane >= 32) & (lane < HD), dots, stat_ref[...]).T
    highest, dots, inverse = flipped[0:1], flipped[32:33], flipped[HD : HD + 1]
    slots = [slots_ref[b * PER + j] for j in range(PER)]
    for j in range(PER):
        keys_ref[j * BLOCK : (j + 1) * BLOCK] = table_ref[slots[j]]
    for j in range(0, PER, 2):
        products = dot(keys_ref[j * BLOCK : (j + 2) * BLOCK], stacked, NT)
        for i in range(2):
            rows = slice(i * BLOCK, (i + 1) * BLOCK)
            top = highest + jnp.where(j + i < count, 0.0, 1e30)
            attention = jnp.exp(products[rows, :BLOCK] - top) * inverse
            score_grad = attention * (products[rows, BLOCK:] - dots)
            terms_ref[(j + i) * BLOCK : (j + i + 1) * BLOCK] = jnp.concatenate(
                [score_grad.astype(jnp.bfloat16), attention.astype(jnp.bfloat16)], axis=1
            )
    dq = dot(keys_ref[...], terms_ref[:, :BLOCK], TN)
    for j in range(0, PER, 2):
        grads = dot(terms_ref[j * BLOCK : (j + 2) * BLOCK], stacked)
        for i in range(2):
            acc_ref[slots[j + i]] += grads[i * BLOCK : (i + 1) * BLOCK]
    dq = (dq.T * SCALE).astype(jnp.bfloat16)
    dq_ref[0] = jnp.concatenate([dq[:HD, :HD], dq[HD:, :HD]], axis=1)

    @pl.when(b == pl.num_programs(0) - 1)
    def _():
        grads_ref[...] = acc_ref[...].astype(jnp.bfloat16)


def backward(slots, count, query, grad, attended, stat, table):
    whole = lambda shape: pl.BlockSpec(shape, lambda b, *_: (0,) * len(shape))
    packed = pl.BlockSpec((1, HD, PAIR), lambda b, *_: (b, 0, 0))
    rowwise = pl.BlockSpec((BLOCK, PAIR), lambda b, *_: (b, 0))
    grid_spec = pltpu.PrefetchScalarGridSpec(
        num_scalar_prefetch=2,
        grid=(BLK,),
        in_specs=[
            packed, pl.BlockSpec((BLOCK, HD), lambda b, *_: (b, 0)), rowwise, rowwise, whole(table.shape)
        ],
        out_specs=[packed, whole(table.shape)],
        scratch_shapes=[
            pltpu.VMEM(table.shape, jnp.float32),
            pltpu.VMEM((PER * BLOCK, PAIR), jnp.bfloat16),
            pltpu.VMEM((PER * BLOCK, 2 * BLOCK), jnp.bfloat16),
        ],
    )
    return pl.pallas_call(
        backward_kernel,
        grid_spec=grid_spec,
        out_shape=(
            jax.ShapeDtypeStruct((BLK, HD, PAIR), jnp.bfloat16),
            jax.ShapeDtypeStruct(table.shape, jnp.bfloat16),
        ),
        compiler_params=pltpu.CompilerParams(vmem_limit_bytes=56 << 20),
        cost_estimate=pl.CostEstimate(
            flops=10 * BLK * PER * BLOCK**3, bytes_accessed=16 << 20, transcendentals=BLK * PER * BLOCK**2
        ),
        name="attend_back",
    )(slots, count, query, grad, attended, stat, table)


def torus(node_count):
    rows = 4 if node_count >= 64 else 2
    return node_count // (2 * rows), rows * 2


def ring_order(planes):
    half = planes // 2
    return [0] + [s * k for k in range(1, half) for s in (-1, 1)] + [half]


def quarter(h):
    return pl.ds(pl.multiple_of(h * PART, PART), PART)


def remote(source, target, send, recv, peer):
    return pltpu.make_async_remote_copy(
        source, target, send, recv, device_id=peer, device_id_type=MESH
    )


def neighbours(planes, group):
    node, head = lax.axis_index("node"), lax.axis_index("head")
    z, g = node // group, node % group
    x_peers = [(node, (head + d) % HEADS) for d in range(1, HEADS)]
    g_peers = [(z * group + (g + d) % group, head) for d in range(1, group)]
    right = (((z + 1) % planes) * group + g, head)
    left = (((z + planes - 1) % planes) * group + g, head)
    return head, z, g, x_peers, g_peers, right, left


def greet(peers):
    barrier = pltpu.get_barrier_semaphore()
    for peer in peers:
        pl.semaphore_signal(barrier, inc=1, device_id=peer, device_id_type=MESH)
    return lambda: pl.semaphore_wait(barrier, len(peers))


def fetch_kernel(
    planes, group, own_ref, asked_ref, weight_ref, query_ref, table_ref, shared_ref, asks_ref,
    pairs, my_pairs, my_queries, ring_a, ring_b, chunk_a, chunk_b, picked_a, picked_b, landed, made, asks,
    o_send, o_recv, q_send, q_recv, ra_send, ra_recv, rb_send, rb_recv,
    ga_send, ga_recv, gb_send, gb_recv, x_send, x_recv, asks_sem,
):
    head, z, g, x_peers, g_peers, right, left = neighbours(planes, group)
    half = planes // 2
    width = group * CAP
    rows = HEADS * BLOCK
    late = pl.ds(SHARED, BLOCK - SHARED)
    own_blocks = pl.ds(head * HEADS, HEADS)
    arrive = greet(x_peers + g_peers + [right, left])

    ring_a[z, own_blocks] = own_ref[:, quarter(head)]
    weight = weight_ref[...]
    step = 3 * HD
    for h in range(HEADS):
        pairs[:, h * PAIR : (h + 1) * PAIR] = weight[:, h * step + HD : (h + 1) * step]
    own = own_ref[...].reshape(rows, WIDE)
    for h in range(HEADS):
        both = dot(own, pairs[:, h * PAIR : (h + 1) * PAIR]).astype(jnp.bfloat16)
        my_pairs[h] = both.reshape(HEADS, BLOCK, PAIR)
        queries = (dot(own, weight[:, h * step : h * step + HD]) * SCALE).astype(jnp.bfloat16)
        queries = queries.reshape(HEADS, BLOCK, HD)
        my_queries[h] = jnp.concatenate([queries[:, :HD], queries[:, HD:]], axis=2)
    arrive()

    def own_copies(kind, source, target):
        return [
            remote(source(peer[1]), target, o_send.at[kind, d], o_recv.at[kind, d], peer)
            for d, peer in enumerate(x_peers)
        ]

    early = pl.ds(0, SHARED)
    corner = own_copies(0, lambda h: own_ref.at[:, quarter(h)], ring_a.at[z, own_blocks])
    lower = own_copies(1, lambda h: my_pairs.at[h, :, late], table_ref.at[own_blocks, late])
    upper = own_copies(2, lambda h: my_pairs.at[h, :, early], table_ref.at[own_blocks, early])
    asking = own_copies(3, lambda h: my_queries.at[h], query_ref.at[own_blocks])
    questions = [
        remote(asked_ref.at[peer[0] % group], asks_ref.at[g], q_send.at[d], q_recv.at[d], peer)
        for d, peer in enumerate(g_peers)
    ]
    sent = []

    def begin(copies):
        for copy in copies:
            copy.start()
            sent.append(copy)

    begin(corner + questions + lower + upper + asking)
    table_ref[own_blocks] = my_pairs[head]
    query_ref[own_blocks] = my_queries[head]
    asks_ref[g] = asked_ref[g]

    def hop(ring, send, recv, way, k):
        at = (z - k + planes) % planes if way == 0 else (z + k) % planes
        view = ring.at[at]
        if k == half - 1:
            view = view.at[pl.ds(way * (BLK // 2), BLK // 2)]
        return remote(view, view, send.at[way, k], recv.at[way, k], left if way else right)

    def hops(ring, send, recv):
        return {(way, k): hop(ring, send, recv, way, k) for way in range(2) for k in range(half)}

    hops_a = hops(ring_a, ra_send, ra_recv)
    hops_b = hops(ring_b, rb_send, rb_recv)
    order = ring_order(planes)
    place = lambda t: (z + order[t] + planes) % planes

    def bring(hops, t):
        offset = order[t]
        if offset == 0:
            begin([hops[0, 0], hops[1, 0]])
        elif offset == half:
            hops[0, half - 1].wait_recv()
            hops[1, half - 1].wait_recv()
        else:
            way, k = (0, -offset) if offset < 0 else (1, offset)
            hops[way, k - 1].wait_recv()
            begin([hops[way, k]])

    def spot(at, owner):
        return pl.ds(BLK + (at * group + owner) * CAP, CAP)

    def copies_a(at):
        return [
            remote(picked_a.at[at, d], landed.at[at, g], ga_send.at[at, d], ga_recv.at[at, d], peer)
            for d, peer in enumerate(g_peers)
        ]

    def copies_b(at):
        return [
            remote(
                picked_b.at[at, d], table_ref.at[spot(at, g), late], gb_send.at[at, d], gb_recv.at[at, d], peer
            )
            for d, peer in enumerate(g_peers)
        ]

    def bring_a(t):
        at = place(t)
        bring(hops_a, t)
        chunk_a[...] = ring_a[at]
        copies = copies_a(at)
        for d, peer in enumerate(g_peers):
            for c in range(CAP):
                picked_a[at, d, c] = chunk_a[asks[peer[0] % group, 0, at * CAP + c]]
            begin([copies[d]])
        for c in range(CAP):
            landed[at, g, c] = chunk_a[asks[g, 0, at * CAP + c]]

    def bring_b(t):
        at = place(t)
        bring(hops_b, t)
        chunk_b[...] = ring_b[at]
        copies = copies_b(at)
        for d, peer in enumerate(g_peers):
            for c in range(CAP):
                picked_b[at, d, c] = chunk_b[asks[peer[0] % group, 0, at * CAP + c]]
            begin([copies[d]])
        for c in range(CAP):
            table_ref[BLK + (at * group + g) * CAP + c, SHARED:] = chunk_b[asks[g, 0, at * CAP + c]]

    arriving = []

    def make(t):
        at = place(t)
        for copy in copies_a(at):
            copy.wait_recv()
        shared = landed[at].reshape(width * PART, WIDE)
        shared_ref[at] = shared
        both = dot(shared, pairs[...]).astype(jnp.bfloat16)
        for h in range(HEADS):
            made[at, h] = both[:, h * PAIR : (h + 1) * PAIR].reshape(width, PART, PAIR)
        slots = pl.ds(BLK + at * width, width)
        copies = [
            remote(
                made.at[at, peer[1]], table_ref.at[slots, quarter(head)], x_send.at[at, d], x_recv.at[at, d],
                peer,
            )
            for d, peer in enumerate(x_peers)
        ]
        begin(copies)
        arriving.extend(copies)
        table_ref[slots, quarter(head)] = made[at, head]

    for copy in corner:
        copy.wait_recv()
    for copy in questions:
        copy.wait_recv()
    answer = pltpu.make_async_copy(asks_ref, asks, asks_sem)
    answer.start()
    answer.wait()
    bring_a(0)
    for copy in lower:
        copy.wait_recv()
    ring_b[z] = table_ref[:BLK, SHARED:]
    bring_b(0)
    pairs_of = [[t, t + 1] for t in range(1, planes - 1, 2)] + [[planes - 1]]
    before = [0]
    for now in pairs_of:
        for t in now:
            bring_a(t)
        for t in before:
            make(t)
        for t in now:
            bring_b(t)
        before = now
    for t in before:
        make(t)
    for copy in upper + asking + arriving:
        copy.wait_recv()
    for t in range(planes):
        for copy in copies_b(place(t)):
            copy.wait_recv()
    for copy in sent:
        copy.wait_send()


def fetch(features, in_weight, wanted, node_count):
    planes, group = torus(node_count)
    own = features.reshape(HEADS, BLOCK, WIDE)
    asked = wanted.reshape(planes, group, CAP).transpose(1, 0, 2).reshape(group, 1, planes * CAP)
    asked = jnp.pad(asked, ((0, 0), (0, 7), (0, 128 - planes * CAP)))
    dma = lambda *shape: pltpu.SemaphoreType.DMA(shape)
    vmem = pl.BlockSpec(memory_space=pltpu.VMEM)
    low = lambda *shape: pltpu.VMEM(shape, jnp.bfloat16)
    late = BLOCK - SHARED
    slots = BLK + planes * group * CAP
    return pl.pallas_call(
        functools.partial(fetch_kernel, planes, group),
        out_shape=(
            jax.ShapeDtypeStruct((BLK, HD, PAIR), jnp.bfloat16),
            jax.ShapeDtypeStruct((slots, BLOCK, PAIR), jnp.bfloat16),
            jax.ShapeDtypeStruct((planes, group * CAP * PART, WIDE), jnp.bfloat16),
            jax.ShapeDtypeStruct((group, 8, 128), jnp.int32),
        ),
        in_specs=[vmem] * 3,
        out_specs=(vmem,) * 4,
        scratch_shapes=[
            low(WIDE, HEADS * PAIR),
            low(HEADS, HEADS, BLOCK, PAIR),
            low(HEADS, HEADS, HD, PAIR),
            low(planes, BLK, PART, WIDE),
            low(planes, BLK, late, PAIR),
            low(BLK, PART, WIDE),
            low(BLK, late, PAIR),
            low(planes, group - 1, CAP, PART, WIDE),
            low(planes, group - 1, CAP, late, PAIR),
            low(planes, group, CAP, PART, WIDE),
            low(planes, HEADS, group * CAP, PART, PAIR),
            pltpu.SMEM((group, 8, 128), jnp.int32),
            dma(4, 3), dma(4, 3), dma(group - 1), dma(group - 1),
            dma(2, planes // 2), dma(2, planes // 2), dma(2, planes // 2), dma(2, planes // 2),
            dma(planes, group - 1), dma(planes, group - 1), dma(planes, group - 1), dma(planes, group - 1),
            dma(planes, 3), dma(planes, 3),
            pltpu.SemaphoreType.DMA,
        ],
        compiler_params=pltpu.CompilerParams(
            collective_id=2, has_side_effects=True, vmem_limit_bytes=48 << 20
        ),
        name="fetch",
    )(own, asked, in_weight)


def return_kernel(
    planes, group, grads_ref, dq_ref, shared_ref, features_ref, norm_ref, weight_ref, out_ref, asks_ref,
    feature_ref, sum_ref,
    pairs, singles, own_pairs, own_queries, heads, leaving, answers_a, answers_b, partial_a, partial_b,
    ring_a, ring_b, summed, late_sums, quarters, acc, base,
    out_mine, out_in, in_mine, in_in, x_sum, g_in, g_sum, z_in, piece,
    o_send, o_recv, x_send, x_recv, ga_send, ga_recv, gb_send, gb_recv, ra_send, ra_recv, rb_send, rb_recv,
    wg_send, wg_recv, wz_send, wz_recv, bz_send, bz_recv, bg_send, bg_recv,
):
    head, z, g, x_peers, g_peers, right, left = neighbours(planes, group)
    z_peers = [(((z + d) % planes) * group + g, head) for d in range(1, planes)]
    half = planes // 2
    width = group * CAP
    low = BLOCK - SHARED
    early, late = pl.ds(0, SHARED), pl.ds(SHARED, low)
    own_blocks = pl.ds(head * HEADS, HEADS)
    arrive = greet(x_peers + g_peers + z_peers)

    weight = weight_ref[...]
    step = 3 * HD
    for h in range(HEADS):
        pairs[:, h * PAIR : (h + 1) * PAIR] = weight[:, h * step + HD : (h + 1) * step]
    singles[...] = jnp.concatenate(
        [weight[:, h * step : h * step + HD] for h in range(HEADS)], axis=1
    )
    for h in range(HEADS):
        some = out_ref[h * HD : (h + 1) * HD]
        out_mine[h] = jnp.concatenate([some[:, :BLOCK], some[:, BLOCK:]], axis=0)
    arrive()

    order = list(reversed(ring_order(planes)))
    places = [(z + offset + planes) % planes for offset in order]
    spot = lambda at, owner: pl.ds(BLK + (at * group + owner) * CAP, CAP)
    slots = lambda at: pl.ds(BLK + at * width, width)
    sent = []

    def begin(copies):
        for copy in copies:
            copy.start()
            sent.append(copy)

    def to_heads(kind, source, target):
        return [
            remote(source(peer[1]), target, o_send.at[kind, d], o_recv.at[kind, d], peer)
            for d, peer in enumerate(x_peers)
        ]

    blocks_of = lambda h: pl.ds(h * HEADS, HEADS)
    own = to_heads(0, lambda h: grads_ref.at[blocks_of(h), early], own_pairs.at[head, :, early])
    own += to_heads(1, lambda h: dq_ref.at[blocks_of(h)], own_queries.at[head])
    out_copies = to_heads(2, lambda h: out_mine.at[h], out_in.at[head])
    far = [
        [
            remote(
                grads_ref.at[slots(at), quarter(peer[1])], heads.at[at, head],
                x_send.at[at, d], x_recv.at[at, d], peer,
            )
            for d, peer in enumerate(x_peers)
        ]
        for at in places
    ]
    far_late = [
        [
            remote(
                grads_ref.at[spot(at, peer[0] % group), late], answers_b.at[at, g],
                gb_send.at[at, d], gb_recv.at[at, d], peer,
            )
            for d, peer in enumerate(g_peers)
        ]
        for at in places
    ]
    ahead = 3
    for t in range(min(ahead, planes)):
        begin(far[t])
        begin(far_late[t])
    acc[...] = jnp.zeros_like(acc)
    own_pairs[head, :, :SHARED] = grads_ref[own_blocks, :SHARED]
    own_queries[head] = dq_ref[own_blocks]

    def spread(t):
        at = places[t]
        heads[at, head] = grads_ref[slots(at), quarter(head)]
        for copy in far[t]:
            copy.wait_recv()
        if t + ahead < planes:
            begin(far[t + ahead])
            begin(far_late[t + ahead])
        if t + ahead == planes - 1:
            begin(own + out_copies)
        some = jnp.concatenate([heads[at, h].reshape(width * PART, PAIR) for h in range(HEADS)], axis=1)
        back = dot(some, pairs[...], NT).astype(jnp.bfloat16)
        leaving[at] = back.reshape(group, CAP, PART, WIDE)
        copies = [
            remote(
                leaving.at[at, peer[0] % group], answers_a.at[at, g], ga_send.at[at, d], ga_recv.at[at, d], peer
            )
            for d, peer in enumerate(g_peers)
        ]
        begin(copies)
        answers_a[at, g] = leaving[at, g]
        acc[...] += dot(some, shared_ref[at], TN)
        return copies

    def choose(t):
        at = places[t]
        side = width * PART
        column = lax.broadcasted_iota(jnp.int32, (1, side), 1)
        target = column % PART
        for j in range(width):
            block = asks_ref[j // CAP, 0, at * CAP + j % CAP]
            target = target + jnp.where(column // PART == j, block * PART, 0)
        row = lax.broadcasted_iota(jnp.int32, (BLK * PART, side), 0)
        return jnp.where(row == target, 1.0, 0.0).astype(jnp.bfloat16)

    def pass_on(t, total, partial, ring, send, recv):
        at, offset = places[t], order[t]
        mid = BLK // 2

        def hop(way, k):
            source, target = partial.at[at], ring.at[way, k]
            if k == 0:
                blocks = pl.ds(way * mid, mid)
                source, target = source.at[blocks], target.at[blocks]
            return remote(source, target, send.at[way, k], recv.at[way, k], left if way else right)

        if offset == half:
            partial[at] = total.astype(jnp.bfloat16)
            begin([hop(0, 0), hop(1, 0)])
            return None
        k = half - 1 - abs(offset)
        ways = [0] if offset > 0 else [1] if offset < 0 else [0, 1]
        for way in ways:
            hop(way, k).wait_recv()
            if k:
                total = total + ring[way, k].astype(jnp.float32)
            elif way:
                total = jnp.concatenate([total[:mid], total[mid:] + ring[way, k, mid:].astype(jnp.float32)], axis=0)
            else:
                total = jnp.concatenate([total[:mid] + ring[way, k, :mid].astype(jnp.float32), total[mid:]], axis=0)
        if offset:
            partial[at] = total.astype(jnp.bfloat16)
            begin([hop(ways[0], k + 1)])
            return None
        return total

    def gather_late(t, chosen):
        at = places[t]
        for copy in far_late[t]:
            copy.wait_recv()
        answers_b[at, g] = grads_ref[spot(at, g), SHARED:]
        total = [
            dot(chosen, answers_b[at, :, :, i * PART : (i + 1) * PART].reshape(width * PART, PAIR))
            for i in range(low // PART)
        ]
        total = jnp.concatenate([x.reshape(BLK, PART, PAIR) for x in total], axis=1)
        return pass_on(t, total, partial_b, ring_b, rb_send, rb_recv)

    def gather(t, chosen, copies):
        for copy in copies:
            copy.wait_recv()
        total = dot(chosen, answers_a[places[t]].reshape(width * PART, WIDE)).reshape(BLK, PART, WIDE)
        return pass_on(t, total, partial_a, ring_a, ra_send, ra_recv)

    before = None
    for t in range(planes):
        copies = spread(t)
        chosen = choose(t)
        if t == planes - 1:
            for copy in own:
                copy.wait_recv()
            some = jnp.concatenate(
                [own_pairs[h, :, :SHARED].reshape(HEADS * SHARED, PAIR) for h in range(HEADS)], axis=1
            )
            queries = jnp.concatenate(
                [
                    jnp.concatenate(
                        [own_queries[h, :, :, :HD], own_queries[h, :, :, HD:]], axis=1
                    ).reshape(HEADS * BLOCK, HD)
                    for h in range(HEADS)
                ],
                axis=1,
            )
            everything = features_ref[...].reshape(HEADS * BLOCK, WIDE)
            acc[...] += dot(some, features_ref[:, :SHARED].reshape(HEADS * SHARED, WIDE), TN)
            single_weight = dot(queries, everything, TN)
            base[...] = (norm_ref[...] + dot(queries, singles[...], NT)).reshape(HEADS, BLOCK, WIDE)
            base[:, :SHARED] += dot(some, pairs[...], NT).reshape(HEADS, SHARED, WIDE)
        total = gather_late(t, chosen)
        if t == planes - 1:
            late_sums[...] = (grads_ref[:BLK, SHARED:].astype(jnp.float32) + total).astype(jnp.bfloat16)
            tail = to_heads(3, lambda h: late_sums.at[blocks_of(h)], own_pairs.at[head, :, late])
            begin(tail)
            own_pairs[head, :, SHARED:] = late_sums[own_blocks]
        if t:
            gather(t - 1, *before)
        before = (chosen, copies)
    summed[...] = gather(planes - 1, *before).astype(jnp.bfloat16)
    final = to_heads(4, lambda h: summed.at[blocks_of(h)], quarters.at[head])
    begin(final)
    quarters[head] = summed[own_blocks]

    for copy in tail:
        copy.wait_recv()
    some = jnp.concatenate(
        [own_pairs[h, :, SHARED:].reshape(HEADS * low, PAIR) for h in range(HEADS)], axis=1
    )
    pair_weight = acc[...] + dot(some, features_ref[:, SHARED:].reshape(HEADS * low, WIDE), TN)
    for h in range(HEADS):
        terms = jnp.concatenate(
            [single_weight[h * HD : (h + 1) * HD], pair_weight[h * PAIR : (h + 1) * PAIR]], axis=0
        )
        terms = jnp.concatenate([terms[:, :BLOCK], terms[:, BLOCK:]], axis=0)
        in_mine[h] = terms.astype(jnp.bfloat16)
        if h == 0:
            in_own = jnp.where(head == 0, terms, 0.0)
        else:
            in_own = in_own + jnp.where(head == h, terms, 0.0)
    in_low = to_heads(5, lambda h: in_mine.at[h], in_in.at[head])
    begin(in_low)

    base[:, SHARED:] += dot(some, pairs[...], NT).reshape(HEADS, low, WIDE)
    feature_ref[:, SHARED:] = base[:, SHARED:].astype(jnp.bfloat16)
    for copy in final:
        copy.wait_recv()
    for h in range(HEADS):
        rows = slice(h * PART, (h + 1) * PART)
        feature_ref[:, rows] = (base[:, rows] + quarters[h].astype(jnp.float32)).astype(jnp.bfloat16)

    def exchange(peers, source, target, send, recv):
        copies = [
            remote(source(d, peer), target(d), send.at[d], recv.at[d], peer) for d, peer in enumerate(peers)
        ]
        begin(copies)
        return copies

    for copy in out_copies + in_low:
        copy.wait_recv()
    out_in[head] = out_mine[head]
    in_total = in_own
    for _, h in x_peers:
        in_total = in_total + in_in[h].astype(jnp.float32)
    out_total = out_in[0] + out_in[1] + out_in[2] + out_in[3]
    x_sum[...] = jnp.concatenate([in_total, out_total], axis=0).reshape(x_sum.shape)
    for copy in exchange(
        g_peers, lambda d, peer: x_sum.at[peer[0] % group], lambda d: g_in.at[d], wg_send, wg_recv
    ):
        copy.wait_recv()
    total = x_sum[g]
    for d in range(group - 1):
        total = total + g_in[d]
    g_sum[...] = total
    for copy in exchange(
        z_peers, lambda d, peer: g_sum.at[peer[0] // group], lambda d: z_in.at[d], wz_send, wz_recv
    ):
        copy.wait_recv()
    total = g_sum[z]
    for d in range(planes - 1):
        total = total + z_in[d]
    piece[...] = total
    sum_ref[g, z] = total
    for copy in exchange(z_peers, lambda d, peer: piece, lambda d: sum_ref.at[g, z], bz_send, bz_recv):
        copy.wait_recv()
    for copy in exchange(g_peers, lambda d, peer: sum_ref.at[g], lambda d: sum_ref.at[g], bg_send, bg_recv):
        copy.wait_recv()
    for copy in sent:
        copy.wait_send()


def give_back(grads, dq, shared, features, norm_grad, in_weight, out_grad, asks, node_count):
    planes, group = torus(node_count)
    rows = 4 * HD * 2 // (planes * group)
    late = BLOCK - SHARED
    dma = lambda *shape: pltpu.SemaphoreType.DMA(shape)
    vmem = pl.BlockSpec(memory_space=pltpu.VMEM)
    low = lambda *shape: pltpu.VMEM(shape, jnp.bfloat16)
    high = lambda *shape: pltpu.VMEM(shape, jnp.float32)
    both = lambda *shape: [dma(*shape)] * 2
    feature_grad, total = pl.pallas_call(
        functools.partial(return_kernel, planes, group),
        out_shape=(
            jax.ShapeDtypeStruct((HEADS, BLOCK, WIDE), jnp.bfloat16),
            jax.ShapeDtypeStruct((group, planes, rows, 128), jnp.float32),
        ),
        in_specs=[vmem] * 7 + [pl.BlockSpec(memory_space=pltpu.SMEM)],
        out_specs=(vmem,) * 2,
        scratch_shapes=[
            low(WIDE, HEADS * PAIR),
            low(WIDE, HEADS * HD),
            low(HEADS, HEADS, BLOCK, PAIR),
            low(HEADS, HEADS, HD, PAIR),
            low(planes, HEADS, group * CAP, PART, PAIR),
            low(planes, group, CAP, PART, WIDE),
            low(planes, group, CAP, PART, WIDE),
            low(planes, group, CAP, late, PAIR),
            low(planes, BLK, PART, WIDE),
            low(planes, BLK, late, PAIR),
            low(2, planes // 2, BLK, PART, WIDE),
            low(2, planes // 2, BLK, late, PAIR),
            low(BLK, PART, WIDE),
            low(BLK, late, PAIR),
            low(HEADS, HEADS, PART, WIDE),
            high(HEADS * PAIR, WIDE),
            high(HEADS, BLOCK, WIDE),
            high(HEADS, 2 * HD, 128),
            high(HEADS, 2 * HD, 128),
            low(HEADS, 6 * HD, 128),
            low(HEADS, 6 * HD, 128),
            high(group, planes, rows, 128),
            high(group - 1, planes, rows, 128),
            high(planes, rows, 128),
            high(planes - 1, rows, 128),
            high(rows, 128),
            *both(6, 3), *both(planes, 3), *both(planes, group - 1), *both(planes, group - 1),
            *both(2, planes // 2), *both(2, planes // 2),
            *both(group - 1), *both(planes - 1), *both(planes - 1), *both(group - 1),
        ],
        compiler_params=pltpu.CompilerParams(
            collective_id=3, has_side_effects=True, vmem_limit_bytes=56 << 20
        ),
        name="give_back",
    )(grads, dq, shared, features.reshape(HEADS, BLOCK, WIDE), norm_grad, in_weight, out_grad, asks)
    total = total.reshape(4 * HD * 2, 128)
    in_total, out_total = total[: 6 * HD], total[6 * HD :]
    in_total = jnp.concatenate([in_total[: 3 * HD], in_total[3 * HD :]], axis=1)
    out_total = jnp.concatenate([out_total[:HD], out_total[HD:]], axis=1)
    return feature_grad.reshape(HEADS * BLOCK, WIDE), in_total.T, out_total


def on_device(features, in_weight, out_weight, cotangent, key_slots, block_count, wanted):
    node_count = lax.axis_size("node")
    node_rows = BLK * BLOCK
    total_nodes = node_rows * node_count
    queries, table, shared, asks = fetch(features, in_weight, wanted, node_count)
    slots = key_slots.reshape(-1)
    wide, stat = forward(slots, block_count, queries, table)
    attended = wide[:, HD:]
    attended_rows = lax.all_to_all(attended, "head", split_axis=0, concat_axis=1, tiled=True)
    summed = features.astype(jnp.float32) + jnp.dot(
        attended_rows, out_weight, preferred_element_type=jnp.float32
    )
    root_mean = jnp.sqrt(jnp.mean(summed * summed, axis=-1, keepdims=True) + 1e-06)
    normed = summed / root_mean
    output = normed.astype(jnp.bfloat16)
    upstream = cotangent.astype(jnp.float32)
    norm_grad = (
        upstream - normed * jnp.mean(upstream * normed, axis=-1, keepdims=True)
    ) / root_mean
    norm_grad_low = norm_grad.astype(jnp.bfloat16)
    out_weight_grad = jnp.dot(attended_rows.T, norm_grad_low, preferred_element_type=jnp.float32)
    attended_grad = jnp.dot(norm_grad_low, out_weight.T, preferred_element_type=jnp.float32).astype(
        jnp.bfloat16
    )
    attended_grad = lax.all_to_all(attended_grad, "head", split_axis=1, concat_axis=0, tiled=True)
    dq, grads = backward(slots, block_count, queries, attended_grad, wide, stat, table)
    feature_grad, in_weight_grad, out_weight_grad = give_back(
        grads, dq, shared, features, norm_grad, in_weight, out_weight_grad, asks, node_count
    )
    grad_factor = total_nodes ** (-0.5)
    return (
        output,
        feature_grad,
        in_weight_grad * grad_factor,
        out_weight_grad * grad_factor,
    )


def solution(mesh):
    placed = (
        P(("node", "head"), None),
        P(),
        P(),
        P(("node", "head"), None),
        P("node", None),
        P("node"),
        P("node", None, None),
    )
    return jax.shard_map(
        on_device,
        mesh=mesh,
        in_specs=placed,
        out_specs=(
            P(("node", "head"), None),
            P(("node", "head"), None),
            P(None, "head"),
            P("head", None),
        ),
        check_vma=False,
    )
```

time: 597 us -> 219 us (0.37)
  waiting for transfers between devices: 438 us -> 4.37 us
  Pallas kernels: 42.7 us -> 183 us
  starting transfers between devices: 41.5 us -> 3.58 us
  other arithmetic: 32.4 us -> 2.5 us
  between operations: 14.1 us -> 0.77 us
    all_to_all x6 -> x1, waiting for transfers between devices: 219 us -> 4.37 us  [on_device(): lax.all_to_all(attended_grad, 'head', split_axis=1, concat_axis=0, tiled=...]
    psum x1 -> x0, waiting for transfers between devices: 179 us -> none  [on_device(): lax.psum((in_weight_grad, out_weight_grad), 'node')]
    pallas_call x0 -> x2, Pallas kernels: none -> 150 us  [the longest x1 87.1 us: give_back(): pl.pallas_call(functools.partial(return_kernel, planes, group), out_shape...]
    reduce_scatter x2 -> x0, waiting for transfers between devices: 39.9 us -> none  [the longest x1 28.6 us: on_device(): lax.psum_scatter(in_weight_grad, 'head', scatter_dimension=1, tiled=True)]
    all_to_all x6 -> x1, starting transfers between devices: 41.4 us -> 3.58 us  [on_device(): lax.all_to_all(attended_grad, 'head', split_axis=1, concat_axis=0, tiled=...]
    scatter-add x1 -> x0, other arithmetic: 17 us -> none  [on_device(): own.at[requests].add(returned).astype(jnp.bfloat16).reshape(node_rows, PAIR)]
    pallas_call x1, Pallas kernels: 32 us -> 21.4 us  [backward(): pl.pallas_call(backward_kernel, grid_spec=grid_spec, out_shape=(jax.Shape...]
    reshape x1 -> x0, other arithmetic: 6.5 us -> none  [on_device(): returned.astype(jnp.float32).reshape(node_count * CAP, BLOCK, PAIR)]
  transfers between devices with their start and end apart: 9 -> 1, of which waited for: 9 -> 1; matrix products, arithmetic and copies ran while one was open for 1% -> 0% of each run, Pallas kernels for 0% -> 0%
where the time goes in v7:
time: 219 us; the launch traced here: 218 us
  Pallas kernels  183 us (84%)
  local copies, waits for them, and re-layouts  14.1 us (6%)
  blocking collectives  7.95 us (4%)
  waiting for transfers between devices  4.37 us (2%)
  starting transfers between devices  3.58 us (2%)
  other arithmetic  2.5 us (1%)
  matrix products  2.29 us (1%)
    pallas_call x1, Pallas kernels, give_back(): pl.pallas_call(functools.partial(return_kernel, planes, group), out_shape...  87.1 us
    pallas_call x1, Pallas kernels, fetch(): pl.pallas_call(functools.partial(fetch_kernel, planes, group), out_shape=...  63.2 us
    pallas_call x1, Pallas kernels, backward(): pl.pallas_call(backward_kernel, grid_spec=grid_spec, out_shape=(jax.Shape...  21.4 us
    pallas_call x1, Pallas kernels, forward(): pl.pallas_call(forward_kernel, grid_spec=grid_spec, out_shape=(jax.ShapeD...  11.1 us
    unnamed x29, local copies, waits for them, and re-layouts  9.3 us
    all_to_all x1, blocking collectives, on_device(): lax.all_to_all(attended, 'head', split_axis=0, concat_axis=1, tiled=True)  7.95 us
  transfers between devices with their start and end apart: 1, of which 1 were waited for; matrix products, arithmetic and copies ran while one was open for 0% of the time, Pallas kernels for 0%

profile of v7, /device:TPU:1, one launch (start us, length us, event | category | flops | bytes accessed | tf_op | source)
XLA Modules:
  0.0 218.3 jit_solution(3881841009834984188)
XLA Ops:
  0.6 0.0 copy-start
  0.6 0.8 reshape.49.slots_ref
  1.5 0.0 copy-start.7
  1.5 0.8 reshape.51
  2.2 0.1 copy.21
  2.3 0.0 copy-start.1
  2.3 0.9 copy-done.1
  3.3 0.0 copy-start.3
  3.3 1.0 copy-done.3
  4.3 0.0 copy-start.2
  4.3 63.2 %fetch.1 = (bf16[16,64,128]{2,1,0:T(8,128)(2,1)S(1)}, bf16[144,128,128]{2,1,0:T(8,128)(2,1)}, bf16[8,256,256]{2,1,0:T(8,128)(2,1)S(1)}, s32[8,8,128]{2,1,0:T(8,128)S(1)}) custom-call(bf16[4,128,256]{2,1,0:T(8,128)(2,1)S(1)} %bitcast.26, s32[8,8,128]{2,1,0:T(8,128)S(1)} %pad.4.asked_ref, bf16[256,768]{1,0:T(8,128)(2,1)S(1)} %copy-done.3), custom_call_target="tpu_custom_call" | custom-call | tf_op jit(solution)/shard_map/fetch/pallas_call | solution.py:401
  67.5 0.0 copy-start.4
  67.5 1.0 copy-done.4
  68.5 0.0 copy-start.6
  68.5 0.6 copy-done.6
  69.1 0.0 copy-start.9
  69.1 0.0 copy-start.8
  69.1 2.4 %copy-done.8 = bf16[144,128,128]{2,1,0:T(8,128)(2,1)S(1)} copy-done((bf16[144,128,128]{2,1,0:T(8,128)(2,1)S(1)}, bf16[144,128,128]{2,1,0:T(8,128)(2,1)}, u32[]{:S(2)}) %copy-start.8) | copy-done | bytes 4718616
  71.5 0.0 copy-start.10
  71.5 0.7 copy-done.10
  72.2 11.1 %attend.1 = (bf16[2048,128]{1,0:T(8,128)(2,1)S(1)}, f32[2048,128]{1,0:T(8,128)S(1)}) custom-call(s32[192]{0:T(256)S(1)} %reshape.49.slots_ref, s32[16]{0:T(128)S(1)} %copy-done.10, bf16[16,64,128]{2,1,0:T(8,128)(2,1)S(1)} %get-tuple-element.14.q_ref, bf16[144,128,128]{2,1,0:T(8,128)(2,1)S(1)} %copy-done.8), custom_call_target="tpu_custom_call" | custom-call | flops 1610612736 | bytes 8388608 | tf_op jit(solution)/shard_map/attend/pallas_call | solution.py:77
  83.2 0.0 copy-start.11
  83.3 1.0 copy-done.11
  84.2 0.2 slice.35
  84.4 0.2 copy.22
  84.6 7.9 %all_to_all.38 = bf16[4,512,64]{1,2,0:T(8,128)(2,1)S(1)} all-to-all(bf16[4,512,64]{1,2,0:T(8,128)(2,1)S(1)} %copy.22), channel_id=1, replica_groups=mesh['node'=64,'head'=4] {'head'}, dimensions={0} | all-to-all | bytes 524288 | tf_op jit(solution)/shard_map/all_to_all | solution.py:773
  92.6 0.0 copy-done
  92.6 0.0 copy-done.2
  92.6 0.4 multiply_reduce_fusion
  93.0 0.0 copy-done.7
  93.0 0.0 copy-done.9
  93.0 0.0 copy-done.13
  93.0 0.2 fusion
  93.3 0.9 fusion.1
  94.2 1.0 convolution_convert_fusion
  95.2 3.6 %all-to-all-start.1 = ((bf16[512,4,64]{0,2,1:T(8,128)(2,1)}), bf16[512,4,64]{0,2,1:T(8,128)(2,1)S(1)}, u32[]{:S(2)}, u32[]{:S(2)}) async-start(bf16[512,4,64]{0,2,1:T(8,128)(2,1)} %bitcast.6), calls=%async_computation.1 | async-start | bytes 524288 | tf_op jit(solution)/shard_map/all_to_all | solution.py:789
  98.8 0.9 fusion.3.out_ref
  99.7 4.4 %all-to-all-done.1 = bf16[512,4,64]{0,2,1:T(8,128)(2,1)S(1)} async-done(((bf16[512,4,64]{0,2,1:T(8,128)(2,1)}), bf16[512,4,64]{0,2,1:T(8,128)(2,1)S(1)}, u32[]{:S(2)}, u32[]{:S(2)}) %all-to-all-start.1) | async-done | bytes 262176 | tf_op jit(solution)/shard_map/all_to_all | solution.py:789
  104.1 1.0 copy.24
  105.1 0.0 copy-done.5
  105.1 21.4 %attend_back.1 = (bf16[16,64,128]{2,1,0:T(8,128)(2,1)}, bf16[144,128,128]{2,1,0:T(8,128)(2,1)}) custom-call(s32[192]{0:T(256)} %copy-done.7, s32[16]{0:T(128)} %count_ref.3, bf16[16,64,128]{2,1,0:T(8,128)(2,1)} %copy-done.9, bf16[2048,64]{1,0:T(8,128)(2,1)} %bitcast.31, bf16[2048,128]{1,0:T(8,128)(2,1)} %copy-done.5, f32[2048,128]{1,0:T(8,128)} %copy-done.11, ...), custom_call_target="tpu_custom_call" | custom-call | flops 4026531840 | bytes 16777216 | tf_op jit(solution)/shard_map/attend_back/pallas_call | solution.py:160
  126.5 0.0 copy-done.12
  126.5 87.1 %give_back.1 = (bf16[4,128,256]{2,1,0:T(8,128)(2,1)}, f32[8,8,8,128]{3,2,1,0:T(8,128)}) custom-call(bf16[144,128,128]{2,1,0:T(8,128)(2,1)} %get-tuple-element.18.grads_ref, bf16[16,64,128]{2,1,0:T(8,128)(2,1)} %get-tuple-element.19.dq_ref, bf16[8,256,256]{2,1,0:T(8,128)(2,1)} %copy-done.4, bf16[4,128,256]{2,1,0:T(8,128)(2,1)} %bitcast.25, ...), custom_call_target="tpu_custom_call" | custom-call | tf_op jit(solution)/shard_map/give_back/pallas_call | solution.py:714
  213.6 0.8 slice_bitcast_fusion.1
  214.3 1.0 fusion.7
  215.3 0.7 fusion.2
  216.0 0.6 maximum_multiply_fusion.1
  216.6 1.7 copy.27
  (7 shorter events, 0.0 us)
Async XLA Ops:
  0.6 92.0 %copy-start = (bf16[256,256]{1,0:T(8,128)(2,1)S(1)}, bf16[256,256]{1,0:T(8,128)(2,1)}, u32[]{:S(2)}) copy-start(bf16[256,256]{1,0:T(8,128)(2,1)} %param.9) | copy-start | bytes 393220
  1.5 91.5 %copy-start.7 = (s32[192]{0:T(256)}, s32[192]{0:T(256)S(1)}, u32[]{:S(2)}) copy-start(s32[192]{0:T(256)S(1)} %reshape.49.slots_ref) | copy-start | bytes 2308
  2.3 1.0 copy-start.1
  3.3 1.0 copy-start.3
  4.3 88.3 %copy-start.2 = (bf16[512,256]{1,0:T(8,128)(2,1)S(1)}, bf16[512,256]{1,0:T(8,128)(2,1)}, u32[]{:S(2)}) copy-start(bf16[512,256]{1,0:T(8,128)(2,1)} %param.7) | copy-start | bytes 786436
  67.5 1.0 copy-start.4
  68.5 0.6 copy-start.6
  69.1 23.9 %copy-start.9 = (bf16[16,64,128]{2,1,0:T(8,128)(2,1)}, bf16[16,64,128]{2,1,0:T(8,128)(2,1)S(1)}, u32[]{:S(2)}) copy-start(bf16[16,64,128]{2,1,0:T(8,128)(2,1)S(1)} %get-tuple-element.14.q_ref) | copy-start | bytes 786436
  69.1 2.4 %copy-start.8 = (bf16[144,128,128]{2,1,0:T(8,128)(2,1)S(1)}, bf16[144,128,128]{2,1,0:T(8,128)(2,1)}, u32[]{:S(2)}) copy-start(bf16[144,128,128]{2,1,0:T(8,128)(2,1)} %get-tuple-element.15.table_ref) | copy-start | bytes 14155780
  71.5 0.7 copy-start.10
  72.2 20.9 %copy-start.13 = (bf16[512,256]{1,0:T(8,128)(2,1)S(1)}, bf16[512,256]{1,0:T(8,128)(2,1)}, u32[]{:S(2)}) copy-start(bf16[512,256]{1,0:T(8,128)(2,1)} %param.10) | copy-start | bytes 786436
  83.2 1.0 copy-start.11
  84.2 20.9 %copy-start.5 = (bf16[2048,128]{1,0:T(8,128)(2,1)}, bf16[2048,128]{1,0:T(8,128)(2,1)S(1)}, u32[]{:S(2)}) copy-start(bf16[2048,128]{1,0:T(8,128)(2,1)S(1)} %get-tuple-element.16.att_ref) | copy-start | bytes 1572868
  94.2 32.3 %copy-start.12 = (f32[512,256]{1,0:T(8,128)}, f32[512,256]{1,0:T(8,128)S(1)}, u32[]{:S(2)}) copy-start(f32[512,256]{1,0:T(8,128)S(1)} %get-tuple-element.24.norm_ref) | copy-start | bytes 1572868
  95.2 8.9 %all-to-all-start.1 = ((bf16[512,4,64]{0,2,1:T(8,128)(2,1)}), bf16[512,4,64]{0,2,1:T(8,128)(2,1)S(1)}, u32[]{:S(2)}, u32[]{:S(2)}) async-start(bf16[512,4,64]{0,2,1:T(8,128)(2,1)} %bitcast.6), calls=%async_computation.1 | async-start | bytes 524288 | tf_op jit(solution)/shard_map/all_to_all | solution.py:789

commit v8 on v7

--- a/solution.py
+++ b/solution.py
@@ -14,6 +14,7 @@
 PER = 12
 CAP = 2
 PAIR = 2 * HD
+PAIRED = 2
 WIDE = 2 * BLOCK
 SHARED = BLOCK // 2
 PART = SHARED // HEADS
@@ -28,13 +29,16 @@
     return lax.dot_general(a, b, dims, preferred_element_type=jnp.float32)
 
 
-def forward_kernel(slots_ref, count_ref, q_ref, table_ref, out_ref, stat_ref):
-    b = pl.program_id(0)
-    count = count_ref[b]
-    packed = q_ref[0]
-    query = jnp.concatenate([packed[:, :HD], packed[:, HD:]], axis=0)
+def unpack(packed):
+    return jnp.concatenate([packed[..., :HD], packed[..., HD:]], axis=-2)
+
+
+def pack(rows):
+    return jnp.concatenate([rows[..., :HD, :], rows[..., HD:, :]], axis=-1)
+
+
+def attend(query, chosen, count):
     query = jnp.concatenate([query, jnp.zeros_like(query)], axis=1)
-    chosen = [table_ref[slots_ref[b * PER + j]] for j in range(PER)]
     scores = []
     for j in range(0, PER, 2):
         pair = dot(query, jnp.concatenate(chosen[j : j + 2], axis=0), NT)
@@ -55,106 +59,67 @@
             jnp.concatenate(chosen[j : j + 2], axis=0),
         )
     total = jnp.sum(total, axis=1, keepdims=True)
-    out_ref[...] = (result / total).astype(jnp.bfloat16)
-    lane = lax.broadcasted_iota(jnp.int32, stat_ref.shape, 1)
-    stat_ref[...] = jnp.where(lane < HD, highest, 1.0 / total)
-
-
-def forward(slots, count, query, table):
-    rows = BLK * BLOCK
+    return (result / total).astype(jnp.bfloat16), highest, total
+
+
+def backward_kernel(slots_ref, count_ref, both_ref, stat_ref, table_ref, dq_ref, grads_ref, acc_ref, keys_ref, terms_ref):
+    step = pl.program_id(0)
+
+    @pl.when(step == 0)
+    def _():
+        acc_ref[...] = jnp.zeros_like(acc_ref)
+
+    stacks, slots = [], []
+    for i in range(PAIRED):
+        b = step * PAIRED + i
+        count = count_ref[b]
+        both = both_ref[i]
+        lane = lax.broadcasted_iota(jnp.int32, both.shape, 1)
+        zero = jnp.zeros_like(both)
+        stacked = jnp.concatenate(
+            [jnp.where(lane < HD, both, zero), jnp.where(lane < HD, zero, both)], axis=0
+        )
+        stacks.append(stacked)
+        highest, dots, inverse = stat_ref[i, 0:1], stat_ref[i, 1:2], stat_ref[i, 2:3]
+        slots.append([slots_ref[b * PER + j] for j in range(PER)])
+        for j in range(PER):
+            keys_ref[i, j * BLOCK : (j + 1) * BLOCK] = table_ref[slots[i][j]]
+        for j in range(0, PER, 2):
+            products = dot(keys_ref[i, j * BLOCK : (j + 2) * BLOCK], stacked, NT)
+            for k in range(2):
+                rows = slice(k * BLOCK, (k + 1) * BLOCK)
+                top = highest + jnp.where(j + k < count, 0.0, 1e30)
+                attention = jnp.exp(products[rows, :BLOCK] - top) * inverse
+                score_grad = attention * (products[rows, BLOCK:] - dots)
+                terms_ref[i, (j + k) * BLOCK : (j + k + 1) * BLOCK] = jnp.concatenate(
+                    [score_grad.astype(jnp.bfloat16), attention.astype(jnp.bfloat16)], axis=1
+                )
+    for i in range(PAIRED):
+        dq = dot(keys_ref[i], terms_ref[i, :, :BLOCK], TN)
+        dq = (dq.T * SCALE).astype(jnp.bfloat16)
+        dq_ref[i] = pack(dq[:, :HD])
+        for j in range(0, PER, 2):
+            grads = dot(terms_ref[i, j * BLOCK : (j + 2) * BLOCK], stacks[i])
+            for k in range(2):
+                acc_ref[slots[i][j + k]] += grads[k * BLOCK : (k + 1) * BLOCK]
+
+    @pl.when(step == pl.num_programs(0) - 1)
+    def _():
+        grads_ref[...] = acc_ref[...].astype(jnp.bfloat16)
+
+
+def backward(slots, count, both, stat, table):
+    whole = lambda shape: pl.BlockSpec(shape, lambda b, *_: (0,) * len(shape))
+    some = lambda *shape: pl.BlockSpec((PAIRED,) + shape, lambda b, *_: (b, 0, 0))
     grid_spec = pltpu.PrefetchScalarGridSpec(
         num_scalar_prefetch=2,
-        grid=(BLK,),
-        in_specs=[
-            pl.BlockSpec((1, HD, PAIR), lambda b, *_: (b, 0, 0)),
-            pl.BlockSpec(table.shape, lambda b, *_: (0, 0, 0)),
-        ],
-        out_specs=[
-            pl.BlockSpec((BLOCK, PAIR), lambda b, *_: (b, 0)),
-            pl.BlockSpec((BLOCK, PAIR), lambda b, *_: (b, 0)),
-        ],
-    )
-    return pl.pallas_call(
-        forward_kernel,
-        grid_spec=grid_spec,
-        out_shape=(
-            jax.ShapeDtypeStruct((rows, PAIR), jnp.bfloat16),
-            jax.ShapeDtypeStruct((rows, PAIR), jnp.float32),
-        ),
-        compiler_params=pltpu.CompilerParams(vmem_limit_bytes=40 << 20),
-        cost_estimate=pl.CostEstimate(
-            flops=4 * BLK * PER * BLOCK**3, bytes_accessed=8 << 20, transcendentals=BLK * PER * BLOCK**2
-        ),
-        name="attend",
-    )(slots, count, query, table)
-
-
-def backward_kernel(
-    slots_ref, count_ref, q_ref, grad_ref, att_ref, stat_ref, table_ref, dq_ref, grads_ref, acc_ref, keys_ref, terms_ref
-):
-    b = pl.program_id(0)
-
-    @pl.when(b == 0)
-    def _():
-        acc_ref[...] = jnp.zeros_like(acc_ref)
-
-    count = count_ref[b]
-    packed = q_ref[0]
-    query = jnp.concatenate([packed[:, :HD], packed[:, HD:]], axis=0)
-    both = jnp.concatenate([query, grad_ref[...]], axis=1)
-    lane = lax.broadcasted_iota(jnp.int32, both.shape, 1)
-    zero = jnp.zeros_like(both)
-    stacked = jnp.concatenate(
-        [jnp.where(lane < HD, both, zero), jnp.where(lane < HD, zero, both)], axis=0
-    )
-    dots = jnp.sum(
-        jnp.where(lane < HD, 0.0, both.astype(jnp.float32) * att_ref[...].astype(jnp.float32)),
-        axis=1,
-        keepdims=True,
-    )
-    flipped = jnp.where((lane >= 32) & (lane < HD), dots, stat_ref[...]).T
-    highest, dots, inverse = flipped[0:1], flipped[32:33], flipped[HD : HD + 1]
-    slots = [slots_ref[b * PER + j] for j in range(PER)]
-    for j in range(PER):
-        keys_ref[j * BLOCK : (j + 1) * BLOCK] = table_ref[slots[j]]
-    for j in range(0, PER, 2):
-        products = dot(keys_ref[j * BLOCK : (j + 2) * BLOCK], stacked, NT)
-        for i in range(2):
-            rows = slice(i * BLOCK, (i + 1) * BLOCK)
-            top = highest + jnp.where(j + i < count, 0.0, 1e30)
-            attention = jnp.exp(products[rows, :BLOCK] - top) * inverse
-            score_grad = attention * (products[rows, BLOCK:] - dots)
-            terms_ref[(j + i) * BLOCK : (j + i + 1) * BLOCK] = jnp.concatenate(
-                [score_grad.astype(jnp.bfloat16), attention.astype(jnp.bfloat16)], axis=1
-            )
-    dq = dot(keys_ref[...], terms_ref[:, :BLOCK], TN)
-    for j in range(0, PER, 2):
-        grads = dot(terms_ref[j * BLOCK : (j + 2) * BLOCK], stacked)
-        for i in range(2):
-            acc_ref[slots[j + i]] += grads[i * BLOCK : (i + 1) * BLOCK]
-    dq = (dq.T * SCALE).astype(jnp.bfloat16)
-    dq_ref[0] = jnp.concatenate([dq[:HD, :HD], dq[HD:, :HD]], axis=1)
-
-    @pl.when(b == pl.num_programs(0) - 1)
-    def _():
-        grads_ref[...] = acc_ref[...].astype(jnp.bfloat16)
-
-
-def backward(slots, count, query, grad, attended, stat, table):
-    whole = lambda shape: pl.BlockSpec(shape, lambda b, *_: (0,) * len(shape))
-    packed = pl.BlockSpec((1, HD, PAIR), lambda b, *_: (b, 0, 0))
-    rowwise = pl.BlockSpec((BLOCK, PAIR), lambda b, *_: (b, 0))
-    grid_spec = pltpu.PrefetchScalarGridSpec(
-        num_scalar_prefetch=2,
-        grid=(BLK,),
-        in_specs=[
-            packed, pl.BlockSpec((BLOCK, HD), lambda b, *_: (b, 0)), rowwise, rowwise, whole(table.shape)
-        ],
-        out_specs=[packed, whole(table.shape)],
+        grid=(BLK // PAIRED,),
+        in_specs=[some(BLOCK, PAIR), some(8, BLOCK), whole(table.shape)],
+        out_specs=[some(HD, PAIR), whole(table.shape)],
         scratch_shapes=[
             pltpu.VMEM(table.shape, jnp.float32),
-            pltpu.VMEM((PER * BLOCK, PAIR), jnp.bfloat16),
-            pltpu.VMEM((PER * BLOCK, 2 * BLOCK), jnp.bfloat16),
+            pltpu.VMEM((PAIRED, PER * BLOCK, PAIR), jnp.bfloat16),
+            pltpu.VMEM((PAIRED, PER * BLOCK, 2 * BLOCK), jnp.bfloat16),
         ],
     )
     return pl.pallas_call(
@@ -169,7 +134,7 @@
             flops=10 * BLK * PER * BLOCK**3, bytes_accessed=16 << 20, transcendentals=BLK * PER * BLOCK**2
         ),
         name="attend_back",
-    )(slots, count, query, grad, attended, stat, table)
+    )(slots, count, both, stat, table)
 
 
 def torus(node_count):
@@ -210,7 +175,9 @@
 
 
 def fetch_kernel(
-    planes, group, own_ref, asked_ref, weight_ref, query_ref, table_ref, shared_ref, asks_ref,
+    planes, group, own_ref, asked_ref, weight_ref, out_weight_ref, cotangent_ref, slots_ref, count_ref,
+    table_ref, shared_ref, asks_ref, both_ref, stat_ref, output_ref, norm_ref, out_grad_ref,
+    query_ref, packed, highs, sums, att_in, att_rows, low_grad, my_grads, grad_in,
     pairs, my_pairs, my_queries, ring_a, ring_b, chunk_a, chunk_b, picked_a, picked_b, landed, made, asks,
     o_send, o_recv, q_send, q_recv, ra_send, ra_recv, rb_send, rb_recv,
     ga_send, ga_recv, gb_send, gb_recv, x_send, x_recv, asks_sem,
@@ -233,8 +200,7 @@
         both = dot(own, pairs[:, h * PAIR : (h + 1) * PAIR]).astype(jnp.bfloat16)
         my_pairs[h] = both.reshape(HEADS, BLOCK, PAIR)
         queries = (dot(own, weight[:, h * step : h * step + HD]) * SCALE).astype(jnp.bfloat16)
-        queries = queries.reshape(HEADS, BLOCK, HD)
-        my_queries[h] = jnp.concatenate([queries[:, :HD], queries[:, HD:]], axis=2)
+        my_queries[h] = pack(queries.reshape(HEADS, BLOCK, HD))
     arrive()
 
     def own_copies(kind, source, target):
@@ -384,11 +350,68 @@
     for t in range(planes):
         for copy in copies_b(place(t)):
             copy.wait_recv()
+
+    attended = own_copies(
+        4, lambda h: packed.at[pl.ds(h * HEADS, HEADS)], att_in.at[head]
+    )
+    for d in list(range(1, HEADS)) + [0]:
+        base = (head + d) % HEADS * HEADS
+
+        @pl.loop(0, HEADS)
+        def _(i):
+            b = base + i
+            chosen = [table_ref[slots_ref[b, j]] for j in range(PER)]
+            result, highest, total = attend(unpack(query_ref[b]), chosen, count_ref[b])
+            packed[b] = pack(result[:, HD:])
+            both_ref[b] = result
+            highs[b] = jnp.broadcast_to(highest, (BLOCK, BLOCK))
+            sums[b] = jnp.broadcast_to(total, (BLOCK, BLOCK))
+
+        if d:
+            begin([attended[d - 1]])
+    att_in[head] = packed[own_blocks]
+    for copy in attended:
+        copy.wait_recv()
+
+    @pl.loop(0, HEADS)
+    def _(i):
+        att = jnp.concatenate([unpack(att_in[h, i]) for h in range(HEADS)], axis=1)
+        att_rows[i] = att
+        summed = own_ref[i].astype(jnp.float32) + dot(att, out_weight_ref[...])
+        root_mean = jnp.sqrt(jnp.mean(summed * summed, axis=-1, keepdims=True) + 1e-06)
+        normed = summed / root_mean
+        output_ref[i] = normed.astype(jnp.bfloat16)
+        upstream = cotangent_ref[i].astype(jnp.float32)
+        grad = (upstream - normed * jnp.mean(upstream * normed, axis=-1, keepdims=True)) / root_mean
+        norm_ref[i] = grad
+        low_grad[i] = grad.astype(jnp.bfloat16)
+        back = dot(grad.astype(jnp.bfloat16), out_weight_ref[...], NT).astype(jnp.bfloat16)
+        for h in range(HEADS):
+            my_grads[h, i] = pack(back[:, h * HD : (h + 1) * HD])
+
+    back = own_copies(5, lambda h: my_grads.at[h], grad_in.at[own_blocks])
+    begin(back)
+    grad_in[own_blocks] = my_grads[head]
+    out_grad_ref[...] = dot(
+        att_rows[...].reshape(rows, WIDE), low_grad[...].reshape(rows, WIDE), TN
+    )
+    for copy in back:
+        copy.wait_recv()
+
+    @pl.loop(0, BLK)
+    def _(b):
+        grad, result = unpack(grad_in[b]), both_ref[b][:, HD:]
+        dots = jnp.sum(grad.astype(jnp.float32) * result.astype(jnp.float32), axis=1, keepdims=True)
+        lane = lax.broadcasted_iota(jnp.int32, (BLOCK, BLOCK), 1)
+        stat = jnp.where(lane == 0, highs[b], jnp.where(lane == 1, dots, 1.0 / sums[b]))
+        stat_ref[b] = stat.T[:8]
+        both_ref[b] = jnp.concatenate([unpack(query_ref[b]), grad], axis=1)
+
     for copy in sent:
         copy.wait_send()
 
 
-def fetch(features, in_weight, wanted, node_count):
+def fetch(features, in_weight, out_weight, cotangent, key_slots, block_count, wanted, node_count):
     planes, group = torus(node_count)
     own = features.reshape(HEADS, BLOCK, WIDE)
     asked = wanted.reshape(planes, group, CAP).transpose(1, 0, 2).reshape(group, 1, planes * CAP)
@@ -401,14 +424,27 @@
     return pl.pallas_call(
         functools.partial(fetch_kernel, planes, group),
         out_shape=(
-            jax.ShapeDtypeStruct((BLK, HD, PAIR), jnp.bfloat16),
             jax.ShapeDtypeStruct((slots, BLOCK, PAIR), jnp.bfloat16),
             jax.ShapeDtypeStruct((planes, group * CAP * PART, WIDE), jnp.bfloat16),
             jax.ShapeDtypeStruct((group, 8, 128), jnp.int32),
+            jax.ShapeDtypeStruct((BLK, BLOCK, PAIR), jnp.bfloat16),
+            jax.ShapeDtypeStruct((BLK, 8, BLOCK), jnp.float32),
+            jax.ShapeDtypeStruct((HEADS, BLOCK, WIDE), jnp.bfloat16),
+            jax.ShapeDtypeStruct((HEADS, BLOCK, WIDE), jnp.float32),
+            jax.ShapeDtypeStruct((WIDE, WIDE), jnp.float32),
         ),
-        in_specs=[vmem] * 3,
-        out_specs=(vmem,) * 4,
+        in_specs=[vmem] * 5 + [pl.BlockSpec(memory_space=pltpu.SMEM)] * 2,
+        out_specs=(vmem,) * 8,
         scratch_shapes=[
+            low(BLK, HD, PAIR),
+            low(BLK, HD, PAIR),
+            pltpu.VMEM((BLK, BLOCK, BLOCK), jnp.float32),
+            pltpu.VMEM((BLK, BLOCK, BLOCK), jnp.float32),
+            low(HEADS, HEADS, HD, PAIR),
+            low(HEADS, BLOCK, WIDE),
+            low(HEADS, BLOCK, WIDE),
+            low(HEADS, HEADS, HD, PAIR),
+            low(BLK, HD, PAIR),
             low(WIDE, HEADS * PAIR),
             low(HEADS, HEADS, BLOCK, PAIR),
             low(HEADS, HEADS, HD, PAIR),
@@ -421,17 +457,17 @@
             low(planes, group, CAP, PART, WIDE),
             low(planes, HEADS, group * CAP, PART, PAIR),
             pltpu.SMEM((group, 8, 128), jnp.int32),
-            dma(4, 3), dma(4, 3), dma(group - 1), dma(group - 1),
+            dma(6, 3), dma(6, 3), dma(group - 1), dma(group - 1),
             dma(2, planes // 2), dma(2, planes // 2), dma(2, planes // 2), dma(2, planes // 2),
             dma(planes, group - 1), dma(planes, group - 1), dma(planes, group - 1), dma(planes, group - 1),
             dma(planes, 3), dma(planes, 3),
             pltpu.SemaphoreType.DMA,
         ],
         compiler_params=pltpu.CompilerParams(
-            collective_id=2, has_side_effects=True, vmem_limit_bytes=48 << 20
+            collective_id=2, has_side_effects=True, vmem_limit_bytes=56 << 20
         ),
         name="fetch",
-    )(own, asked, in_weight)
+    )(own, asked, in_weight, out_weight, cotangent.reshape(own.shape), key_slots, block_count)
 
 
 def return_kernel(
@@ -619,7 +655,7 @@
             everything = features_ref[...].reshape(HEADS * BLOCK, WIDE)
             acc[...] += dot(some, features_ref[:, :SHARED].reshape(HEADS * SHARED, WIDE), TN)
             single_weight = dot(queries, everything, TN)
-            base[...] = (norm_ref[...] + dot(queries, singles[...], NT)).reshape(HEADS, BLOCK, WIDE)
+            base[...] = norm_ref[...] + dot(queries, singles[...], NT).reshape(HEADS, BLOCK, WIDE)
             base[:, :SHARED] += dot(some, pairs[...], NT).reshape(HEADS, SHARED, WIDE)
         total = gather_late(t, chosen)
         if t == planes - 1:
@@ -764,36 +800,17 @@
 
 def on_device(features, in_weight, out_weight, cotangent, key_slots, block_count, wanted):
     node_count = lax.axis_size("node")
-    node_rows = BLK * BLOCK
-    total_nodes = node_rows * node_count
-    queries, table, shared, asks = fetch(features, in_weight, wanted, node_count)
-    slots = key_slots.reshape(-1)
-    wide, stat = forward(slots, block_count, queries, table)
-    attended = wide[:, HD:]
-    attended_rows = lax.all_to_all(attended, "head", split_axis=0, concat_axis=1, tiled=True)
-    summed = features.astype(jnp.float32) + jnp.dot(
-        attended_rows, out_weight, preferred_element_type=jnp.float32
-    )
-    root_mean = jnp.sqrt(jnp.mean(summed * summed, axis=-1, keepdims=True) + 1e-06)
-    normed = summed / root_mean
-    output = normed.astype(jnp.bfloat16)
-    upstream = cotangent.astype(jnp.float32)
-    norm_grad = (
-        upstream - normed * jnp.mean(upstream * normed, axis=-1, keepdims=True)
-    ) / root_mean
-    norm_grad_low = norm_grad.astype(jnp.bfloat16)
-    out_weight_grad = jnp.dot(attended_rows.T, norm_grad_low, preferred_element_type=jnp.float32)
-    attended_grad = jnp.dot(norm_grad_low, out_weight.T, preferred_element_type=jnp.float32).astype(
-        jnp.bfloat16
-    )
-    attended_grad = lax.all_to_all(attended_grad, "head", split_axis=1, concat_axis=0, tiled=True)
-    dq, grads = backward(slots, block_count, queries, attended_grad, wide, stat, table)
+    total_nodes = BLK * BLOCK * node_count
+    table, shared, asks, both, stat, output, norm_grad, out_weight_grad = fetch(
+        features, in_weight, out_weight, cotangent, key_slots, block_count, wanted, node_count
+    )
+    dq, grads = backward(key_slots.reshape(-1), block_count, both, stat, table)
     feature_grad, in_weight_grad, out_weight_grad = give_back(
         grads, dq, shared, features, norm_grad, in_weight, out_weight_grad, asks, node_count
     )
     grad_factor = total_nodes ** (-0.5)
     return (
-        output,
+        output.reshape(features.shape),
         feature_grad,
         in_weight_grad * grad_factor,
         out_weight_grad * grad_factor,

time: 219 us -> 198 us (0.904)
  blocking collectives: 7.95 us -> 0 us
  local copies, waits for them, and re-layouts: 14.1 us -> 6.91 us
  Pallas kernels: 183 us -> 188 us
  waiting for transfers between devices: 4.37 us -> 0 us
  starting transfers between devices: 3.58 us -> 0 us
  matrix products: 2.29 us -> 0 us
    pallas_call x1, Pallas kernels: 63.2 us -> 86.6 us  [fetch(): pl.pallas_call(functools.partial(fetch_kernel, planes, group), out_shape=...]
    pallas_call x1 -> x0, Pallas kernels: 11.1 us -> none  [forward(): pl.pallas_call(forward_kernel, grid_spec=grid_spec, out_shape=(jax.ShapeD...]
    all_to_all x1 -> x0, blocking collectives: 7.95 us -> none  [on_device(): lax.all_to_all(attended, 'head', split_axis=0, concat_axis=1, tiled=True)]
    unnamed x29 -> x4, local copies, waits for them, and re-layouts: 9.3 us -> 2.37 us
    pallas_call x1, Pallas kernels: 21.4 us -> 16.4 us  [backward(): pl.pallas_call(backward_kernel, grid_spec=grid_spec, out_shape=(jax.Shape...]
    all_to_all x1 -> x0, waiting for transfers between devices: 4.37 us -> none  [on_device(): lax.all_to_all(attended_grad, 'head', split_axis=1, concat_axis=0, tiled=...]
    all_to_all x1 -> x0, starting transfers between devices: 3.58 us -> none  [on_device(): lax.all_to_all(attended_grad, 'head', split_axis=1, concat_axis=0, tiled=...]
    dot_general x3 -> x0, matrix products: 2.29 us -> none  [the longest x1 0.97 us: on_device(): jnp.dot(norm_grad_low, out_weight.T, preferred_element_type=jnp.float32)]
  transfers between devices with their start and end apart: 1 -> 0, of which waited for: 1 -> 0; matrix products, arithmetic and copies ran while one was open for 0% -> 0% of each run, Pallas kernels for 0% -> 0%
where the time goes in v8:
time: 198 us; the launch traced here: 197 us
  Pallas kernels  188 us (95%)
  local copies, waits for them, and re-layouts  6.91 us (3%)
    pallas_call x1, Pallas kernels, fetch(): pl.pallas_call(functools.partial(fetch_kernel, planes, group), out_shape=...  86.6 us
    pallas_call x1, Pallas kernels, give_back(): pl.pallas_call(functools.partial(return_kernel, planes, group), out_shape...  85.5 us
    pallas_call x1, Pallas kernels, backward(): pl.pallas_call(backward_kernel, grid_spec=grid_spec, out_shape=(jax.Shape...  16.4 us

profile of v8, /device:TPU:1, one launch (start us, length us, event | category | flops | bytes accessed | tf_op | source)
XLA Modules:
  0.0 197.3 jit_solution(12416167545811894487)
XLA Ops:
  0.6 1.3 reshape.42.slots_ref
  2.0 0.8 reshape.38
  2.7 0.1 copy.12
  2.8 0.6 pad.4.asked_ref
  3.4 86.6 %fetch.1 = (bf16[144,128,128]{2,1,0:T(8,128)(2,1)}, bf16[8,256,256]{2,1,0:T(8,128)(2,1)}, s32[8,8,128]{2,1,0:T(8,128)}, bf16[16,128,128]{2,1,0:T(8,128)(2,1)}, f...) custom-call(bf16[4,128,256]{2,1,0:T(8,128)(2,1)} %bitcast.16, ...), custom_call_target="tpu_custom_call" | custom-call | tf_op jit(solution)/shard_map/fetch/pallas_call | solution.py:424
  90.0 16.4 %attend_back.1 = (bf16[16,64,128]{2,1,0:T(8,128)(2,1)}, bf16[144,128,128]{2,1,0:T(8,128)(2,1)}) custom-call(s32[192]{0:T(256)} %reshape.42.slots_ref, s32[16]{0:T(128)} %count_ref.3, bf16[16,128,128]{2,1,0:T(8,128)(2,1)} %get-tuple-element.17.both_ref, f32[16,8,128]{2,1,0:T(8,128)} %get-tuple-element.18.stat_ref, ...), custom_call_target="tpu_custom_call" | custom-call | flops 4026531840 | bytes 16777216 | tf_op jit(solution)/shard_map/attend_back/pallas_call | solution.py:125
  106.4 0.0 copy-start
  106.4 85.5 %give_back.1 = (bf16[4,128,256]{2,1,0:T(8,128)(2,1)}, f32[8,8,8,128]{3,2,1,0:T(8,128)}) custom-call(bf16[144,128,128]{2,1,0:T(8,128)(2,1)} %get-tuple-element.20.grads_ref, bf16[16,64,128]{2,1,0:T(8,128)(2,1)} %get-tuple-element.21.dq_ref, bf16[8,256,256]{2,1,0:T(8,128)(2,1)} %get-tuple-element.22.shared_ref, bf16[4,128,256]{2,1,0:T(8,128)(2,1)} %bitcast.17, ...), custom_call_target="tpu_custom_call" | custom-call | tf_op jit(solution)/shard_map/give_back/pallas_call | solution.py:750
  191.9 0.8 slice_bitcast_fusion.1
  192.6 1.0 fusion.1
  193.6 0.7 fusion
  194.3 0.6 maximum_multiply_fusion.1
  194.9 0.0 copy-done
  194.9 0.7 copy.15
  195.6 1.7 copy.16
  (1 shorter events, 0.0 us)
Async XLA Ops:
  106.4 88.6 %copy-start = (bf16[4,128,256]{2,1,0:T(8,128)(2,1)S(1)}, bf16[4,128,256]{2,1,0:T(8,128)(2,1)}, u32[]{:S(2)}) copy-start(bf16[4,128,256]{2,1,0:T(8,128)(2,1)} %get-tuple-element.16) | copy-start | bytes 786436

commit v9 on v8

--- a/solution.py
+++ b/solution.py
@@ -357,15 +357,18 @@
     for d in list(range(1, HEADS)) + [0]:
         base = (head + d) % HEADS * HEADS
 
-        @pl.loop(0, HEADS)
+        @pl.loop(0, HEADS // PAIRED)
         def _(i):
-            b = base + i
-            chosen = [table_ref[slots_ref[b, j]] for j in range(PER)]
-            result, highest, total = attend(unpack(query_ref[b]), chosen, count_ref[b])
-            packed[b] = pack(result[:, HD:])
-            both_ref[b] = result
-            highs[b] = jnp.broadcast_to(highest, (BLOCK, BLOCK))
-            sums[b] = jnp.broadcast_to(total, (BLOCK, BLOCK))
+            blocks = [base + i * PAIRED + k for k in range(PAIRED)]
+            chosen = [[table_ref[slots_ref[b, j]] for j in range(PER)] for b in blocks]
+            results = [
+                attend(unpack(query_ref[b]), some, count_ref[b]) for b, some in zip(blocks, chosen)
+            ]
+            for b, (result, highest, total) in zip(blocks, results):
+                packed[b] = pack(result[:, HD:])
+                both_ref[b] = result
+                highs[b] = jnp.broadcast_to(highest, (BLOCK, BLOCK))
+                sums[b] = jnp.broadcast_to(total, (BLOCK, BLOCK))
 
         if d:
             begin([attended[d - 1]])
@@ -398,14 +401,19 @@
     for copy in back:
         copy.wait_recv()
 
-    @pl.loop(0, BLK)
-    def _(b):
-        grad, result = unpack(grad_in[b]), both_ref[b][:, HD:]
-        dots = jnp.sum(grad.astype(jnp.float32) * result.astype(jnp.float32), axis=1, keepdims=True)
-        lane = lax.broadcasted_iota(jnp.int32, (BLOCK, BLOCK), 1)
-        stat = jnp.where(lane == 0, highs[b], jnp.where(lane == 1, dots, 1.0 / sums[b]))
-        stat_ref[b] = stat.T[:8]
-        both_ref[b] = jnp.concatenate([unpack(query_ref[b]), grad], axis=1)
+    @pl.loop(0, BLK // 4)
+    def _(i):
+        done = []
+        for k in range(4):
+            b = i * 4 + k
+            grad, result = unpack(grad_in[b]), both_ref[b][:, HD:]
+            dots = jnp.sum(grad.astype(jnp.float32) * result.astype(jnp.float32), axis=1, keepdims=True)
+            lane = lax.broadcasted_iota(jnp.int32, (BLOCK, BLOCK), 1)
+            stat = jnp.where(lane == 0, highs[b], jnp.where(lane == 1, dots, 1.0 / sums[b]))
+            done.append((b, stat.T[:8], jnp.concatenate([unpack(query_ref[b]), grad], axis=1)))
+        for b, stat, both in done:
+            stat_ref[b] = stat
+            both_ref[b] = both
 
     for copy in sent:
         copy.wait_send()
@@ -633,7 +641,7 @@
         total = dot(chosen, answers_a[places[t]].reshape(width * PART, WIDE)).reshape(BLK, PART, WIDE)
         return pass_on(t, total, partial_a, ring_a, ra_send, ra_recv)
 
-    before = None
+    pending = []
     for t in range(planes):
         copies = spread(t)
         chosen = choose(t)
@@ -663,14 +671,13 @@
             tail = to_heads(3, lambda h: late_sums.at[blocks_of(h)], own_pairs.at[head, :, late])
             begin(tail)
             own_pairs[head, :, SHARED:] = late_sums[own_blocks]
-        if t:
-            gather(t - 1, *before)
-        before = (chosen, copies)
-    summed[...] = gather(planes - 1, *before).astype(jnp.bfloat16)
-    final = to_heads(4, lambda h: summed.at[blocks_of(h)], quarters.at[head])
-    begin(final)
-    quarters[head] = summed[own_blocks]
-
+        pending.append((t, chosen, copies))
+
+    def gather_some(count):
+        for _ in range(min(count, len(pending) - 1)):
+            gather(*pending.pop(0))
+
+    gather_some(1)
     for copy in tail:
         copy.wait_recv()
     some = jnp.concatenate(
@@ -690,14 +697,6 @@
     in_low = to_heads(5, lambda h: in_mine.at[h], in_in.at[head])
     begin(in_low)
 
-    base[:, SHARED:] += dot(some, pairs[...], NT).reshape(HEADS, low, WIDE)
-    feature_ref[:, SHARED:] = base[:, SHARED:].astype(jnp.bfloat16)
-    for copy in final:
-        copy.wait_recv()
-    for h in range(HEADS):
-        rows = slice(h * PART, (h + 1) * PART)
-        feature_ref[:, rows] = (base[:, rows] + quarters[h].astype(jnp.float32)).astype(jnp.bfloat16)
-
     def exchange(peers, source, target, send, recv):
         copies = [
             remote(source(d, peer), target(d), send.at[d], recv.at[d], peer) for d, peer in enumerate(peers)
@@ -705,6 +704,7 @@
         begin(copies)
         return copies
 
+    gather_some(2)
     for copy in out_copies + in_low:
         copy.wait_recv()
     out_in[head] = out_mine[head]
@@ -713,26 +713,43 @@
         in_total = in_total + in_in[h].astype(jnp.float32)
     out_total = out_in[0] + out_in[1] + out_in[2] + out_in[3]
     x_sum[...] = jnp.concatenate([in_total, out_total], axis=0).reshape(x_sum.shape)
-    for copy in exchange(
+    copies = exchange(
         g_peers, lambda d, peer: x_sum.at[peer[0] % group], lambda d: g_in.at[d], wg_send, wg_recv
-    ):
+    )
+    gather_some(2)
+    for copy in copies:
         copy.wait_recv()
     total = x_sum[g]
     for d in range(group - 1):
         total = total + g_in[d]
     g_sum[...] = total
-    for copy in exchange(
+    copies = exchange(
         z_peers, lambda d, peer: g_sum.at[peer[0] // group], lambda d: z_in.at[d], wz_send, wz_recv
-    ):
+    )
+    gather_some(planes)
+    for copy in copies:
         copy.wait_recv()
     total = g_sum[z]
     for d in range(planes - 1):
         total = total + z_in[d]
     piece[...] = total
     sum_ref[g, z] = total
-    for copy in exchange(z_peers, lambda d, peer: piece, lambda d: sum_ref.at[g, z], bz_send, bz_recv):
-        copy.wait_recv()
-    for copy in exchange(g_peers, lambda d, peer: sum_ref.at[g], lambda d: sum_ref.at[g], bg_send, bg_recv):
+    copies = exchange(z_peers, lambda d, peer: piece, lambda d: sum_ref.at[g, z], bz_send, bz_recv)
+    summed[...] = gather(*pending.pop(0)).astype(jnp.bfloat16)
+    final = to_heads(4, lambda h: summed.at[blocks_of(h)], quarters.at[head])
+    begin(final)
+    quarters[head] = summed[own_blocks]
+    for copy in copies:
+        copy.wait_recv()
+    copies = exchange(g_peers, lambda d, peer: sum_ref.at[g], lambda d: sum_ref.at[g], bg_send, bg_recv)
+    base[:, SHARED:] += dot(some, pairs[...], NT).reshape(HEADS, low, WIDE)
+    feature_ref[:, SHARED:] = base[:, SHARED:].astype(jnp.bfloat16)
+    for copy in final:
+        copy.wait_recv()
+    for h in range(HEADS):
+        rows = slice(h * PART, (h + 1) * PART)
+        feature_ref[:, rows] = (base[:, rows] + quarters[h].astype(jnp.float32)).astype(jnp.bfloat16)
+    for copy in copies:
         copy.wait_recv()
     for copy in sent:
         copy.wait_send()

time: 198 us -> 188 us (0.949)
  Pallas kernels: 188 us -> 179 us
    pallas_call x1, Pallas kernels: 85.5 us -> 78.6 us  [give_back(): pl.pallas_call(functools.partial(return_kernel, planes, group), out_shape...]
    pallas_call x1, Pallas kernels: 86.6 us -> 83.8 us  [fetch(): pl.pallas_call(functools.partial(fetch_kernel, planes, group), out_shape=...]
where the time goes in v9:
time: 188 us
  Pallas kernels  179 us (95%)
  local copies, waits for them, and re-layouts  6.91 us (4%)
    pallas_call x1, Pallas kernels, fetch(): pl.pallas_call(functools.partial(fetch_kernel, planes, group), out_shape=...  83.8 us
    pallas_call x1, Pallas kernels, give_back(): pl.pallas_call(functools.partial(return_kernel, planes, group), out_shape...  78.6 us
    pallas_call x1, Pallas kernels, backward(): pl.pallas_call(backward_kernel, grid_spec=grid_spec, out_shape=(jax.Shape...  16.4 us

profile of v9, /device:TPU:1, one launch (start us, length us, event | category | flops | bytes accessed | tf_op | source)
XLA Modules:
  0.0 187.7 jit_solution(16893265206449745397)
XLA Ops:
  0.6 1.3 reshape.42.slots_ref
  2.0 0.8 reshape.38
  2.7 0.1 copy.12
  2.8 0.6 pad.4.asked_ref
  3.4 83.8 %fetch.1 = (bf16[144,128,128]{2,1,0:T(8,128)(2,1)}, bf16[8,256,256]{2,1,0:T(8,128)(2,1)}, s32[8,8,128]{2,1,0:T(8,128)}, bf16[16,128,128]{2,1,0:T(8,128)(2,1)}, f...) custom-call(bf16[4,128,256]{2,1,0:T(8,128)(2,1)} %bitcast.16, ...), custom_call_target="tpu_custom_call" | custom-call | tf_op jit(solution)/shard_map/fetch/pallas_call | solution.py:432
  87.2 16.4 %attend_back.1 = (bf16[16,64,128]{2,1,0:T(8,128)(2,1)}, bf16[144,128,128]{2,1,0:T(8,128)(2,1)}) custom-call(s32[192]{0:T(256)} %reshape.42.slots_ref, s32[16]{0:T(128)} %count_ref.3, bf16[16,128,128]{2,1,0:T(8,128)(2,1)} %get-tuple-element.17.both_ref, f32[16,8,128]{2,1,0:T(8,128)} %get-tuple-element.18.stat_ref, ...), custom_call_target="tpu_custom_call" | custom-call | flops 4026531840 | bytes 16777216 | tf_op jit(solution)/shard_map/attend_back/pallas_call | solution.py:125
  103.6 0.0 copy-start
  103.6 78.6 %give_back.1 = (bf16[4,128,256]{2,1,0:T(8,128)(2,1)}, f32[8,8,8,128]{3,2,1,0:T(8,128)}) custom-call(bf16[144,128,128]{2,1,0:T(8,128)(2,1)} %get-tuple-element.20.grads_ref, bf16[16,64,128]{2,1,0:T(8,128)(2,1)} %get-tuple-element.21.dq_ref, bf16[8,256,256]{2,1,0:T(8,128)(2,1)} %get-tuple-element.22.shared_ref, bf16[4,128,256]{2,1,0:T(8,128)(2,1)} %bitcast.17, ...), custom_call_target="tpu_custom_call" | custom-call | tf_op jit(solution)/shard_map/give_back/pallas_call | solution.py:767
  182.2 0.8 slice_bitcast_fusion.1
  183.0 1.0 fusion.1
  184.0 0.7 fusion
  184.6 0.6 maximum_multiply_fusion.1
  185.3 0.0 copy-done
  185.3 0.7 copy.15
  186.0 1.7 copy.16
  (1 shorter events, 0.0 us)
Async XLA Ops:
  103.6 81.7 %copy-start = (bf16[4,128,256]{2,1,0:T(8,128)(2,1)S(1)}, bf16[4,128,256]{2,1,0:T(8,128)(2,1)}, u32[]{:S(2)}) copy-start(bf16[4,128,256]{2,1,0:T(8,128)(2,1)} %get-tuple-element.16) | copy-start | bytes 786436

commit v10 on v9

--- a/solution.py
+++ b/solution.py
@@ -81,7 +81,7 @@
         )
         stacks.append(stacked)
         highest, dots, inverse = stat_ref[i, 0:1], stat_ref[i, 1:2], stat_ref[i, 2:3]
-        slots.append([slots_ref[b * PER + j] for j in range(PER)])
+        slots.append([slots_ref[b, j] for j in range(PER)])
         for j in range(PER):
             keys_ref[i, j * BLOCK : (j + 1) * BLOCK] = table_ref[slots[i][j]]
         for j in range(0, PER, 2):
@@ -376,7 +376,7 @@
     for copy in attended:
         copy.wait_recv()
 
-    @pl.loop(0, HEADS)
+    @pl.loop(0, HEADS, unroll=True)
     def _(i):
         att = jnp.concatenate([unpack(att_in[h, i]) for h in range(HEADS)], axis=1)
         att_rows[i] = att
@@ -821,7 +821,7 @@
     table, shared, asks, both, stat, output, norm_grad, out_weight_grad = fetch(
         features, in_weight, out_weight, cotangent, key_slots, block_count, wanted, node_count
     )
-    dq, grads = backward(key_slots.reshape(-1), block_count, both, stat, table)
+    dq, grads = backward(key_slots, block_count, both, stat, table)
     feature_grad, in_weight_grad, out_weight_grad = give_back(
         grads, dq, shared, features, norm_grad, in_weight, out_weight_grad, asks, node_count
     )

time: 188 us -> 186 us (0.989)
  no operation moved by 1% of the time
where the time goes in v10:
time: 186 us; the launch traced here: 185 us
  Pallas kernels  178 us (96%)
  local copies, waits for them, and re-layouts  5.57 us (3%)
    pallas_call x1, Pallas kernels, fetch(): pl.pallas_call(functools.partial(fetch_kernel, planes, group), out_shape=...  82.7 us
    pallas_call x1, Pallas kernels, give_back(): pl.pallas_call(functools.partial(return_kernel, planes, group), out_shape...  78.6 us
    pallas_call x1, Pallas kernels, backward(): pl.pallas_call(backward_kernel, grid_spec=grid_spec, out_shape=(jax.Shape...  16.5 us

profile of v10, /device:TPU:1, one launch (start us, length us, event | category | flops | bytes accessed | tf_op | source)
XLA Modules:
  0.0 185.3 jit_solution(11124829058772123608)
XLA Ops:
  0.6 0.8 reshape.35
  1.4 0.1 copy.12
  1.5 0.6 pad.4.asked_ref
  2.1 82.7 %fetch.1 = (bf16[144,128,128]{2,1,0:T(8,128)(2,1)}, bf16[8,256,256]{2,1,0:T(8,128)(2,1)}, s32[8,8,128]{2,1,0:T(8,128)}, bf16[16,128,128]{2,1,0:T(8,128)(2,1)}, f...) custom-call(bf16[4,128,256]{2,1,0:T(8,128)(2,1)} %bitcast.16, ...), custom_call_target="tpu_custom_call" | custom-call | tf_op jit(solution)/shard_map/fetch/pallas_call | solution.py:432
  84.8 16.5 %attend_back.1 = (bf16[16,64,128]{2,1,0:T(8,128)(2,1)}, bf16[144,128,128]{2,1,0:T(8,128)(2,1)}) custom-call(s32[16,12]{1,0:T(8,128)} %slots_ref.3, s32[16]{0:T(128)} %count_ref.3, bf16[16,128,128]{2,1,0:T(8,128)(2,1)} %get-tuple-element.17.both_ref, f32[16,8,128]{2,1,0:T(8,128)} %get-tuple-element.18.stat_ref, bf16[144,128,128]{2,1,0:T(8,128)(2,1)} %get-tuple-element.19.table_ref), custom_call_target="tpu_custom_call" | custom-call | flops 4026531840 | bytes 16777216 | tf_op jit(solution)/shard_map/attend_back/pallas_call | solution.py:125
  101.3 0.0 copy-start
  101.3 78.6 %give_back.1 = (bf16[4,128,256]{2,1,0:T(8,128)(2,1)}, f32[8,8,8,128]{3,2,1,0:T(8,128)}) custom-call(bf16[144,128,128]{2,1,0:T(8,128)(2,1)} %get-tuple-element.20.grads_ref, bf16[16,64,128]{2,1,0:T(8,128)(2,1)} %get-tuple-element.21.dq_ref, bf16[8,256,256]{2,1,0:T(8,128)(2,1)} %get-tuple-element.22.shared_ref, bf16[4,128,256]{2,1,0:T(8,128)(2,1)} %bitcast.17, ...), custom_call_target="tpu_custom_call" | custom-call | tf_op jit(solution)/shard_map/give_back/pallas_call | solution.py:767
  179.9 0.8 slice_bitcast_fusion.1
  180.7 1.0 fusion.1
  181.6 0.7 fusion
  182.3 0.6 maximum_multiply_fusion.1
  183.0 0.0 copy-done
  183.0 0.7 copy.15
  183.7 1.7 copy.16
  (1 shorter events, 0.0 us)
Async XLA Ops:
  101.3 81.7 %copy-start = (bf16[4,128,256]{2,1,0:T(8,128)(2,1)S(1)}, bf16[4,128,256]{2,1,0:T(8,128)(2,1)}, u32[]{:S(2)}) copy-start(bf16[4,128,256]{2,1,0:T(8,128)(2,1)} %get-tuple-element.16) | copy-start | bytes 786436
